TPU v7x, 32 devices: a whole 2x2x4 slice. The times are simulated.
32 devices in a mesh: rep: 8 (over y, x, core), fsdp: 4 (over z).
Axes of the slice: x: 2, y: 2, z: 4, core: 2. Of those that a mesh axis runs over, the one named last changes fastest.
Arguments:
- tokens: bfloat16 [16, 1024, 2048], P('rep', 'fsdp'), may hold values from -6 to 6
- lengths: int32 [16], P('rep'), may hold values from 256 to 1024, as said below
- query_weight: bfloat16 [2048, 2048], P('fsdp'), may hold values from -0.125 to 0.125
- key_weight: bfloat16 [2048, 2048], P('fsdp'), may hold values from -0.125 to 0.125
- value_weight: bfloat16 [2048, 2048], P('fsdp'), may hold values from -0.125 to 0.125
- out_weight: bfloat16 [2048, 2048], P('fsdp'), may hold values from -3 to 3
- query_bias: bfloat16 [2048], P('fsdp'), may hold values from -3 to 3
- value_bias: bfloat16 [2048], P('fsdp'), may hold values from -3 to 3
- out_bias: bfloat16 [2048], P('fsdp'), may hold values from -3 to 3
- first_gain: bfloat16 [2048], P('fsdp'), may hold values from 0.5 to 1.5
- first_shift: bfloat16 [2048], P('fsdp'), may hold values from -3 to 3
- up_weight: bfloat16 [2048, 8192], P('fsdp'), may hold values from -0.125 to 0.125
- up_bias: bfloat16 [8192], P('fsdp'), may hold values from -3 to 3
- down_weight: bfloat16 [8192, 2048], P('fsdp'), may hold values from -0.0625 to 0.0625
- down_bias: bfloat16 [2048], P('fsdp'), may hold values from -3 to 3
- second_gain: bfloat16 [2048], P('fsdp'), may hold values from 0.5 to 1.5
- second_shift: bfloat16 [2048], P('fsdp'), may hold values from -3 to 3
- cotangent: bfloat16 [16, 1024, 2048], P('rep', 'fsdp'), may hold values from -6 to 6
Outputs:
- layer_out: bfloat16 [16, 1024, 2048], P('rep', 'fsdp')
- tokens_grad: float32 [16, 1024, 2048], P('rep', 'fsdp')
- grad_query_weight: float32 [2048, 2048], P('fsdp')
- grad_key_weight: float32 [2048, 2048], P('fsdp')
- grad_value_weight: float32 [2048, 2048], P('fsdp')
- grad_out_weight: float32 [2048, 2048], P('fsdp')
- grad_query_bias: float32 [2048], P('fsdp')
- grad_value_bias: float32 [2048], P('fsdp')
- grad_out_bias: float32 [2048], P('fsdp')
- grad_first_gain: float32 [2048], P('fsdp')
- grad_first_shift: float32 [2048], P('fsdp')
- grad_up_weight: float32 [2048, 8192], P('fsdp')
- grad_up_bias: float32 [8192], P('fsdp')
- grad_down_weight: float32 [8192, 2048], P('fsdp')
- grad_down_bias: float32 [2048], P('fsdp')
- grad_second_gain: float32 [2048], P('fsdp')
- grad_second_shift: float32 [2048], P('fsdp')
Inputs may be any that keep to these rules, and one draw needn't show every extreme that they name: `lengths`: of each replica group's 2 consecutive slots, one, drawn from the seed, has length 1024; the others are at least 256.
All inputs are finite; a program needn't handle non-finite values.
Results may differ from a plain program's by a relative error of at most 0.02.
Values may be sent and summed in bfloat16 or wider, within the bound.
No kernel may reach another device: no remote copies, remote signals or barrier semaphores. Data moves between devices by JAX's collectives and lax.ppermute only.
A program may use at most 384 MiB of HBM per device.

v0:
```python
import jax
import jax.numpy as jnp
from jax import lax
from jax.sharding import PartitionSpec as P

HEADS = 16


EPSILON = 1e-06


def layer_norm(summed, gain, shift):
    center = summed - jnp.mean(summed, axis=-1, keepdims=True)
    spread = jnp.mean(center * center, axis=-1, keepdims=True)
    return center * lax.rsqrt(spread + EPSILON) * gain + shift


def matmul(left, right):
    return jnp.dot(left, right, preferred_element_type=jnp.float32)


def times_transposed(left, right):
    return lax.dot_general(
        left, right, (((1,), (1,)), ((), ())), preferred_element_type=jnp.float32
    )


def inner_rows(left, right):
    return lax.dot_general(
        left, right, (((0,), (0,)), ((), ())), preferred_element_type=jnp.float32
    )


def forward(
    tokens,
    lengths,
    query_weight,
    key_weight,
    value_weight,
    out_weight,
    query_bias,
    value_bias,
    out_bias,
    first_gain,
    first_shift,
    up_weight,
    up_bias,
    down_weight,
    down_bias,
    second_gain,
    second_shift,
):
    slots_here, block, width = tokens.shape
    seqlen = block * lax.axis_size("fsdp")
    head_dim = width // HEADS
    row_count = slots_here * block
    scaling = head_dim ** (-0.5)
    attention = (
        lax.all_gather(query_weight, "fsdp", axis=0, tiled=True),
        lax.all_gather(key_weight, "fsdp", axis=0, tiled=True),
        lax.all_gather(value_weight, "fsdp", axis=0, tiled=True),
        lax.all_gather(out_weight, "fsdp", axis=0, tiled=True),
        lax.all_gather(query_bias, "fsdp", axis=0, tiled=True),
        lax.all_gather(value_bias, "fsdp", axis=0, tiled=True),
        lax.all_gather(out_bias, "fsdp", axis=0, tiled=True),
        lax.all_gather(first_gain, "fsdp", axis=0, tiled=True),
        lax.all_gather(first_shift, "fsdp", axis=0, tiled=True),
    )
    (
        full_query,
        full_key,
        full_value,
        full_out,
        bias_query,
        bias_value,
        bias_out,
        gain_one,
        shift_one,
    ) = attention
    flat = tokens.reshape(row_count, width)
    query = (matmul(flat, full_query) + bias_query.astype(jnp.float32)).astype(jnp.bfloat16)
    keys = matmul(flat, full_key).astype(jnp.bfloat16)
    values = (matmul(flat, full_value) + bias_value.astype(jnp.float32)).astype(jnp.bfloat16)
    all_keys, all_values = (
        lax.all_gather(keys.reshape(slots_here, block, width), "fsdp", axis=1, tiled=True),
        lax.all_gather(values.reshape(slots_here, block, width), "fsdp", axis=1, tiled=True),
    )
    query4 = query.reshape(slots_here, block, HEADS, head_dim)
    keys4 = all_keys.reshape(slots_here, seqlen, HEADS, head_dim)
    values4 = all_values.reshape(slots_here, seqlen, HEADS, head_dim)
    key_mask = jnp.arange(seqlen)[None, :] < lengths[:, None]
    scores = (
        jnp.einsum("gqhd,gkhd->ghqk", query4, keys4, preferred_element_type=jnp.float32) * scaling
    )
    scores = jnp.where(key_mask[:, None, None, :], scores, -1e30)
    log_total = jax.nn.logsumexp(scores, axis=-1, keepdims=True)
    probs = jnp.exp(scores - log_total).astype(jnp.bfloat16)
    context = jnp.einsum("ghqk,gkhd->gqhd", probs, values4, preferred_element_type=jnp.float32)
    context = context.reshape(row_count, width).astype(jnp.bfloat16)
    summed1 = flat.astype(jnp.float32) + matmul(context, full_out) + bias_out.astype(jnp.float32)
    normed1 = layer_norm(summed1, gain_one.astype(jnp.float32), shift_one.astype(jnp.float32))
    hidden_in = normed1.astype(jnp.bfloat16)
    feedforward = (
        lax.all_gather(up_weight, "fsdp", axis=0, tiled=True),
        lax.all_gather(down_weight, "fsdp", axis=0, tiled=True),
        lax.all_gather(up_bias, "fsdp", axis=0, tiled=True),
        lax.all_gather(down_bias, "fsdp", axis=0, tiled=True),
        lax.all_gather(second_gain, "fsdp", axis=0, tiled=True),
        lax.all_gather(second_shift, "fsdp", axis=0, tiled=True),
    )
    full_up, full_down, bias_up, bias_down, gain_two, shift_two = feedforward
    before = matmul(hidden_in, full_up) + bias_up.astype(jnp.float32)
    activated = jax.nn.gelu(before, approximate=True).astype(jnp.bfloat16)
    summed2 = normed1 + matmul(activated, full_down) + bias_down.astype(jnp.float32)
    positions = lax.axis_index("fsdp") * block + jnp.arange(block)
    valid = (positions[None, :] < lengths[:, None]).astype(jnp.float32).reshape(row_count, 1)
    result = valid * layer_norm(
        summed2, gain_two.astype(jnp.float32), shift_two.astype(jnp.float32)
    )
    return {
        "weights": attention + feedforward,
        "query4": query4,
        "keys4": keys4,
        "values4": values4,
        "key_mask": key_mask,
        "log_total": log_total,
        "context": context,
        "summed1": summed1,
        "hidden_in": hidden_in,
        "before": before,
        "activated": activated,
        "summed2": summed2,
        "valid": valid,
        "result": result,
    }


def local(
    tokens,
    lengths,
    query_weight,
    key_weight,
    value_weight,
    out_weight,
    query_bias,
    value_bias,
    out_bias,
    first_gain,
    first_shift,
    up_weight,
    up_bias,
    down_weight,
    down_bias,
    second_gain,
    second_shift,
    cotangent,
):
    slots_here, block, width = tokens.shape
    parts = lax.axis_size("fsdp")
    seqlen = block * parts
    head_dim = width // HEADS
    row_count = slots_here * block
    scaling = head_dim ** (-0.5)
    arguments = (
        tokens,
        lengths,
        query_weight,
        key_weight,
        value_weight,
        out_weight,
        query_bias,
        value_bias,
        out_bias,
        first_gain,
        first_shift,
        up_weight,
        up_bias,
        down_weight,
        down_bias,
        second_gain,
        second_shift,
    )
    first = forward(*arguments)
    layer_out = first["result"].astype(jnp.bfloat16).reshape(slots_here, block, width)
    (
        full_query,
        full_key,
        full_value,
        full_out,
        bias_query,
        bias_value,
        bias_out,
        gain_one,
        shift_one,
        full_up,
        full_down,
        bias_up,
        bias_down,
        gain_two,
        shift_two,
    ) = first["weights"]
    flat = tokens.reshape(row_count, width)
    grad_out = cotangent.reshape(row_count, width).astype(jnp.float32) * first["valid"]
    _, second_pull = jax.vjp(
        layer_norm, first["summed2"], gain_two.astype(jnp.float32), shift_two.astype(jnp.float32)
    )
    dsum2, gain_two_grad, shift_two_grad = second_pull(grad_out)
    ddown = dsum2.astype(jnp.bfloat16)
    down_bias_grad = jnp.sum(ddown.astype(jnp.float32), axis=0)
    dactive = times_transposed(ddown, full_down)
    _, gelu_pull = jax.vjp(lambda inner: jax.nn.gelu(inner, approximate=True), first["before"])
    dbefore = gelu_pull(dactive)[0].astype(jnp.bfloat16)
    up_bias_grad = jnp.sum(dbefore.astype(jnp.float32), axis=0)
    dnormed1 = dsum2 + times_transposed(dbefore, full_up)
    _, first_pull = jax.vjp(
        layer_norm, first["summed1"], gain_one.astype(jnp.float32), shift_one.astype(jnp.float32)
    )
    dsum1, gain_one_grad, shift_one_grad = first_pull(dnormed1)
    dattn = dsum1.astype(jnp.bfloat16)
    out_bias_grad = jnp.sum(dattn.astype(jnp.float32), axis=0)
    dcontext = (
        times_transposed(dattn, full_out)
        .astype(jnp.bfloat16)
        .reshape(slots_here, block, HEADS, head_dim)
    )
    query4, keys4, values4 = (first["query4"], first["keys4"], first["values4"])
    scores = (
        jnp.einsum("gqhd,gkhd->ghqk", query4, keys4, preferred_element_type=jnp.float32) * scaling
    )
    scores = jnp.where(first["key_mask"][:, None, None, :], scores, -1e30)
    probs_full = jnp.exp(scores - first["log_total"])
    probs_low = probs_full.astype(jnp.bfloat16)
    dprobs = jnp.einsum("gqhd,gkhd->ghqk", dcontext, values4, preferred_element_type=jnp.float32)
    row_delta = jnp.sum(dprobs * probs_full, axis=-1, keepdims=True)
    dscores = (probs_full * (dprobs - row_delta)).astype(jnp.bfloat16)
    dvalues_all = jnp.einsum(
        "ghqk,gqhd->gkhd", probs_low, dcontext, preferred_element_type=jnp.float32
    )
    dkeys_all = (
        jnp.einsum("ghqk,gqhd->gkhd", dscores, query4, preferred_element_type=jnp.float32) * scaling
    )
    dquery = (
        jnp.einsum("ghqk,gkhd->gqhd", dscores, keys4, preferred_element_type=jnp.float32) * scaling
    )
    dquery = dquery.reshape(row_count, width).astype(jnp.bfloat16)
    dkeys_own, dvalues_own = (
        lax.psum_scatter(
            dkeys_all.reshape(slots_here, seqlen, width).astype(jnp.bfloat16),
            "fsdp",
            scatter_dimension=1,
            tiled=True,
        ).astype(jnp.float32),
        lax.psum_scatter(
            dvalues_all.reshape(slots_here, seqlen, width).astype(jnp.bfloat16),
            "fsdp",
            scatter_dimension=1,
            tiled=True,
        ).astype(jnp.float32),
    )
    dkeys = dkeys_own.reshape(row_count, width).astype(jnp.bfloat16)
    dvalues = dvalues_own.reshape(row_count, width).astype(jnp.bfloat16)
    query_bias_grad = jnp.sum(dquery.astype(jnp.float32), axis=0)
    value_bias_grad = jnp.sum(dvalues.astype(jnp.float32), axis=0)
    tokens_grad = (
        dsum1
        + times_transposed(dquery, full_query)
        + times_transposed(dkeys, full_key)
        + times_transposed(dvalues, full_value)
    ).reshape(slots_here, block, width)
    hidden_in = first["hidden_in"]
    activated = first["activated"]
    context = first["context"]
    owned = (
        lax.all_to_all(flat, "fsdp", split_axis=1, concat_axis=0, tiled=True),
        lax.all_to_all(context, "fsdp", split_axis=1, concat_axis=0, tiled=True),
        lax.all_to_all(hidden_in, "fsdp", split_axis=1, concat_axis=0, tiled=True),
        lax.all_to_all(activated, "fsdp", split_axis=1, concat_axis=0, tiled=True),
    )
    gathered = (
        lax.all_gather(dquery, "fsdp", axis=0, tiled=True),
        lax.all_gather(dkeys, "fsdp", axis=0, tiled=True),
        lax.all_gather(dvalues, "fsdp", axis=0, tiled=True),
        lax.all_gather(dattn, "fsdp", axis=0, tiled=True),
        lax.all_gather(dbefore, "fsdp", axis=0, tiled=True),
        lax.all_gather(ddown, "fsdp", axis=0, tiled=True),
    )
    matrices = (
        inner_rows(owned[0], gathered[0]),
        inner_rows(owned[0], gathered[1]),
        inner_rows(owned[0], gathered[2]),
        inner_rows(owned[1], gathered[3]),
    )
    up_share = inner_rows(owned[2], gathered[4])
    down_share = inner_rows(owned[3], gathered[5])
    vectors = (
        lax.psum_scatter(
            query_bias_grad.astype(jnp.bfloat16), "fsdp", scatter_dimension=0, tiled=True
        ).astype(jnp.float32),
        lax.psum_scatter(
            value_bias_grad.astype(jnp.bfloat16), "fsdp", scatter_dimension=0, tiled=True
        ).astype(jnp.float32),
        lax.psum_scatter(
            out_bias_grad.astype(jnp.bfloat16), "fsdp", scatter_dimension=0, tiled=True
        ).astype(jnp.float32),
        lax.psum_scatter(
            gain_one_grad.astype(jnp.bfloat16), "fsdp", scatter_dimension=0, tiled=True
        ).astype(jnp.float32),
        lax.psum_scatter(
            shift_one_grad.astype(jnp.bfloat16), "fsdp", scatter_dimension=0, tiled=True
        ).astype(jnp.float32),
        lax.psum_scatter(
            up_bias_grad.astype(jnp.bfloat16), "fsdp", scatter_dimension=0, tiled=True
        ).astype(jnp.float32),
        lax.psum_scatter(
            down_bias_grad.astype(jnp.bfloat16), "fsdp", scatter_dimension=0, tiled=True
        ).astype(jnp.float32),
        lax.psum_scatter(
            gain_two_grad.astype(jnp.bfloat16), "fsdp", scatter_dimension=0, tiled=True
        ).astype(jnp.float32),
        lax.psum_scatter(
            shift_two_grad.astype(jnp.bfloat16), "fsdp", scatter_dimension=0, tiled=True
        ).astype(jnp.float32),
    )
    totals = (
        lax.psum(matrices[0].astype(jnp.bfloat16), "rep").astype(jnp.float32),
        lax.psum(matrices[1].astype(jnp.bfloat16), "rep").astype(jnp.float32),
        lax.psum(matrices[2].astype(jnp.bfloat16), "rep").astype(jnp.float32),
        lax.psum(matrices[3].astype(jnp.bfloat16), "rep").astype(jnp.float32),
        lax.psum(vectors[0].astype(jnp.bfloat16), "rep").astype(jnp.float32),
        lax.psum(vectors[1].astype(jnp.bfloat16), "rep").astype(jnp.float32),
        lax.psum(vectors[2].astype(jnp.bfloat16), "rep").astype(jnp.float32),
        lax.psum(vectors[3].astype(jnp.bfloat16), "rep").astype(jnp.float32),
        lax.psum(vectors[4].astype(jnp.bfloat16), "rep").astype(jnp.float32),
        lax.psum(up_share.astype(jnp.bfloat16), "rep").astype(jnp.float32),
        lax.psum(vectors[5].astype(jnp.bfloat16), "rep").astype(jnp.float32),
        lax.psum(down_share.astype(jnp.bfloat16), "rep").astype(jnp.float32),
        lax.psum(vectors[6].astype(jnp.bfloat16), "rep").astype(jnp.float32),
        lax.psum(vectors[7].astype(jnp.bfloat16), "rep").astype(jnp.float32),
        lax.psum(vectors[8].astype(jnp.bfloat16), "rep").astype(jnp.float32),
    )
    return (
        layer_out,
        tokens_grad,
        totals[0],
        totals[1],
        totals[2],
        totals[3],
        totals[4],
        totals[5],
        totals[6],
        totals[7],
        totals[8],
        totals[9],
        totals[10],
        totals[11],
        totals[12],
        totals[13],
        totals[14],
    )


def solution(mesh):
    placed = (
        P("rep", "fsdp", None),
        P("rep"),
        P("fsdp", None),
        P("fsdp", None),
        P("fsdp", None),
        P("fsdp", None),
        P("fsdp"),
        P("fsdp"),
        P("fsdp"),
        P("fsdp"),
        P("fsdp"),
        P("fsdp", None),
        P("fsdp"),
        P("fsdp", None),
        P("fsdp"),
        P("fsdp"),
        P("fsdp"),
        P("rep", "fsdp", None),
    )
    return jax.shard_map(
        local,
        mesh=mesh,
        in_specs=placed,
        out_specs=(
            P("rep", "fsdp", None),
            P("rep", "fsdp", None),
            P("fsdp", None),
            P("fsdp", None),
            P("fsdp", None),
            P("fsdp", None),
            P("fsdp"),
            P("fsdp"),
            P("fsdp"),
            P("fsdp"),
            P("fsdp"),
            P("fsdp", None),
            P("fsdp"),
            P("fsdp", None),
            P("fsdp"),
            P("fsdp"),
            P("fsdp"),
        ),
        check_vma=False,
    )
```

profile of v0, /device:TPU:18, one launch (start us, length us, event | category | flops | bytes accessed | tf_op | source)
XLA Modules:
  0.0 4510.4 jit_solution(8837136320118019839)
XLA Ops:
  19.9 138.6 %all-gather.23.cloned.1.call-done = bf16[2048,2048]{1,0:T(8,128)(2,1)} async-done(((bf16[512,2048]{1,0:T(8,128)(2,1)}), bf16[2048,2048]{1,0:T(8,128)(2,1)}) %all-gather.23.cloned.1.call-update) | async-done | bytes 8388624 | tf_op jit(solution)/shard_map/all_gather | solution.py:61
  167.7 140.4 %all-gather.29.cloned.1.call-done = bf16[2048,2048]{1,0:T(8,128)(2,1)} async-done(((bf16[512,2048]{1,0:T(8,128)(2,1)}), bf16[2048,2048]{1,0:T(8,128)(2,1)}) %all-gather.29.cloned.1.call-update) | async-done | bytes 8388624 | tf_op jit(solution)/shard_map/all_gather | solution.py:60
  471.7 136.9 %all-gather.25.cloned.1.call-done = bf16[2,1024,2048]{2,1,0:T(8,128)(2,1)} async-done(((bf16[2,256,2048]{2,1,0:T(8,128)(2,1)}), bf16[2,1024,2048]{2,1,0:T(8,128)(2,1)}) %all-gather.25.cloned.1.call-update) | async-done | bytes 8388624 | tf_op jit(solution)/shard_map/all_gather | solution.py:86
  620.6 137.3 %all-gather.31.cloned.1.call-done = bf16[2,1024,2048]{1,2,0:T(8,128)(2,1)} async-done(((bf16[2,256,2048]{1,2,0:T(8,128)(2,1)}), bf16[2,1024,2048]{1,2,0:T(8,128)(2,1)}) %all-gather.31.cloned.1.call-update) | async-done | bytes 8388624 | tf_op jit(solution)/shard_map/all_gather | solution.py:85
  811.9 95.4 %all-gather.33.cloned.1.call-done = bf16[2048,2048]{1,0:T(8,128)(2,1)} async-done(((bf16[512,2048]{1,0:T(8,128)(2,1)}), bf16[2048,2048]{1,0:T(8,128)(2,1)}) %all-gather.33.cloned.1.call-update) | async-done | bytes 8388624 | tf_op jit(solution)/shard_map/all_gather | solution.py:62
  919.3 549.1 %all-gather.35.cloned.1.call-done = bf16[2048,8192]{1,0:T(8,128)(2,1)} async-done(((bf16[512,8192]{1,0:T(8,128)(2,1)}), bf16[2048,8192]{1,0:T(8,128)(2,1)}) %all-gather.35.cloned.1.call-update) | async-done | bytes 33554448 | tf_op jit(solution)/shard_map/all_gather | solution.py:104
  1468.4 31.7 multiply_convert_fusion.2
  1500.2 529.4 %all-gather.37.cloned.1.call-done = bf16[8192,2048]{1,0:T(8,128)(2,1)} async-done(((bf16[2048,2048]{1,0:T(8,128)(2,1)}), bf16[8192,2048]{1,0:T(8,128)(2,1)}) %all-gather.37.cloned.1.call-update) | async-done | bytes 33554448 | tf_op jit(solution)/shard_map/all_gather | solution.py:105
  2065.0 35.0 fusion.29
  2100.0 28.0 multiply_reduce_fusion.3
  2148.4 28.3 multiply_reduce_fusion
  2176.8 27.9 multiply_convert_fusion
  2280.2 93.7 %reduce-scatter.3.cloned.1.call-done = bf16[2,256,2048]{2,1,0:T(8,128)(2,1)} async-done(((bf16[2,1024,2048]{2,1,0:T(8,128)(2,1)}), bf16[2,256,2048]{2,1,0:T(8,128)(2,1)}) %reduce-scatter.3.cloned.1.call-update) | async-done | bytes 2097168 | tf_op jit(solution)/shard_map/reduce_scatter | solution.py:247
  2373.9 147.4 %reduce-scatter.5.cloned.1.call-done = bf16[2,256,2048]{2,1,0:T(8,128)(2,1)} async-done(((bf16[2,1024,2048]{2,1,0:T(8,128)(2,1)}), bf16[2,256,2048]{2,1,0:T(8,128)(2,1)}) %reduce-scatter.5.cloned.1.call-update) | async-done | bytes 2097168 | tf_op jit(solution)/shard_map/reduce_scatter | solution.py:253
  2539.4 96.2 %all-to-all-done = bf16[512,4,512]{2,0,1:T(8,128)(2,1)} async-done(((bf16[512,4,512]{2,0,1:T(8,128)(2,1)}), bf16[512,4,512]{2,0,1:T(8,128)(2,1)}, u32[]{:S(2)}, u32[]{:S(2)}) %all-to-all-start) | async-done | bytes 2097184 | tf_op jit(solution)/shard_map/all_to_all | solution.py:274
  2654.8 85.9 %all-to-all-done.1 = bf16[512,4,512]{2,0,1:T(8,128)(2,1)S(1)} async-done(((bf16[512,4,512]{2,0,1:T(8,128)(2,1)}), bf16[512,4,512]{2,0,1:T(8,128)(2,1)S(1)}, u32[]{:S(2)}, u32[]{:S(2)}) %all-to-all-start.1) | async-done | bytes 2097184 | tf_op jit(solution)/shard_map/all_to_all | solution.py:275
  2752.9 61.3 %all-gather.45.cloned.1.call-done = bf16[2048,2048]{1,0:T(8,128)(2,1)} async-done(((bf16[512,2048]{1,0:T(8,128)(2,1)}), bf16[2048,2048]{1,0:T(8,128)(2,1)}) %all-gather.45.cloned.1.call-update) | async-done | bytes 8388624 | tf_op jit(solution)/shard_map/all_gather | solution.py:283
  2824.2 249.5 %all-gather.39.cloned.1.call-done = bf16[2048,2048]{1,0:T(8,128)(2,1)} async-done(((bf16[512,2048]{1,0:T(8,128)(2,1)}), bf16[2048,2048]{1,0:T(8,128)(2,1)}) %all-gather.39.cloned.1.call-update) | async-done | bytes 8388624 | tf_op jit(solution)/shard_map/all_gather | solution.py:280
  3090.8 177.1 %all-gather.49.cloned.1.call-done = bf16[2048,2048]{1,0:T(8,128)(2,1)} async-done(((bf16[512,2048]{1,0:T(8,128)(2,1)}), bf16[2048,2048]{1,0:T(8,128)(2,1)}) %all-gather.49.cloned.1.call-update) | async-done | bytes 8388624 | tf_op jit(solution)/shard_map/all_gather | solution.py:285
  3291.8 126.7 %all-gather.41.cloned.1.call-done = bf16[2048,2048]{1,0:T(8,128)(2,1)} async-done(((bf16[512,2048]{1,0:T(8,128)(2,1)}), bf16[2048,2048]{1,0:T(8,128)(2,1)}) %all-gather.41.cloned.1.call-update) | async-done | bytes 8388624 | tf_op jit(solution)/shard_map/all_gather | solution.py:281
  3428.4 139.4 %all-gather.43.cloned.1.call-done = bf16[2048,2048]{1,0:T(8,128)(2,1)} async-done(((bf16[512,2048]{1,0:T(8,128)(2,1)}), bf16[2048,2048]{1,0:T(8,128)(2,1)}) %all-gather.43.cloned.1.call-update) | async-done | bytes 8388624 | tf_op jit(solution)/shard_map/all_gather | solution.py:282
  3577.7 551.2 %all-gather.47.cloned.1.call-done = bf16[2048,8192]{1,0:T(8,128)(2,1)} async-done(((bf16[512,8192]{1,0:T(8,128)(2,1)}), bf16[2048,8192]{1,0:T(8,128)(2,1)}) %all-gather.47.cloned.1.call-update) | async-done | bytes 33554448 | tf_op jit(solution)/shard_map/all_gather | solution.py:284
  4128.9 26.2 convolution_convert_fusion
  4237.3 229.1 %all-reduce.14.cloned.1.call-done = (bf16[512,2048]{0,1:T(8,128)(2,1)}, bf16[512,2048]{0,1:T(8,128)(2,1)}, bf16[512,2048]{0,1:T(8,128)(2,1)}, bf16[512,2048]{1,0...) async-done(((bf16[512,2048]{0,1:T(8,128)(2,1)}, bf16[512,2048]{0,1:T(8,128)(2,1)}, bf16[512,2048]{0,1:T(8,128)(2,1)}, bf16[512,2048]{1,0:T(8,128)(2,1)}, ...) | async-done | bytes 25165840 | tf_op jit(solution)/shard_map/psum | solution.py:325
  (261 shorter events, 632.6 us)
Async XLA Ops:
  7.2 151.4 %all-gather.23.cloned.1.call-start = ((), (), s32[]{:S(2)}) async-start(), calls=%async_computation.6 | async-start | bytes 10485760 | tf_op jit(solution)/shard_map/all_gather | solution.py:61
  7.9 300.1 %all-gather.29.cloned.1.call-start = ((), (), s32[]{:S(2)}) async-start(), calls=%async_computation.9 | async-start | bytes 10485760 | tf_op jit(solution)/shard_map/all_gather | solution.py:60
  8.7 449.8 %all-gather.27.cloned.1.call-start = ((), (), s32[]{:S(2)}) async-start(), calls=%async_computation.8 | async-start | bytes 10485760 | tf_op jit(solution)/shard_map/all_gather | solution.py:59
  9.4 599.2 %all-gather.25.cloned.1.call-start = ((), (), s32[]{:S(2)}) async-start(), calls=%async_computation.7 | async-start | bytes 10485760 | tf_op jit(solution)/shard_map/all_gather | solution.py:86
  167.6 590.3 %all-gather.31.cloned.1.call-start = ((), (), s32[]{:S(2)}) async-start(), calls=%async_computation.10 | async-start | bytes 10485760 | tf_op jit(solution)/shard_map/all_gather | solution.py:85
  321.2 586.1 %all-gather.33.cloned.1.call-start = ((), (), s32[]{:S(2)}) async-start(), calls=%async_computation.11 | async-start | bytes 10485760 | tf_op jit(solution)/shard_map/all_gather | solution.py:62
  321.7 1146.7 %all-gather.35.cloned.1.call-start = ((), (), s32[]{:S(2)}) async-start(), calls=%async_computation.12 | async-start | bytes 41943040 | tf_op jit(solution)/shard_map/all_gather | solution.py:104
  322.6 1707.0 %all-gather.37.cloned.1.call-start = ((), (), s32[]{:S(2)}) async-start(), calls=%async_computation.13 | async-start | bytes 41943040 | tf_op jit(solution)/shard_map/all_gather | solution.py:105
  323.4 2050.5 %reduce-scatter.3.cloned.1.call-start = ((), (), s32[]{:S(2)}) async-start(), calls=%async_computation.14 | async-start | bytes 10485760 | tf_op jit(solution)/shard_map/reduce_scatter | solution.py:247
  441.0 351.8 %copy-start.26 = (pred[2,1024]{1,0:T(4,128)(4,1)}, pred[2,1024]{1,0:T(4,128)(4,1)S(1)}, u32[]{:S(2)}) copy-start(pred[2,1024]{1,0:T(4,128)(4,1)S(1)} %iota_compare_fusion) | copy-start | bytes 6148
  916.5 583.7 %copy-start.30 = (f32[512]{0:T(512)}, f32[512]{0:T(512)S(1)}, u32[]{:S(2)}) copy-start(f32[512]{0:T(512)S(1)} %multiply_reduce_fusion.7) | copy-start | bytes 6148
  919.3 580.9 %copy-start.17 = (bf16[512,2048]{1,0:T(8,128)(2,1)}, bf16[512,2048]{1,0:T(8,128)(2,1)S(1)}, u32[]{:S(2)}) copy-start(bf16[512,2048]{1,0:T(8,128)(2,1)S(1)} %fusion.10) | copy-start | bytes 6291460
  2228.5 292.8 %reduce-scatter.5.cloned.1.call-start = ((), (), s32[]{:S(2)}) async-start(), calls=%async_computation.15 | async-start | bytes 10485760 | tf_op jit(solution)/shard_map/reduce_scatter | solution.py:253
  2261.2 553.0 %all-gather.45.cloned.1.call-start = ((), (), s32[]{:S(2)}) async-start(), calls=%async_computation.19 | async-start | bytes 10485760 | tf_op jit(solution)/shard_map/all_gather | solution.py:283
  2262.0 811.7 %all-gather.39.cloned.1.call-start = ((), (), s32[]{:S(2)}) async-start(), calls=%async_computation.16 | async-start | bytes 10485760 | tf_op jit(solution)/shard_map/all_gather | solution.py:280
  2279.4 988.6 %all-gather.49.cloned.1.call-start = ((), (), s32[]{:S(2)}) async-start(), calls=%async_computation.21 | async-start | bytes 10485760 | tf_op jit(solution)/shard_map/all_gather | solution.py:285
  2280.2 1138.4 %all-gather.41.cloned.1.call-start = ((), (), s32[]{:S(2)}) async-start(), calls=%async_computation.17 | async-start | bytes 10485760 | tf_op jit(solution)/shard_map/all_gather | solution.py:281
  2373.9 1193.9 %all-gather.43.cloned.1.call-start = ((), (), s32[]{:S(2)}) async-start(), calls=%async_computation.18 | async-start | bytes 10485760 | tf_op jit(solution)/shard_map/all_gather | solution.py:282
  2521.3 1607.6 %all-gather.47.cloned.1.call-start = ((), (), s32[]{:S(2)}) async-start(), calls=%async_computation.20 | async-start | bytes 41943040 | tf_op jit(solution)/shard_map/all_gather | solution.py:284
  2529.1 106.4 %all-to-all-start = ((bf16[512,4,512]{2,0,1:T(8,128)(2,1)}), bf16[512,4,512]{2,0,1:T(8,128)(2,1)}, u32[]{:S(2)}, u32[]{:S(2)}) async-start(bf16[512,4,512]{2,0,1:T(8,128)(2,1)} %copy.96), calls=%async_computation.2 | async-start | bytes 4194304 | tf_op jit(solution)/shard_map/all_to_all | solution.py:274
  2635.5 105.1 %all-to-all-start.1 = ((bf16[512,4,512]{2,0,1:T(8,128)(2,1)}), bf16[512,4,512]{2,0,1:T(8,128)(2,1)S(1)}, u32[]{:S(2)}, u32[]{:S(2)}) async-start(bf16[512,4,512]{2,0,1:T(8,128)(2,1)} %copy.98), calls=%async_computation.3 | async-start | bytes 4194304 | tf_op jit(solution)/shard_map/all_to_all | solution.py:275
  2742.0 341.6 %all-to-all-start.3 = ((bf16[512,4,2048]{2,0,1:T(8,128)(2,1)}), bf16[512,4,2048]{2,0,1:T(8,128)(2,1)}, u32[]{:S(2)}, u32[]{:S(2)}) async-start(bf16[512,4,2048]{2,0,1:T(8,128)(2,1)} %bitcast.140), calls=%async_computation.5 | async-start | bytes 16777216 | tf_op jit(solution)/shard_map/all_to_all | solution.py:277
  3083.6 494.1 %all-to-all-start.2 = ((bf16[512,4,512]{2,0,1:T(8,128)(2,1)}), bf16[512,4,512]{2,0,1:T(8,128)(2,1)S(1)}, u32[]{:S(2)}, u32[]{:S(2)}) async-start(bf16[512,4,512]{2,0,1:T(8,128)(2,1)} %bitcast.134), calls=%async_computation.4 | async-start | bytes 4194304 | tf_op jit(solution)/shard_map/all_to_all | solution.py:276
  3090.8 1375.6 %all-reduce.14.cloned.1.call-start = ((), (), s32[]{:S(2)}) async-start(), calls=%async_computation.22 | async-start | bytes 50331648 | tf_op jit(solution)/shard_map/psum | solution.py:325
  (50 other events, 1382.7 us)
Sparse Core Ops, SparseCore 0:
  9.6 148.9 all-gather.22
  160.1 147.8 all-gather.28
  309.6 148.7 all-gather.26
  460.4 148.0 all-gather.24
  610.6 147.3 all-gather.30
  759.3 147.8 all-gather.32
  908.8 559.5 all-gather.34
  1470.0 559.5 all-gather.36
  2228.6 145.1 reduce-scatter.2
  2376.1 145.1 reduce-scatter.4
  2522.9 291.3 all-gather.44
  2816.2 257.4 all-gather.38
  3075.3 192.6 all-gather.48
  3269.4 149.0 all-gather.40
  3419.9 147.8 all-gather.42
  3569.3 559.5 all-gather.46
  4155.2 311.1 all-reduce.13
where the time goes:
time: 4520 us; the launch traced here: 4510 us
  waiting for transfers between devices  3710 us (82%)
  matrix products  392 us (9%)
  blocking collectives  164 us (4%)
  local copies, waits for them, and re-layouts  107 us (2%)
  other arithmetic  90.6 us (2%)
    all_gather x1, waiting for transfers between devices, local(): lax.all_gather(dbefore, 'fsdp', axis=0, tiled=True)  551 us
    all_gather x1, waiting for transfers between devices, forward(): lax.all_gather(up_weight, 'fsdp', axis=0, tiled=True)  549 us
    all_gather x1, waiting for transfers between devices, forward(): lax.all_gather(down_weight, 'fsdp', axis=0, tiled=True)  529 us
    all_gather x1, waiting for transfers between devices, local(): lax.all_gather(dquery, 'fsdp', axis=0, tiled=True)  250 us
    psum x1, waiting for transfers between devices, local(): lax.psum(matrices[0].astype(jnp.bfloat16), 'rep').astype(jnp.float32)  229 us
    all_gather x1, waiting for transfers between devices, local(): lax.all_gather(ddown, 'fsdp', axis=0, tiled=True)  177 us
    reduce_scatter x1, waiting for transfers between devices, local(): lax.psum_scatter(dvalues_all.reshape(slots_here, seqlen, width).astype(jn...  147 us
    all_gather x1, waiting for transfers between devices, forward(): lax.all_gather(key_weight, 'fsdp', axis=0, tiled=True)  140 us
  transfers between devices with their start and end apart: 21, of which 19 were waited for; matrix products, arithmetic and copies ran while one was open for 7% of the time, Pallas kernels for 0%

commit v1 on v0

v1 whole, which is shorter than its diff:
```python
import jax
import jax.numpy as jnp
from jax import lax
from jax.sharding import PartitionSpec as P

HEADS = 16
TEAM = 4
EPSILON = 1e-06
BF = jnp.bfloat16
F32 = jnp.float32


def mm(left, right):
    return jnp.dot(left, right, preferred_element_type=F32)


def mm_t(left, right):
    return lax.dot_general(left, right, (((1,), (1,)), ((), ())), preferred_element_type=F32)


def t_mm(left, right):
    return lax.dot_general(left, right, (((0,), (0,)), ((), ())), preferred_element_type=F32)


def pick(array, index, axis=0):
    return lax.dynamic_index_in_dim(array, index, axis, keepdims=False)


def normalise(summed):
    center = summed - jnp.mean(summed, axis=-1, keepdims=True)
    spread = jnp.mean(center * center, axis=-1, keepdims=True)
    scale = lax.rsqrt(spread + EPSILON)
    return center * scale, scale


def norm_backward(grad, gain, normal, scale):
    dn = grad * gain
    first = jnp.mean(dn, axis=-1, keepdims=True)
    second = jnp.mean(dn * normal, axis=-1, keepdims=True)
    return scale * (dn - first - normal * second)


def gelu_parts(u):
    inner = 0.7978845608 * (u + 0.044715 * u * u * u)
    t = jnp.tanh(inner)
    value = 0.5 * u * (1.0 + t)
    slope = 0.5 * (1.0 + t) + 0.5 * u * (1.0 - t * t) * 0.7978845608 * (
        1.0 + 3.0 * 0.044715 * u * u
    )
    return value, slope


def attend(query, keys, values, mask, scaling):
    scores = jnp.einsum("qhd,khd->hqk", query, keys, preferred_element_type=F32) * scaling
    scores = jnp.where(mask[None, None, :], scores, -1e30)
    log_total = jax.nn.logsumexp(scores, axis=-1, keepdims=True)
    probs = jnp.exp(scores - log_total).astype(BF)
    context = jnp.einsum("hqk,khd->qhd", probs, values, preferred_element_type=F32)
    return context.astype(BF), log_total


def attend_backward(query, keys, values, mask, log_total, dcontext, scaling):
    scores = jnp.einsum("qhd,khd->hqk", query, keys, preferred_element_type=F32) * scaling
    scores = jnp.where(mask[None, None, :], scores, -1e30)
    probs = jnp.exp(scores - log_total)
    low = probs.astype(BF)
    dprobs = jnp.einsum("qhd,khd->hqk", dcontext, values, preferred_element_type=F32)
    delta = jnp.sum(dprobs * probs, axis=-1, keepdims=True)
    dscores = (probs * (dprobs - delta)).astype(BF)
    dvalues = jnp.einsum("hqk,qhd->khd", low, dcontext, preferred_element_type=F32)
    dkeys = jnp.einsum("hqk,qhd->khd", dscores, query, preferred_element_type=F32) * scaling
    dquery = jnp.einsum("hqk,khd->qhd", dscores, keys, preferred_element_type=F32) * scaling
    return dquery.astype(BF), dkeys.astype(BF), dvalues.astype(BF)


def local(
    tokens,
    lengths,
    query_weight,
    key_weight,
    value_weight,
    out_weight,
    query_bias,
    value_bias,
    out_bias,
    first_gain,
    first_shift,
    up_weight,
    up_bias,
    down_weight,
    down_bias,
    second_gain,
    second_shift,
    cotangent,
):
    slots_here, block, width = tokens.shape
    reps, parts = lax.axis_size("rep"), lax.axis_size("fsdp")
    copies = reps // TEAM
    hidden = up_weight.shape[1]
    shard = query_weight.shape[0]
    head_dim = width // HEADS
    scaling = head_dim ** (-0.5)
    rep, z = lax.axis_index("rep"), lax.axis_index("fsdp")
    q, d = rep % TEAM, rep // TEAM
    parity = z % 2
    team_slots = TEAM * slots_here
    held = team_slots // parts
    rows = slots_here * block
    heads_each = HEADS // reps

    def swap(x, mask):
        return lax.ppermute(x, "rep", [(i, i ^ mask) for i in range(reps)])

    def routes(turn):
        pairs = []
        for copy in range(copies):
            for member in range(TEAM):
                for place in range(parts):
                    i = (place + turn) % 2
                    slot = member * slots_here + i
                    to_place = slot % parts
                    to_member = ((slot // parts) * parts + place) // 2
                    pairs.append(
                        (
                            (copy * TEAM + member) * parts + place,
                            (copy * TEAM + to_member) * parts + to_place,
                        )
                    )
        return pairs

    even, odd = routes(0), routes(1)
    axes = ("rep", "fsdp")

    def to_team(x):
        first = lax.ppermute(pick(x, parity), axes, even)
        second = lax.ppermute(pick(x, 1 - parity), axes, odd)
        return jnp.concatenate([first, second], axis=0)

    def from_team(x):
        first = lax.ppermute(x[:block], axes, [(b, a) for a, b in even])
        second = lax.ppermute(x[block:], axes, [(b, a) for a, b in odd])
        straight = jnp.stack([first, second])
        turned = jnp.stack([second, first])
        return jnp.where(parity == 0, straight, turned)

    def team_rows(own):
        far = swap(own, 2)
        mine = jnp.concatenate([own, swap(own, 1)], axis=0)
        other = jnp.concatenate([far, swap(far, 1)], axis=0)
        return mine, other

    def team_sum(mine, other):
        far = other[:rows] + swap(other[rows:].astype(BF), 1).astype(F32)
        far = swap(far.astype(BF), 2).astype(F32)
        near = swap(mine[rows:].astype(BF), 1).astype(F32)
        return mine[:rows] + near + far

    all_lengths = lax.all_gather(lengths, "rep", axis=0, tiled=True)

    def row_places(member):
        place = []
        for o in (parity, 1 - parity):
            at = (member * 2 + o) % parts
            place.append(at * block + jnp.arange(block))
        return jnp.concatenate(place)

    def slot_length(member):
        return all_lengths[d * team_slots + ((member * 2) // parts) * parts + z]

    members = [q ^ m for m in range(TEAM)]
    masks = [row_places(m) < slot_length(m) for m in members]
    valid = masks[0].astype(F32)[:, None]

    def by_slot(mine, other):
        if held == 2:
            return [mine, other]
        return [jnp.concatenate([mine, other], axis=0)]

    def by_pair(pieces):
        if held == 2:
            return pieces
        whole = pieces[0]
        return [whole[: 2 * rows], whole[2 * rows :]]

    key_masks = by_slot(jnp.concatenate(masks[:2]), jnp.concatenate(masks[2:]))

    def head_columns(w, e):
        lead = w.shape[:-1]
        split = w.reshape(lead + (copies, heads_each, TEAM, head_dim))
        at = len(lead)
        split = pick(pick(split, e, at), q, at + 1)
        return split.reshape(lead + (heads_each * head_dim,))

    def over_z(x):
        return lax.all_gather(x, "fsdp", axis=0, tiled=True)

    def spread(x):
        return [x] + [swap(x, TEAM * m) for m in range(1, copies)]

    qkv_own = jnp.concatenate(
        [head_columns(w, d) for w in (query_weight, key_weight, value_weight)], axis=1
    )
    span = heads_each * head_dim
    qkv = spread(over_z(qkv_own))

    vectors = jnp.concatenate(
        [
            query_bias,
            value_bias,
            out_bias,
            first_gain,
            first_shift,
            down_bias,
            second_gain,
            second_shift,
            up_bias,
        ]
    )
    vectors = lax.all_gather(vectors, "fsdp", axis=0, tiled=False).astype(F32)
    names = [vectors[:, i * shard : (i + 1) * shard].reshape(width) for i in range(8)]
    bias_query, bias_value, bias_out, gain_one, shift_one, bias_down, gain_two, shift_two = names
    bias_up = vectors[:, 8 * shard :].reshape(parts, reps, hidden // parts // reps)

    per_shard = HEADS // parts
    split_out = out_weight.reshape(-1, head_dim, copies, width // copies)
    split_out = pick(split_out, d, 2)
    if per_shard >= TEAM:
        split_out = split_out.reshape(per_shard // TEAM, TEAM, head_dim, width // copies)
        out_own = pick(split_out, q, 1)
        out_all = over_z(out_own)
    else:
        out_own = pick(split_out, q % per_shard, 0)[None]
        out_all = over_z(out_own).reshape(HEADS // TEAM, TEAM // per_shard, head_dim, -1)
        out_all = pick(out_all, q // per_shard, 1)
    out_columns = jnp.stack(spread(out_all.reshape(HEADS // TEAM * head_dim, width // copies)))
    out_full = jnp.concatenate([pick(out_columns, d ^ e) for e in range(copies)], axis=1)
    out_rows = [
        lax.dynamic_slice_in_dim(out_full, (d ^ m) * span, span, 0) for m in range(copies)
    ]
    out_rel = jnp.concatenate(out_rows, axis=0)

    unit = hidden // parts // reps
    up_own = pick(up_weight.reshape(shard, parts, reps, unit), rep, 2).reshape(shard, parts * unit)
    down_own = pick(down_weight.reshape(reps, unit, width), rep, 0)
    up = spread(over_z(up_own))
    down = spread(over_z(down_own))
    up_biases = [pick(bias_up, rep ^ (TEAM * m), 1).reshape(1, -1) for m in range(copies)]

    own_tokens = to_team(tokens)
    tokens_mine, tokens_other = team_rows(own_tokens)
    slot_tokens = by_slot(tokens_mine, tokens_other)
    kept = []
    contexts = []
    for tok, mask in zip(slot_tokens, key_masks):
        per_part = []
        context = []
        for m in range(copies):
            both = mm(tok, qkv[m])
            shape = (tok.shape[0], heads_each, head_dim)
            qb = head_columns(bias_query, d ^ m)
            vb = head_columns(bias_value, d ^ m)
            query = (both[:, :span] + qb).astype(BF).reshape(shape)
            keys = both[:, span : 2 * span].astype(BF).reshape(shape)
            values = (both[:, 2 * span :] + vb).astype(BF).reshape(shape)
            ctx, log_total = attend(query, keys, values, mask, scaling)
            per_part.append((query, keys, values, log_total))
            context.append(ctx.reshape(tok.shape[0], span))
        kept.append(per_part)
        contexts.append(jnp.concatenate(context, axis=1))
    partial = by_pair([mm(ctx, out_rel) for ctx in contexts])
    attended = team_sum(*partial)
    summed1 = own_tokens.astype(F32) + attended + bias_out
    normal1, scale1 = normalise(summed1)
    normed1 = normal1 * gain_one + shift_one
    hidden_pairs = team_rows(normed1.astype(BF))

    slopes, active, partial = [], [], []
    for rows_in in hidden_pairs:
        slope_parts, active_parts = [], []
        total = 0.0
        for m in range(copies):
            before = mm(rows_in, up[m]) + up_biases[m]
            value, slope = gelu_parts(before)
            value = value.astype(BF)
            slope_parts.append(slope)
            active_parts.append(value)
            total = total + mm(value, down[m])
        slopes.append(slope_parts)
        active.append(active_parts)
        partial.append(total)
    summed2 = normed1 + team_sum(*partial) + bias_down
    normal2, scale2 = normalise(summed2)
    result = valid * (normal2 * gain_two + shift_two)
    layer_out = from_team(result.astype(BF))

    grad_out = to_team(cotangent).astype(F32) * valid
    dsum2 = norm_backward(grad_out, gain_two, normal2, scale2)
    gain_two_grad = jnp.sum(grad_out * normal2, axis=0)
    shift_two_grad = jnp.sum(grad_out, axis=0)
    ddown = dsum2.astype(BF)
    down_bias_grad = jnp.sum(ddown.astype(F32), axis=0)
    ddown_pairs = team_rows(ddown)
    partial, dbefores = [], []
    for i, rows_in in enumerate(ddown_pairs):
        total = 0.0
        dbefore_parts = []
        for m in range(copies):
            dbefore = (mm_t(rows_in, down[m]) * slopes[i][m]).astype(BF)
            dbefore_parts.append(dbefore)
            total = total + mm_t(dbefore, up[m])
        dbefores.append(dbefore_parts)
        partial.append(total)
    dnormed1 = dsum2 + team_sum(*partial)
    dsum1 = norm_backward(dnormed1, gain_one, normal1, scale1)
    gain_one_grad = jnp.sum(dnormed1 * normal1, axis=0)
    shift_one_grad = jnp.sum(dnormed1, axis=0)
    dattn = dsum1.astype(BF)
    out_bias_grad = jnp.sum(dattn.astype(F32), axis=0)

    def over_copies(shares):
        total = shares[0]
        for m in range(1, copies):
            total = total + swap(shares[m].astype(BF), TEAM * m).astype(F32)
        return total.astype(BF)

    def to_owner(x):
        return lax.psum_scatter(x, "fsdp", scatter_dimension=0, tiled=True)

    def from_all(x):
        return lax.all_gather(x, "rep", axis=0, tiled=False)

    down_share = over_copies(
        [
            t_mm(active[0][m], ddown_pairs[0]) + t_mm(active[1][m], ddown_pairs[1])
            for m in range(copies)
        ]
    )
    down_grad = from_all(to_owner(down_share)).reshape(reps * unit, width).astype(F32)
    up_share = over_copies(
        [
            t_mm(hidden_pairs[0], dbefores[0][m]) + t_mm(hidden_pairs[1], dbefores[1][m])
            for m in range(copies)
        ]
    )
    up_grad = from_all(to_owner(up_share)).reshape(reps, shard, parts, unit)
    up_grad = up_grad.transpose(1, 2, 0, 3).reshape(shard, hidden).astype(F32)

    dattn_slots = by_slot(*team_rows(dattn))
    out_share = 0.0
    partial = []
    qkv_shares = [0.0] * copies
    query_sums, value_sums = [0.0] * copies, [0.0] * copies
    for i, rows_in in enumerate(dattn_slots):
        out_share = out_share + t_mm(contexts[i], rows_in)
        dcontext = mm_t(rows_in, out_rel).astype(BF)
        total = 0.0
        for m in range(copies):
            query, keys, values, log_total = kept[i][m]
            dctx = dcontext[:, m * span : (m + 1) * span].reshape(query.shape)
            dq, dk, dv = attend_backward(
                query, keys, values, key_masks[i], log_total, dctx, scaling
            )
            both = jnp.concatenate([g.reshape(-1, span) for g in (dq, dk, dv)], axis=1)
            total = total + mm_t(both, qkv[m])
            qkv_shares[m] = qkv_shares[m] + t_mm(slot_tokens[i], both)
            sums = jnp.sum(both.astype(F32), axis=0)
            query_sums[m] = query_sums[m] + sums[:span]
            value_sums[m] = value_sums[m] + sums[2 * span :]
        partial.append(total)
    dtokens = dsum1 + team_sum(*by_pair(partial))
    tokens_grad = from_team(dtokens.astype(BF)).astype(F32)

    out_rows = [
        lax.dynamic_slice_in_dim(out_share, (d ^ e) * span, span, 0) for e in range(copies)
    ]
    out_rows = jnp.concatenate(out_rows, axis=0).reshape(-1, copies, width // copies)
    out_mine = over_copies([pick(out_rows, d ^ m, 1) for m in range(copies)])
    if per_shard >= TEAM:
        out_final = to_owner(out_mine)
        out_final = out_final.reshape(per_shard // TEAM, head_dim, -1)
        out_grad = from_all(out_final)
        out_grad = out_grad.reshape(
            copies, TEAM, per_shard // TEAM, head_dim, width // copies
        ).transpose(2, 1, 3, 0, 4)
    else:
        fill = TEAM // per_shard
        out_mine = out_mine.reshape(HEADS // TEAM, 1, head_dim, -1)
        chosen = (jnp.arange(fill) == q // per_shard)[None, :, None, None]
        out_mine = jnp.where(chosen, out_mine, jnp.zeros((), BF))
        out_final = to_owner(out_mine.reshape(parts * head_dim, -1))
        out_grad = from_all(out_final).reshape(
            copies, fill, per_shard, head_dim, width // copies
        )
        out_grad = pick(out_grad, z % fill, 1).transpose(1, 2, 0, 3)
    out_grad = out_grad.reshape(-1, width).astype(F32)

    qkv_final = from_all(to_owner(over_copies(qkv_shares)))
    qkv_final = qkv_final.reshape(copies, TEAM, shard, 3, heads_each, head_dim)
    qkv_grads = [
        qkv_final[:, :, :, i].transpose(2, 0, 3, 1, 4).reshape(shard, width).astype(F32)
        for i in range(3)
    ]

    def place_heads(shares):
        full = jnp.zeros((copies, heads_each, TEAM, head_dim), F32)
        for m in range(copies):
            share = shares[m].reshape(1, heads_each, 1, head_dim)
            full = lax.dynamic_update_slice(full, share, (d ^ m, 0, q, 0))
        return full.reshape(width)

    up_sums = jnp.zeros((parts, reps, unit), F32)
    for m in range(copies):
        share = sum(jnp.sum(pair[m].astype(F32), axis=0) for pair in dbefores)
        up_sums = lax.dynamic_update_slice(
            up_sums, share.reshape(parts, 1, unit), (0, rep ^ (TEAM * m), 0)
        )
    sums = [
        place_heads(query_sums),
        place_heads(value_sums),
        out_bias_grad,
        gain_one_grad,
        shift_one_grad,
        down_bias_grad,
        gain_two_grad,
        shift_two_grad,
    ]
    sums = jnp.concatenate([s.reshape(parts, shard) for s in sums] + [up_sums.reshape(parts, -1)], axis=1)
    sums = pick(lax.psum(sums, ("rep", "fsdp")), z)
    small = [sums[i * shard : (i + 1) * shard] for i in range(8)]
    up_bias_grad = sums[8 * shard :]
    return (
        layer_out,
        tokens_grad,
        qkv_grads[0],
        qkv_grads[1],
        qkv_grads[2],
        out_grad,
        small[0],
        small[1],
        small[2],
        small[3],
        small[4],
        up_grad,
        up_bias_grad,
        down_grad,
        small[5],
        small[6],
        small[7],
    )


def solution(mesh):
    three, two, one = P("rep", "fsdp", None), P("fsdp", None), P("fsdp")
    placed = (three, P("rep"), two, two, two, two, one, one, one, one, one)
    placed += (two, one, two, one, one, one, three)
    given = (three, three, two, two, two, two, one, one, one, one, one)
    given += (two, one, two, one, one, one)
    return jax.shard_map(local, mesh=mesh, in_specs=placed, out_specs=given, check_vma=False)
```

time: 4520 us -> 1820 us (0.40)
  waiting for transfers between devices: 3710 us -> 1000 us
  blocking collectives: 164 us -> 36.2 us
  local copies, waits for them, and re-layouts: 107 us -> 205 us
  other arithmetic: 90.6 us -> 152 us
    all_gather x14 -> x8, waiting for transfers between devices: 3050 us -> 113 us  [the longest x4 113 us: from_all(): return lax.all_gather(x, 'rep', axis=0, tiled=False)]
    ppermute x0 -> x40, waiting for transfers between devices: none -> 769 us  [the longest x32 674 us: swap(): return lax.ppermute(x, 'rep', [(i, i ^ mask) for i in range(reps)])]
    reduce_scatter x2 -> x4, waiting for transfers between devices: 241 us -> 55.1 us  [to_owner(): return lax.psum_scatter(x, 'fsdp', scatter_dimension=0, tiled=True)]
    all_to_all x4 -> x0, waiting for transfers between devices: 182 us -> none  [the longest x1 96.2 us: local(): lax.all_to_all(flat, 'fsdp', split_axis=1, concat_axis=0, tiled=True)]
    psum x1, waiting for transfers between devices: 229 us -> 62.4 us  [local(): sums = pick(lax.psum(sums, ('rep', 'fsdp')), z)]
    all_gather x9 -> x1, blocking collectives: 125 us -> 11.6 us  [local(): vectors = lax.all_gather(vectors, 'fsdp', axis=0, tiled=False).astype(F32)]
    unnamed x131 -> x401, local copies, waits for them, and re-layouts: 32.7 us -> 79.1 us
    dot_general x24 -> x66, matrix products: 392 us -> 349 us  [the longest x14 105 us: mm_t(): lax.dot_general(left, right, (((1,), (1,)), ((), ())), preferred_element_...]
  transfers between devices with their start and end apart: 21 -> 53, of which waited for: 19 -> 22; matrix products, arithmetic and copies ran while one was open for 7% -> 31% of each run, Pallas kernels for 0% -> 0%
where the time goes in v1:
time: 1820 us; the launch traced here: 1800 us
  waiting for transfers between devices  1000 us (55%)
  matrix products  349 us (19%)
  local copies, waits for them, and re-layouts  205 us (11%)
  other arithmetic  152 us (8%)
  starting transfers between devices  41.5 us (2%)
  blocking collectives  36.2 us (2%)
    ppermute x32, waiting for transfers between devices, swap(): return lax.ppermute(x, 'rep', [(i, i ^ mask) for i in range(reps)])  674 us
    all_gather x4, waiting for transfers between devices, from_all(): return lax.all_gather(x, 'rep', axis=0, tiled=False)  113 us
    dot_general x14, matrix products, mm_t(): lax.dot_general(left, right, (((1,), (1,)), ((), ())), preferred_element_...  105 us
    dot_general x14, matrix products, t_mm(): lax.dot_general(left, right, (((0,), (0,)), ((), ())), preferred_element_...  94.5 us
    unnamed x401, local copies, waits for them, and re-layouts  79.1 us
    dot_general x14, matrix products, mm(): return jnp.dot(left, right, preferred_element_type=F32)  78.9 us
    psum x1, waiting for transfers between devices, local(): sums = pick(lax.psum(sums, ('rep', 'fsdp')), z)  62.4 us
    reduce_scatter x4, waiting for transfers between devices, to_owner(): return lax.psum_scatter(x, 'fsdp', scatter_dimension=0, tiled=True)  55.1 us
  transfers between devices with their start and end apart: 53, of which 22 were waited for; matrix products, arithmetic and copies ran while one was open for 31% of the time, Pallas kernels for 0%

profile of v1, /device:TPU:18, one launch (start us, length us, event | category | flops | bytes accessed | tf_op | source)
XLA Modules:
  0.0 1804.4 jit_solution(18295616831885969260)
XLA Ops:
  45.3 54.5 %collective-permute-done = bf16[256,2048]{1,0:T(8,128)(2,1)S(1)} collective-permute-done((bf16[256,2048]{1,0:T(8,128)(2,1)S(1)}, bf16[256,2048]{1,0:T(8,128)(2,1)S(1)}, u32[]{:S(2)}, u32[]{:S(2)}) %collective-permute-start) | collective-permute-done | bytes 1048608 | tf_op jit(solution)/shard_map/ppermute | solution.py:135
  101.0 40.8 %collective-permute-done.1 = bf16[256,2048]{1,0:T(8,128)(2,1)S(1)} collective-permute-done((bf16[256,2048]{1,0:T(8,128)(2,1)S(1)}, bf16[256,2048]{1,0:T(8,128)(2,1)S(1)}, u32[]{:S(2)}, u32[]{:S(2)}) %collective-permute-start.1) | collective-permute-done | bytes 1048608 | tf_op jit(solution)/shard_map/ppermute | solution.py:136
  147.8 24.6 %all-reduce = s32[16]{0:T(128)S(1)} all-reduce(s32[16]{0:T(128)S(1)} %dynamic-update-slice), channel_id=1, replica_groups=mesh['rep'=8,'fsdp'=4] {'rep'}, use_global_device_ids=true, to_apply=%add | all-reduce | flops 16 | bytes 128
  222.6 50.8 %collective-permute-done.3 = bf16[2048,768]{0,1:T(8,128)(2,1)S(1)} collective-permute-done((bf16[2048,768]{0,1:T(8,128)(2,1)}, bf16[2048,768]{0,1:T(8,128)(2,1)S(1)}, u32[]{:S(2)}, u32[]{:S(2)}) %collective-permute-start.3) | collective-permute-done | bytes 3145760 | tf_op jit(solution)/shard_map/ppermute | solution.py:112
  331.8 46.3 %collective-permute-done.9 = bf16[512,2048]{1,0:T(8,128)(2,1)S(1)} collective-permute-done((bf16[512,2048]{1,0:T(8,128)(2,1)S(1)}, bf16[512,2048]{1,0:T(8,128)(2,1)S(1)}, u32[]{:S(2)}, u32[]{:S(2)}) %collective-permute-start.9) | collective-permute-done | bytes 2097184 | tf_op jit(solution)/shard_map/ppermute | solution.py:112
  385.1 44.1 %collective-permute-done.14 = bf16[512,2048]{1,0:T(8,128)(2,1)S(1)} collective-permute-done((bf16[512,2048]{1,0:T(8,128)(2,1)}, bf16[512,2048]{1,0:T(8,128)(2,1)S(1)}, u32[]{:S(2)}, u32[]{:S(2)}) %collective-permute-start.14) | collective-permute-done | bytes 2097184 | tf_op jit(solution)/shard_map/ppermute | solution.py:112
  453.0 23.6 %collective-permute-done.11 = bf16[2048,1024]{0,1:T(8,128)(2,1)} collective-permute-done((bf16[2048,1024]{0,1:T(8,128)(2,1)}, bf16[2048,1024]{0,1:T(8,128)(2,1)}, u32[]{:S(2)}, u32[]{:S(2)}) %collective-permute-start.11) | collective-permute-done | bytes 4194336 | tf_op jit(solution)/shard_map/ppermute | solution.py:112
  488.0 78.1 %collective-permute-done.12 = bf16[1024,2048]{1,0:T(8,128)(2,1)S(1)} collective-permute-done((bf16[1024,2048]{1,0:T(8,128)(2,1)}, bf16[1024,2048]{1,0:T(8,128)(2,1)S(1)}, u32[]{:S(2)}, u32[]{:S(2)}) %collective-permute-start.12) | collective-permute-done | bytes 4194336 | tf_op jit(solution)/shard_map/ppermute | solution.py:112
  601.1 38.9 %collective-permute-done.17 = bf16[512,2048]{1,0:T(8,128)(2,1)S(1)} collective-permute-done((bf16[512,2048]{1,0:T(8,128)(2,1)S(1)}, bf16[512,2048]{1,0:T(8,128)(2,1)S(1)}, u32[]{:S(2)}, u32[]{:S(2)}) %collective-permute-start.17) | collective-permute-done | bytes 2097184 | tf_op jit(solution)/shard_map/ppermute | solution.py:112
  651.1 45.3 %collective-permute-done.24 = bf16[512,2048]{1,0:T(8,128)(2,1)S(1)} collective-permute-done((bf16[512,2048]{1,0:T(8,128)(2,1)S(1)}, bf16[512,2048]{1,0:T(8,128)(2,1)S(1)}, u32[]{:S(2)}, u32[]{:S(2)}) %collective-permute-start.24) | collective-permute-done | bytes 2097184 | tf_op jit(solution)/shard_map/ppermute | solution.py:112
  781.3 46.1 %collective-permute-done.27 = bf16[512,2048]{1,0:T(8,128)(2,1)S(1)} collective-permute-done((bf16[512,2048]{1,0:T(8,128)(2,1)S(1)}, bf16[512,2048]{1,0:T(8,128)(2,1)S(1)}, u32[]{:S(2)}, u32[]{:S(2)}) %collective-permute-start.27) | collective-permute-done | bytes 2097184 | tf_op jit(solution)/shard_map/ppermute | solution.py:112
  841.9 45.3 %collective-permute-done.30 = bf16[512,2048]{1,0:T(8,128)(2,1)S(1)} collective-permute-done((bf16[512,2048]{1,0:T(8,128)(2,1)S(1)}, bf16[512,2048]{1,0:T(8,128)(2,1)S(1)}, u32[]{:S(2)}, u32[]{:S(2)}) %collective-permute-start.30) | collective-permute-done | bytes 2097184 | tf_op jit(solution)/shard_map/ppermute | solution.py:112
  925.0 91.3 %collective-permute-done.37 = bf16[512,1024]{1,0:T(8,128)(2,1)S(1)} collective-permute-done((bf16[512,1024]{1,0:T(8,128)(2,1)S(1)}, bf16[512,1024]{1,0:T(8,128)(2,1)S(1)}, u32[]{:S(2)}, u32[]{:S(2)}) %collective-permute-start.37) | collective-permute-done | bytes 1048608 | tf_op jit(solution)/shard_map/ppermute | solution.py:112
  1085.2 71.6 %collective-permute-done.39 = bf16[1024,2048]{1,0:T(8,128)(2,1)} collective-permute-done((bf16[1024,2048]{1,0:T(8,128)(2,1)S(1)}, bf16[1024,2048]{1,0:T(8,128)(2,1)}, u32[]{:S(2)}, u32[]{:S(2)}) %collective-permute-start.39) | collective-permute-done | bytes 4194336 | tf_op jit(solution)/shard_map/ppermute | solution.py:112
  1287.0 50.7 %collective-permute-done.36 = bf16[2048,768]{1,0:T(8,128)(2,1)} collective-permute-done((bf16[2048,768]{1,0:T(8,128)(2,1)S(1)}, bf16[2048,768]{1,0:T(8,128)(2,1)}, u32[]{:S(2)}, u32[]{:S(2)}) %collective-permute-start.36) | collective-permute-done | bytes 3145760 | tf_op jit(solution)/shard_map/ppermute | solution.py:112
  1349.9 55.0 %reduce-scatter.5.cloned.1.call-done = bf16[512,768]{1,0:T(8,128)(2,1)} async-done(((bf16[2048,768]{1,0:T(8,128)(2,1)}), bf16[512,768]{1,0:T(8,128)(2,1)}) %reduce-scatter.5.cloned.1.call-update) | async-done | bytes 786448 | tf_op jit(solution)/shard_map/reduce_scatter | solution.py:327
  1437.3 41.3 %collective-permute-done.33 = bf16[512,2048]{1,0:T(8,128)(2,1)S(1)} collective-permute-done((bf16[512,2048]{1,0:T(8,128)(2,1)S(1)}, bf16[512,2048]{1,0:T(8,128)(2,1)S(1)}, u32[]{:S(2)}, u32[]{:S(2)}) %collective-permute-start.33) | collective-permute-done | bytes 2097184 | tf_op jit(solution)/shard_map/ppermute | solution.py:112
  1489.2 62.4 %all-reduce.3.cloned.1.call-done = f32[4,6144]{1,0:T(4,128)} async-done(((f32[4,6144]{1,0:T(4,128)}), f32[4,6144]{1,0:T(4,128)}) %all-reduce.3.cloned.1.call-update) | async-done | bytes 98320 | tf_op jit(solution)/shard_map/psum | solution.py:428
  1556.9 24.5 %all-gather.26.cloned.1.call-done = bf16[1024,1024]{1,0:T(8,128)(2,1)} async-done(((bf16[128,1024]{1,0:T(8,128)(2,1)}), bf16[1024,1024]{1,0:T(8,128)(2,1)}) %all-gather.26.cloned.1.call-update) | async-done | bytes 2097168 | tf_op jit(solution)/shard_map/all_gather | solution.py:330
  1590.6 47.2 %all-gather.28.cloned.1.call-done = bf16[4096,1024]{1,0:T(8,128)(2,1)} async-done(((bf16[512,1024]{1,0:T(8,128)(2,1)}), bf16[4096,1024]{1,0:T(8,128)(2,1)}) %all-gather.28.cloned.1.call-update) | async-done | bytes 8388624 | tf_op jit(solution)/shard_map/all_gather | solution.py:330
  1637.8 17.1 reshape.588
  1654.9 15.2 copy.194
  1670.1 18.0 copy.240
  1706.0 35.7 %all-gather.24.cloned.1.call-done = bf16[4096,768]{1,0:T(8,128)(2,1)} async-done(((bf16[512,768]{1,0:T(8,128)(2,1)}), bf16[4096,768]{1,0:T(8,128)(2,1)}) %all-gather.24.cloned.1.call-update) | async-done | bytes 6291472 | tf_op jit(solution)/shard_map/all_gather | solution.py:330
  (710 shorter events, 718.1 us)
Async XLA Ops:
  7.2 167.6 %all-gather.20.cloned.1.call-start = ((), (), s32[]{:S(2)}) async-start(), calls=%async_computation.11 | async-start | bytes 1310720 | tf_op jit(solution)/shard_map/all_gather | solution.py:195
  12.0 190.8 %all-gather.16.cloned.1.call-start = ((), (), s32[]{:S(2)}) async-start(), calls=%async_computation.4 | async-start | bytes 3932160 | tf_op jit(solution)/shard_map/all_gather | solution.py:195
  25.7 357.2 %all-gather.18.cloned.1.call-start = ((), (), s32[]{:S(2)}) async-start(), calls=%async_computation.5 | async-start | bytes 5242880 | tf_op jit(solution)/shard_map/all_gather | solution.py:195
  40.1 344.3 %all-gather.22.cloned.1.call-start = ((), (), s32[]{:S(2)}) async-start(), calls=%async_computation.12 | async-start | bytes 5242880 | tf_op jit(solution)/shard_map/all_gather | solution.py:195
  42.4 99.3 %collective-permute-start.1 = (bf16[256,2048]{1,0:T(8,128)(2,1)S(1)}, bf16[256,2048]{1,0:T(8,128)(2,1)S(1)}, u32[]{:S(2)}, u32[]{:S(2)}) collective-permute-start(bf16[256,2048]{1,0:T(8,128)(2,1)S(1)} %get-tuple-element.69), channel_id=1, source_target_pairs={{0,1},{1,0},{2,5},{3,4},{4,3},{5,2},{6,7},{7,6},{8,9},{9,8},{10,13... | collective-permute-start | bytes 3145736 | tf_op jit(solution)/shard_map/ppermute | solution.py:136
  146.1 1201.8 %reduce-scatter.7.cloned.1.call-start = ((), (), s32[]{:S(2)}) async-start(), calls=%async_computation.7 | async-start | bytes 1310720 | tf_op jit(solution)/shard_map/reduce_scatter | solution.py:327
  202.7 70.7 %collective-permute-start.3 = (bf16[2048,768]{0,1:T(8,128)(2,1)}, bf16[2048,768]{0,1:T(8,128)(2,1)S(1)}, u32[]{:S(2)}, u32[]{:S(2)}) collective-permute-start(bf16[2048,768]{0,1:T(8,128)(2,1)} %all-gather.16.cloned.1.call-done), channel_id=1, source_target_pairs={{0,16},{4,20},{8,24},{12,28},{16,0},{20,4},{24,8},{28,12},{1,17},{... | collective-permute-start | bytes 9437192 | tf_op jit(solution)/shard_map/ppermute | solution.py:112
  382.9 93.7 %collective-permute-start.11 = (bf16[2048,1024]{0,1:T(8,128)(2,1)}, bf16[2048,1024]{0,1:T(8,128)(2,1)}, u32[]{:S(2)}, u32[]{:S(2)}) collective-permute-start(bf16[2048,1024]{0,1:T(8,128)(2,1)} %all-gather.18.cloned.1.call-done), channel_id=1, source_target_pairs={{0,16},{4,20},{8,24},{12,28},{16,0},{20,4},{24,8},{28,12},{1,17},{... | collective-permute-start | bytes 12582920 | tf_op jit(solution)/shard_map/ppermute | solution.py:112
  384.5 181.5 %collective-permute-start.12 = (bf16[1024,2048]{1,0:T(8,128)(2,1)}, bf16[1024,2048]{1,0:T(8,128)(2,1)S(1)}, u32[]{:S(2)}, u32[]{:S(2)}) collective-permute-start(bf16[1024,2048]{1,0:T(8,128)(2,1)} %bitcast.453), channel_id=1, source_target_pairs={{0,16},{4,20},{8,24},{12,28},{16,0},{20,4},{24,8},{28,12},{1,17},{... | collective-permute-start | bytes 12582920 | tf_op jit(solution)/shard_map/ppermute | solution.py:112
  841.9 60.4 %collective-permute-start.28 = (bf16[512,2048]{1,0:T(8,128)(2,1)S(1)}, bf16[512,2048]{1,0:T(8,128)(2,1)S(1)}, u32[]{:S(2)}, u32[]{:S(2)}) collective-permute-start(bf16[512,2048]{1,0:T(8,128)(2,1)S(1)} %get-tuple-element.36), channel_id=1, source_target_pairs={{0,4},{4,0},{8,12},{12,8},{16,20},{20,16},{24,28},{28,24},{1,5},{5... | collective-permute-start | bytes 6291464 | tf_op jit(solution)/shard_map/ppermute | solution.py:112
  900.6 133.7 %collective-permute-start.38 = (bf16[2048,1024]{1,0:T(8,128)(2,1)}, bf16[2048,1024]{1,0:T(8,128)(2,1)}, u32[]{:S(2)}, u32[]{:S(2)}) collective-permute-start(bf16[2048,1024]{1,0:T(8,128)(2,1)} %add_convert_fusion.3), channel_id=1, source_target_pairs={{0,16},{4,20},{8,24},{12,28},{16,0},{20,4},{24,8},{28,12},{1,17},{... | collective-permute-start | bytes 12582920 | tf_op jit(solution)/shard_map/ppermute | solution.py:112
  922.3 94.0 %collective-permute-start.37 = (bf16[512,1024]{1,0:T(8,128)(2,1)S(1)}, bf16[512,1024]{1,0:T(8,128)(2,1)S(1)}, u32[]{:S(2)}, u32[]{:S(2)}) collective-permute-start(bf16[512,1024]{1,0:T(8,128)(2,1)S(1)} %bitcast.391), channel_id=1, source_target_pairs={{0,16},{4,20},{8,24},{12,28},{16,0},{20,4},{24,8},{28,12},{1,17},{... | collective-permute-start | bytes 3145736 | tf_op jit(solution)/shard_map/ppermute | solution.py:112
  1017.9 330.5 %reduce-scatter.9.cloned.1.call-start = ((), (), s32[]{:S(2)}) async-start(), calls=%async_computation.9 | async-start | bytes 5242880 | tf_op jit(solution)/shard_map/reduce_scatter | solution.py:327
  1045.9 303.3 %reduce-scatter.11.cloned.1.call-start = ((), (), s32[]{:S(2)}) async-start(), calls=%async_computation.10 | async-start | bytes 5242880 | tf_op jit(solution)/shard_map/reduce_scatter | solution.py:327
  1064.4 92.4 %collective-permute-start.39 = (bf16[1024,2048]{1,0:T(8,128)(2,1)S(1)}, bf16[1024,2048]{1,0:T(8,128)(2,1)}, u32[]{:S(2)}, u32[]{:S(2)}) collective-permute-start(bf16[1024,2048]{1,0:T(8,128)(2,1)S(1)} %add_convert_fusion.1), channel_id=1, source_target_pairs={{0,16},{4,20},{8,24},{12,28},{16,0},{20,4},{24,8},{28,12},{1,17},{... | collective-permute-start | bytes 12582920 | tf_op jit(solution)/shard_map/ppermute | solution.py:112
  1168.3 236.6 %reduce-scatter.5.cloned.1.call-start = ((), (), s32[]{:S(2)}) async-start(), calls=%async_computation.6 | async-start | bytes 3932160 | tf_op jit(solution)/shard_map/reduce_scatter | solution.py:327
  1268.7 69.0 %collective-permute-start.36 = (bf16[2048,768]{1,0:T(8,128)(2,1)S(1)}, bf16[2048,768]{1,0:T(8,128)(2,1)}, u32[]{:S(2)}, u32[]{:S(2)}) collective-permute-start(bf16[2048,768]{1,0:T(8,128)(2,1)S(1)} %add_convert_fusion.5), channel_id=1, source_target_pairs={{0,16},{4,20},{8,24},{12,28},{16,0},{20,4},{24,8},{28,12},{1,17},{... | collective-permute-start | bytes 9437192 | tf_op jit(solution)/shard_map/ppermute | solution.py:112
  1342.4 209.2 %all-reduce.3.cloned.1.call-start = ((), (), s32[]{:S(2)}) async-start(), calls=%async_computation.8 | async-start | bytes 196608 | tf_op jit(solution)/shard_map/psum | solution.py:428
  1347.8 233.5 %all-gather.26.cloned.1.call-start = ((), (), s32[]{:S(2)}) async-start(), calls=%async_computation.14 | async-start | bytes 2359296 | tf_op jit(solution)/shard_map/all_gather | solution.py:330
  1348.4 289.4 %all-gather.28.cloned.1.call-start = ((), (), s32[]{:S(2)}) async-start(), calls=%async_computation.15 | async-start | bytes 9437184 | tf_op jit(solution)/shard_map/all_gather | solution.py:330
  1349.1 345.0 %all-gather.30.cloned.1.call-start = ((), (), s32[]{:S(2)}) async-start(), calls=%async_computation.16 | async-start | bytes 9437184 | tf_op jit(solution)/shard_map/all_gather | solution.py:330
  1349.7 392.0 %all-gather.24.cloned.1.call-start = ((), (), s32[]{:S(2)}) async-start(), calls=%async_computation.13 | async-start | bytes 7077888 | tf_op jit(solution)/shard_map/all_gather | solution.py:330
  1481.5 73.0 %collective-permute-start.35 = (bf16[256,2048]{1,0:T(8,128)(2,1)}, bf16[256,2048]{1,0:T(8,128)(2,1)S(1)}, u32[]{:S(2)}, u32[]{:S(2)}) collective-permute-start(bf16[256,2048]{1,0:T(8,128)(2,1)} %get-tuple-element.60), channel_id=1, source_target_pairs={{1,0},{0,1},{5,2},{4,3},{3,4},{2,5},{7,6},{6,7},{9,8},{8,9},{13,10... | collective-permute-start | bytes 3145736 | tf_op jit(solution)/shard_map/ppermute | solution.py:141
  1481.5 73.0 %collective-permute-start.34 = (bf16[256,2048]{1,0:T(8,128)(2,1)}, bf16[256,2048]{1,0:T(8,128)(2,1)S(1)}, u32[]{:S(2)}, u32[]{:S(2)}) collective-permute-start(bf16[256,2048]{1,0:T(8,128)(2,1)} %get-tuple-element.59), channel_id=1, source_target_pairs={{0,0},{1,1},{4,2},{5,3},{2,4},{3,5},{6,6},{7,7},{8,8},{9,9},{12,10... | collective-permute-start | bytes 3145736 | tf_op jit(solution)/shard_map/ppermute | solution.py:140
  (209 other events, 5219.8 us)
Sparse Core Ops, SparseCore 0:
  12.1 28.4 all-gather.19
  42.7 91.3 all-gather.15
  136.3 82.4 all-gather.17
  220.2 79.2 all-gather.21
  1018.0 27.9 reduce-scatter.6
  1048.3 77.3 reduce-scatter.8
  1168.5 79.3 reduce-scatter.10
  1342.5 62.4 reduce-scatter.4
  1411.5 140.0 all-reduce.2
  1553.4 27.8 all-gather.25
  1583.4 54.3 all-gather.27
  1639.7 54.3 all-gather.29
  1696.2 45.5 all-gather.23

commit v2 on v1

v2 whole, which is shorter than its diff:
```python
import jax
import jax.numpy as jnp
from jax import lax
from jax.experimental import pallas as pl
from jax.experimental.pallas import tpu as pltpu
from jax.sharding import PartitionSpec as P

HEADS = 16
TEAM = 4
LANES = 128
EPSILON = 1e-06
BF = jnp.bfloat16
F32 = jnp.float32
VMEM_LIMIT = 48 * 1024 * 1024
FREE = pl.CostEstimate(flops=0, bytes_accessed=0, transcendentals=0)

(
    QKV_Z,
    OUT_Z,
    UP_Z,
    DOWN_Z,
    FAR,
    QKV,
    OTHER,
    MINE,
    BOTH,
    CONTEXT,
    KEPT,
    AWAY,
    OUT_SWAPPED,
    SEND,
    BACK,
    UP,
    THEIRS,
    ATTENDED,
    HIDDEN,
    VALUE,
    SLOPE,
    DOWN,
    PARTIAL,
    COTANGENT,
    COT,
    NORMAL2,
    DDOWN,
    RESULT,
    LAYER,
    DBEFORE,
    SHARE,
    RECEIVED,
    PART,
    DATTN,
    DATTN_NEAR,
    DATTN_FAR,
    DATTN_MINE,
    DQKV,
    OUT,
    WHOLE,
    VECTOR,
    DATTN_OTHER,
    OWN,
    GRAD,
) = range(44)


def mm(left, right):
    return jnp.dot(left, right, preferred_element_type=F32)


def mm_t(left, right):
    return lax.dot_general(left, right, (((1,), (1,)), ((), ())), preferred_element_type=F32)


def t_mm(left, right):
    return lax.dot_general(left, right, (((0,), (0,)), ((), ())), preferred_element_type=F32)


def pick(array, index, axis=0):
    return lax.dynamic_index_in_dim(array, index, axis, keepdims=False)


def tie(*arrays):
    return lax.optimization_barrier(arrays)


def normalise(summed):
    center = summed - jnp.mean(summed, axis=-1, keepdims=True)
    spread = jnp.mean(center * center, axis=-1, keepdims=True)
    scale = lax.rsqrt(spread + EPSILON)
    return center * scale, scale


def norm_backward(grad, gain, normal, scale):
    dn = grad * gain
    first = jnp.mean(dn, axis=-1, keepdims=True)
    second = jnp.mean(dn * normal, axis=-1, keepdims=True)
    return scale * (dn - first - normal * second)


def gelu_parts(u):
    inner = 0.7978845608 * (u + 0.044715 * u * u * u)
    t = jnp.tanh(inner)
    half = 0.5 * (1.0 + t)
    slope = half + 0.5 * u * (1.0 - t * t) * (0.7978845608 + 0.7978845608 * 0.134145 * u * u)
    return u * half, slope


def dot(kind, pairs, finish, outs, columns=(), tiles=(), left=(0, 1), right=(0, 1), strip=256):
    count = len(pairs)
    xs, ws = [x for x, _ in pairs], [w for _, w in pairs]
    flip = kind == "tn"
    m = xs[0].shape[1] // left[1] if flip else xs[0].shape[0]
    n = ws[0].shape[0] if kind == "nt" else ws[0].shape[1] // right[1]
    depths = [x.shape[0] if flip else x.shape[1] for x in xs]
    by_rows = flip and m > n
    size = m if by_rows else n
    step = next((s for s in (512, 384, 256) if size % s == 0), size)
    m_block, n_block = (step, n) if by_rows else (m, step)
    strip = strip if m_block % strip == 0 else m_block
    inputs = 2 * count + len(columns) + len(tiles)

    def kernel(*refs):
        x_refs, w_refs = refs[:count], refs[count : 2 * count]
        column_refs = refs[2 * count : 2 * count + len(columns)]
        tile_refs = refs[2 * count + len(columns) : inputs]
        out_refs = refs[inputs : inputs + len(outs)]
        if flip:
            flipped = refs[inputs + len(outs) :]

            def turn():
                for a, b in zip(flipped, x_refs, strict=True):
                    a[...] = b[...].T

            if by_rows:
                turn()
            else:
                pl.when(pl.program_id(0) == 0)(turn)
            x_refs = flipped
        for at in range(0, m_block, strip):
            some = slice(at, at + strip)
            total = 0.0
            for x, w in zip(x_refs, w_refs, strict=True):
                product = mm_t(x[some, :], w[...]) if kind == "nt" else mm(x[some, :], w[...])
                total = total + product
            extra = [c[...] for c in column_refs] + [t[some, :] for t in tile_refs]
            for ref, value in zip(out_refs, finish(total, *extra), strict=True):
                ref[some, :] = value.astype(ref.dtype)

    if by_rows:
        per = left[0] * (m // step)
        x_specs = [pl.BlockSpec((k, step), lambda j: (0, per + j)) for k in depths]
        w_specs = [pl.BlockSpec((k, n), lambda j: (0, right[0])) for k in depths]
        out_spec = pl.BlockSpec((step, n), lambda j: (j, 0))
    else:
        per = right[0] * (n // step)
        if flip:
            x_specs = [pl.BlockSpec((k, m), lambda j: (0, left[0])) for k in depths]
        else:
            x_specs = [pl.BlockSpec((m, k), lambda j: (0, 0)) for k in depths]
        if kind == "nt":
            w_specs = [pl.BlockSpec((step, k), lambda j: (j, 0)) for k in depths]
        else:
            w_specs = [pl.BlockSpec((k, step), lambda j: (0, per + j)) for k in depths]
        out_spec = pl.BlockSpec((m, step), lambda j: (0, j))
    results = pl.pallas_call(
        kernel,
        grid=(size // step,),
        in_specs=x_specs
        + w_specs
        + [pl.BlockSpec((1, step), lambda j: (0, j))] * len(columns)
        + [out_spec] * len(tiles),
        out_specs=[out_spec] * len(outs),
        out_shape=[jax.ShapeDtypeStruct((m, n), t) for t in outs],
        scratch_shapes=[pltpu.VMEM((m_block, k), BF) for k in depths] if flip else [],
        compiler_params=pltpu.CompilerParams(vmem_limit_bytes=VMEM_LIMIT),
        cost_estimate=FREE,
    )(*xs, *ws, *columns, *tiles)
    return results if len(outs) > 1 else results[0]


def plain(total):
    return (total,)


def attend(qkv, mask, heads):
    rows = qkv.shape[0]
    head_dim = qkv.shape[1] // (3 * heads)
    scaling = head_dim ** (-0.5)
    step = min(256, rows)

    def kernel(qkv_ref, mask_ref, context_ref, total_ref):
        keys = qkv_ref[:, head_dim : 2 * head_dim]
        values = qkv_ref[:, 2 * head_dim :]
        keep = mask_ref[...] > 0
        for at in range(0, rows, step):
            query = qkv_ref[at : at + step, :head_dim]
            scores = jnp.where(keep, mm_t(query, keys) * scaling, -1e30)
            most = jnp.max(scores, axis=1, keepdims=True)
            shares = jnp.exp(scores - most)
            total = jnp.sum(shares, axis=1, keepdims=True)
            probs = (shares * (1.0 / total)).astype(BF)
            context_ref[at : at + step, :] = mm(probs, values).astype(BF)
            log_total = jnp.broadcast_to(most + jnp.log(total), (step, 128))
            total_ref[0, :, at : at + step] = jnp.transpose(log_total)[0:1, :]

    return pl.pallas_call(
        kernel,
        grid=(heads,),
        in_specs=[
            pl.BlockSpec((rows, 3 * head_dim), lambda h: (0, h)),
            pl.BlockSpec((1, rows), lambda h: (0, 0)),
        ],
        out_specs=[
            pl.BlockSpec((rows, head_dim), lambda h: (0, h)),
            pl.BlockSpec((1, 1, rows), lambda h: (h, 0, 0)),
        ],
        out_shape=[
            jax.ShapeDtypeStruct((rows, heads * head_dim), BF),
            jax.ShapeDtypeStruct((heads, 1, rows), F32),
        ],
        compiler_params=pltpu.CompilerParams(vmem_limit_bytes=VMEM_LIMIT),
        cost_estimate=FREE,
    )(qkv, mask)


def attend_backward(qkv, dcontext, log_total, mask, heads, part):
    rows = qkv.shape[0]
    head_dim = qkv.shape[1] // (3 * heads)
    scaling = head_dim ** (-0.5)
    step = min(256, rows)

    def kernel(qkv_ref, dcontext_ref, total_ref, mask_ref, dqkv_ref, sums_ref):
        keys = qkv_ref[:, head_dim : 2 * head_dim]
        values = qkv_ref[:, 2 * head_dim :]
        keep = mask_ref[...] > 0
        dkeys, dvalues, query_sum = 0.0, 0.0, 0.0
        for at in range(0, rows, step):
            query = qkv_ref[at : at + step, :head_dim]
            dctx = dcontext_ref[at : at + step, :]
            scores = mm_t(keys, query) * scaling
            probs = jnp.exp(scores - total_ref[0, :, at : at + step])
            probs = jnp.where(keep, probs, 0.0)
            dprobs = mm_t(values, dctx)
            delta = jnp.sum(dprobs * probs, axis=0, keepdims=True)
            dscores = (probs * (dprobs - delta)).astype(BF)
            dvalues = dvalues + mm(probs.astype(BF), dctx)
            dkeys = dkeys + mm(dscores, query)
            dquery = (t_mm(dscores, keys) * scaling).astype(BF)
            dqkv_ref[at : at + step, :head_dim] = dquery
            query_sum = query_sum + jnp.sum(dquery.astype(F32), axis=0, keepdims=True)
        dvalues = dvalues.astype(BF)
        dqkv_ref[:, head_dim : 2 * head_dim] = (dkeys * scaling).astype(BF)
        dqkv_ref[:, 2 * head_dim :] = dvalues
        value_sum = jnp.sum(dvalues.astype(F32), axis=0, keepdims=True)
        sums_ref[...] = jnp.concatenate([query_sum, query_sum, value_sum], axis=1)

    return pl.pallas_call(
        kernel,
        grid=(heads,),
        in_specs=[
            pl.BlockSpec((rows, 3 * head_dim), lambda h: (0, h)),
            pl.BlockSpec((rows, head_dim), lambda h: (0, part * heads + h)),
            pl.BlockSpec((1, 1, rows), lambda h: (h, 0, 0)),
            pl.BlockSpec((rows, 1), lambda h: (0, 0)),
        ],
        out_specs=[
            pl.BlockSpec((rows, 3 * head_dim), lambda h: (0, h)),
            pl.BlockSpec((1, 3 * head_dim), lambda h: (0, h)),
        ],
        out_shape=[
            jax.ShapeDtypeStruct(qkv.shape, BF),
            jax.ShapeDtypeStruct((1, qkv.shape[1]), F32),
        ],
        compiler_params=pltpu.CompilerParams(vmem_limit_bytes=VMEM_LIMIT),
        cost_estimate=FREE,
    )(qkv, dcontext, log_total, mask)


def place_rows(pieces, places, shape):
    count, (rows, width) = len(pieces), pieces[0].shape

    def kernel(places_ref, *refs):
        for i in range(count):

            @pl.when(pl.program_id(0) == i)
            def _(i=i):
                refs[-1][...] = refs[i][...].astype(F32)

    return pl.pallas_call(
        kernel,
        grid_spec=pltpu.PrefetchScalarGridSpec(
            num_scalar_prefetch=1,
            grid=(count,),
            in_specs=[pl.BlockSpec((rows, width), lambda i, s: (0, 0))] * count,
            out_specs=pl.BlockSpec((rows, width), lambda i, s: (s[i], 0)),
        ),
        out_shape=jax.ShapeDtypeStruct(shape, F32),
        compiler_params=pltpu.CompilerParams(vmem_limit_bytes=VMEM_LIMIT),
        cost_estimate=FREE,
    )(jnp.stack(places).astype(jnp.int32), *pieces)


def place_columns(pieces, places, shape, block, column):
    count, (rows, width) = len(pieces), pieces[0].shape
    step = min(64, rows)

    def kernel(places_ref, *refs):
        for p in range(count):
            for i in range(width // block):
                at = pl.multiple_of(column(i, places_ref[p]) * block, block)
                value = refs[p][:, i * block : (i + 1) * block].astype(F32)
                refs[-1][:, pl.ds(at, block)] = value

    return pl.pallas_call(
        kernel,
        grid_spec=pltpu.PrefetchScalarGridSpec(
            num_scalar_prefetch=1,
            grid=(rows // step,),
            in_specs=[pl.BlockSpec((step, width), lambda i, s: (i, 0))] * count,
            out_specs=pl.BlockSpec((step, shape[1]), lambda i, s: (i, 0)),
        ),
        out_shape=jax.ShapeDtypeStruct(shape, F32),
        compiler_params=pltpu.CompilerParams(vmem_limit_bytes=VMEM_LIMIT),
        cost_estimate=FREE,
    )(jnp.stack(places).astype(jnp.int32), *pieces)


def take_columns(arrays, index, count, block):
    if block % LANES != 0:
        pieces = []
        for i in range(count):
            for w in arrays:
                pieces.append(lax.dynamic_slice_in_dim(w, index[i] * block, block, 1))
        return jnp.concatenate(pieces, axis=1)
    rows, n = arrays[0].shape[0], len(arrays)

    def kernel(index_ref, *refs):
        for i in range(n):
            refs[-1][:, i * block : (i + 1) * block] = refs[i][...]

    return pl.pallas_call(
        kernel,
        grid_spec=pltpu.PrefetchScalarGridSpec(
            num_scalar_prefetch=1,
            grid=(count,),
            in_specs=[pl.BlockSpec((rows, block), lambda i, s: (0, s[i]))] * n,
            out_specs=pl.BlockSpec((rows, n * block), lambda i, s: (0, i)),
        ),
        out_shape=jax.ShapeDtypeStruct((rows, count * n * block), BF),
        compiler_params=pltpu.CompilerParams(vmem_limit_bytes=VMEM_LIMIT),
        cost_estimate=FREE,
    )(jnp.stack(index).astype(jnp.int32), *arrays)


def place_heads_grad(gathered, reps, run, head_dim):
    shard = gathered.shape[1]
    step = min(64, shard)

    def kernel(in_ref, *outs):
        for r in range(reps):
            for j in range(run):
                at = (((r // TEAM) * run + j) * TEAM + r % TEAM) * head_dim
                for i in range(3):
                    start = (3 * j + i) * head_dim
                    value = in_ref[r, :, start : start + head_dim].astype(F32)
                    outs[i][:, at : at + head_dim] = value

    return pl.pallas_call(
        kernel,
        grid=(shard // step,),
        in_specs=[pl.BlockSpec((reps, step, run * 3 * head_dim), lambda i: (0, i, 0))],
        out_specs=[pl.BlockSpec((step, HEADS * head_dim), lambda i: (i, 0))] * 3,
        out_shape=[jax.ShapeDtypeStruct((shard, HEADS * head_dim), F32)] * 3,
        compiler_params=pltpu.CompilerParams(vmem_limit_bytes=VMEM_LIMIT),
        cost_estimate=FREE,
    )(gathered)


def local(
    tokens,
    lengths,
    query_weight,
    key_weight,
    value_weight,
    out_weight,
    query_bias,
    value_bias,
    out_bias,
    first_gain,
    first_shift,
    up_weight,
    up_bias,
    down_weight,
    down_bias,
    second_gain,
    second_shift,
    cotangent,
):
    slots_here, block, width = tokens.shape
    reps, parts = lax.axis_size("rep"), lax.axis_size("fsdp")
    copies = reps // TEAM
    hidden = up_weight.shape[1]
    shard = query_weight.shape[0]
    head_dim = width // HEADS
    team_heads = HEADS // TEAM
    run = team_heads // copies
    rep, z = lax.axis_index("rep"), lax.axis_index("fsdp")
    q, d = rep % TEAM, rep // TEAM
    parity = z % 2
    held = TEAM * slots_here // parts
    rows = slots_here * block
    half = rows // 2
    unit = hidden // parts // reps
    wide = width // copies
    halves = 2 if unit % (2 * LANES) == 0 else 1
    half_unit = unit // halves
    per_shard = HEADS // parts

    def swap(x, mask):
        return lax.ppermute(x, "rep", [(i, i ^ mask) for i in range(reps)])

    def shift(x, by):
        return lax.ppermute(x, "fsdp", [(i, (i - by) % parts) for i in range(parts)])

    def from_next(k):
        return (z + k) % parts

    def routes(turn):
        pairs = []
        for copy in range(copies):
            for member in range(TEAM):
                for place in range(parts):
                    slot = member * slots_here + (place + turn) % 2
                    to_member = ((slot // parts) * parts + place) // 2
                    source = (copy * TEAM + member) * parts + place
                    target = (copy * TEAM + to_member) * parts + slot % parts
                    pairs.append((source, target))
        return pairs

    even, odd = routes(0), routes(1)
    axes = ("rep", "fsdp")
    v = {}

    def order(*names):
        names = list(dict.fromkeys(names))
        v.update(zip(names, tie(*[v[n] for n in names]), strict=True))

    def to_team(x):
        first = lax.ppermute(pick(x, parity), axes, even)
        second = lax.ppermute(pick(x, 1 - parity), axes, odd)
        return first, second

    def from_team(first, second):
        return settle(*leave_team(first, second))

    def leave_team(first, second):
        first = lax.ppermute(first, axes, [(b, a) for a, b in even])
        second = lax.ppermute(second, axes, [(b, a) for a, b in odd])
        return first, second

    def settle(first, second):
        straight = jnp.stack([first, second])
        turned = jnp.stack([second, first])
        return jnp.where(parity == 0, straight, turned)

    vectors = jnp.concatenate(
        [
            query_bias,
            value_bias,
            out_bias,
            first_gain,
            first_shift,
            down_bias,
            second_gain,
            second_shift,
            up_bias,
        ]
    )[None]
    pieces = [vectors] + [shift(vectors, k) for k in range(1, parts)]
    there = [lengths] + [swap(lengths, m) for m in range(1, TEAM)]
    first, second = to_team(tokens)
    first, second, *pieces = tie(first, second, *pieces, *there)
    pieces, there = pieces[:parts], pieces[parts:]
    vectors = jnp.zeros((parts, vectors.shape[1]), BF)
    for k, piece in enumerate(pieces):
        vectors = lax.dynamic_update_slice(vectors, piece, (from_next(k), 0))
    vectors = vectors.astype(F32)
    names = [vectors[:, i * shard : (i + 1) * shard].reshape(width) for i in range(8)]
    bias_query, bias_value, bias_out, gain_one, shift_one, bias_down, gain_two, shift_two = names
    bias_up = vectors[:, 8 * shard :].reshape(parts, reps, unit)
    slot_lengths = jnp.zeros((TEAM, slots_here), jnp.int32)
    for m in range(TEAM):
        slot_lengths = lax.dynamic_update_slice(slot_lengths, there[m][None], (q ^ m, 0))
    slot_lengths = slot_lengths.reshape(-1)

    def live(member):
        place = [
            ((member * 2 + o) % parts) * block + jnp.arange(block) for o in (parity, 1 - parity)
        ]
        length = pick(slot_lengths, ((member * 2) // parts) * parts + z)
        return jnp.concatenate(place) < length

    masks = [live(q ^ m).astype(F32) for m in range(TEAM)]
    valid = masks[0][:, None]
    mask_mine, mask_other = jnp.concatenate(masks[:2]), jnp.concatenate(masks[2:])

    def head_columns(w, e):
        lead = w.shape[:-1]
        at = len(lead)
        split = w.reshape(lead + (copies, run, TEAM, head_dim))
        return pick(pick(split, e, at), q, at + 1)

    def over_z(x):
        return lax.all_gather(x, "fsdp", axis=0, tiled=True)

    def spread(x):
        return [x] + [swap(x, TEAM * m) for m in range(1, copies)]

    heads_here = [(d * run + j) * TEAM + q for j in range(run)]
    qkv_own = [
        take_columns([query_weight, key_weight, value_weight], [h], 1, head_dim)
        for h in heads_here
    ]
    split_out = out_weight.reshape(-1, head_dim, copies, wide)
    split_out = pick(split_out, d, 2)
    if per_shard >= TEAM:
        split_out = split_out.reshape(per_shard // TEAM, TEAM, head_dim, wide)
        out_own = pick(split_out, q, 1)
    else:
        out_own = pick(split_out, q % per_shard, 0)[None]
    up_own = [
        take_columns(
            [up_weight],
            [(t * reps + rep) * halves + h for t in range(parts)],
            parts,
            half_unit,
        )
        for h in range(halves)
    ]
    down_split = pick(down_weight.reshape(reps, halves, half_unit, width), rep)
    down_own = [down_split[h] for h in range(halves)]
    first, second, out_own, *own = tie(first, second, out_own, *qkv_own, *up_own, *down_own)
    qkv_own, up_own, down_own = own[:run], own[run : run + halves], own[run + halves :]
    for j in range(run):
        v[QKV_Z, j] = over_z(qkv_own[j])
    v[OUT_Z] = over_z(out_own)
    for h in range(halves):
        v[UP_Z, h] = over_z(up_own[h])
    for h in range(halves):
        v[DOWN_Z, h] = over_z(down_own[h])
    own_tokens = jnp.concatenate([first, second], axis=0)
    v[FAR, 0], v[FAR, 1] = swap(first, 2), swap(second, 2)
    near = [swap(x, 1) for x in (first, second)]
    order((FAR, 0), (FAR, 1), (QKV_Z, 0))
    for m in range(1, copies):
        v[QKV, 0, m] = swap(v[QKV_Z, 0], TEAM * m)
    far = [v[FAR, 0], v[FAR, 1]]
    far_near = [swap(x, 1) for x in far]

    def own_units(table, m):
        return pick(table, rep ^ (TEAM * m), 1).transpose(1, 0, 2).reshape(1, -1)

    bias_up = bias_up.reshape(parts, reps, halves, half_unit)
    up_biases = [own_units(bias_up, m) for m in range(copies)]
    qkv_bias = []
    for m in range(copies):
        qb, vb = head_columns(bias_query, d ^ m), head_columns(bias_value, d ^ m)
        qkv_bias.append(jnp.stack([qb, jnp.zeros_like(qb), vb], axis=1).reshape(1, -1))
    span = run * head_dim

    tokens_mine = jnp.concatenate([first, second] + near, axis=0)
    tokens_other = jnp.concatenate(far + far_near, axis=0)
    v[OTHER] = tokens_other
    order(OTHER, *[(QKV_Z, j) for j in range(run)])
    tokens_other = v[OTHER]
    for j in range(1, run):
        for m in range(1, copies):
            v[QKV, j, m] = swap(v[QKV_Z, j], TEAM * m)
    qkv_weight = {0: jnp.concatenate([v[QKV_Z, j] for j in range(run)], axis=1)}

    if held == 2:
        slots = (OTHER, MINE)
        v[MINE] = tokens_mine
        slot_masks = {OTHER: mask_other, MINE: mask_mine}
    else:
        slots = (BOTH,)
        v[BOTH] = jnp.concatenate([tokens_mine, tokens_other], axis=0)
        slot_masks = {BOTH: jnp.concatenate([mask_mine, mask_other])}
    log_totals = {}

    def project_step(name, m):
        v[QKV, name, m] = dot(
            "nn", [(v[name], qkv_weight[m])], lambda t, b: (t + b,), [BF], columns=[qkv_bias[m]]
        )

    def attend_only(name, m):
        qkv = v[QKV, name, m]
        context, log_totals[name, m] = attend(qkv, slot_masks[name][None], run)
        v[CONTEXT, name, m] = context

    def attend_step(name, m):
        project_step(name, m)
        attend_only(name, m)

    def out_step(name, kind):
        context = jnp.concatenate([v[CONTEXT, name, m] for m in range(copies)], axis=1)
        v[CONTEXT, name] = context
        return dot("nn", [(context, out_full)], plain, [kind])

    def add(x, received):
        total = x.astype(F32)
        for y in received:
            total = total + y.astype(F32)
        return total.astype(BF)

    def first_hop(partial):
        n = partial.shape[0] // 2
        v[KEPT], v[AWAY] = partial[:n], partial[n:]

    def next_hop():
        return add(v[KEPT], [v[AWAY]])

    attend_step(slots[0], 0)
    if held == 2:
        order(MINE, (CONTEXT, OTHER, 0))
        attend_step(MINE, 0)
    order(
        (CONTEXT, slots[-1], 0),
        OUT_Z,
        *[(QKV, j, m) for j in range(run) for m in range(1, copies)],
    )
    out_z = v[OUT_Z]
    if per_shard < TEAM:
        fill = TEAM // per_shard
        out_z = out_z.reshape(HEADS // TEAM, fill, head_dim, wide)
        out_z = pick(out_z, q // per_shard, 1)
    out_z = out_z.reshape(team_heads * head_dim, wide)
    out_swapped = [out_z] + [swap(out_z, TEAM * m) for m in range(1, copies)]
    for m in range(1, copies):
        qkv_weight[m] = jnp.concatenate([v[QKV, j, m] for j in range(run)], axis=1)
        attend_step(slots[0], m)
        if m == 1:
            v[OUT_SWAPPED] = jnp.stack(out_swapped)
            order(OUT_SWAPPED, (CONTEXT, slots[0], m))
    out_columns = v[OUT_SWAPPED]
    out_full = jnp.concatenate([pick(out_columns, d ^ e) for e in range(copies)], axis=1)
    out_rows = [
        lax.dynamic_slice_in_dim(out_full, (d ^ m) * span, span, 0) for m in range(copies)
    ]
    out_full = jnp.concatenate(out_rows, axis=0)
    if held == 2:
        first_hop(out_step(OTHER, BF))
        order(KEPT, AWAY, MINE)
        v[AWAY] = swap(v[AWAY], 1)
        project_step(MINE, 1)
        order(AWAY, (QKV, MINE, 1))
        v[SEND] = next_hop()
        order(SEND, (QKV, MINE, 1), (UP_Z, 0))
        v[BACK] = swap(v[SEND], 2)
        for m in range(1, copies):
            if m > 1:
                project_step(MINE, m)
            attend_only(MINE, m)
        partial = out_step(MINE, F32)
    else:
        order((CONTEXT, BOTH, 0), (UP_Z, 0))
        partial = out_step(BOTH, F32)
        first_hop(partial[2 * rows :].astype(BF))
        v[AWAY] = swap(v[AWAY], 1)
        v[BACK] = swap(next_hop(), 2)
        partial = partial[: 2 * rows]
    for m in range(1, copies):
        v[UP, 0, m] = swap(v[UP_Z, 0], TEAM * m)
    v[THEIRS] = partial[rows:].astype(BF)
    order(
        THEIRS,
        BACK,
        *[(UP_Z, h) for h in range(1, halves)],
        *[(UP, 0, m) for m in range(1, copies)],
    )
    for h in range(1, halves):
        for m in range(1, copies):
            v[UP, h, m] = swap(v[UP_Z, h], TEAM * m)
    v[ATTENDED] = partial[:rows] + swap(v[THEIRS], 1).astype(F32)
    summed1 = own_tokens.astype(F32) + v[ATTENDED] + v[BACK].astype(F32) + bias_out
    normal1, scale1 = normalise(summed1)
    normed1 = normal1 * gain_one + shift_one

    def first_swaps(own):
        return [swap(own[:half], 2), swap(own[half:], 2)], swap(own, 1)

    def chunk_of(far_rows):
        return jnp.concatenate([far_rows, swap(far_rows, 1)], axis=0)

    def chunk_sum(sums):
        mine, theirs, backs = sums
        return mine + theirs.astype(F32) + jnp.concatenate(backs, axis=0).astype(F32)

    v[HIDDEN, 0] = normed1.astype(BF)
    (v[FAR, 0], v[FAR, 1]), v[HIDDEN, 1] = first_swaps(v[HIDDEN, 0])
    up_parts = {0: jnp.concatenate([v[UP_Z, h] for h in range(halves)], axis=1)}

    def up_step(i, m):
        v[VALUE, i, m], v[SLOPE, i, m] = dot(
            "nn",
            [(v[HIDDEN, i], up_parts[m])],
            lambda t, b: gelu_parts(t + b),
            [BF, BF],
            columns=[up_biases[m]],
        )

    up_step(0, 0)
    order(
        (HIDDEN, 1),
        (VALUE, 0, 0),
        *[(UP, h, m) for h in range(1, halves) for m in range(1, copies)],
    )
    up_step(1, 0)
    order((FAR, 0), (VALUE, 1, 0), (DOWN_Z, 0))
    for m in range(1, copies):
        v[DOWN, 0, m] = swap(v[DOWN_Z, 0], TEAM * m)
    v[HIDDEN, 2] = chunk_of(v[FAR, 0])
    up_step(2, 0)
    order((FAR, 1), (VALUE, 2, 0))
    v[HIDDEN, 3] = chunk_of(v[FAR, 1])
    up_step(3, 0)
    for m in range(1, copies):
        up_parts[m] = jnp.concatenate([v[UP, h, m] for h in range(halves)], axis=1)
        for i in (2, 3, 0, 1):
            up_step(i, m)
            if m == 1 and i == 3:
                order(
                    (VALUE, 3, 1),
                    (VALUE, 2, 1),
                    (HIDDEN, 0),
                    (HIDDEN, 1),
                    *[(DOWN_Z, h) for h in range(1, halves)],
                    *[(DOWN, 0, n) for n in range(1, copies)],
                )
                for h in range(1, halves):
                    for n in range(1, copies):
                        v[DOWN, h, n] = swap(v[DOWN_Z, h], TEAM * n)
    order(
        *[(VALUE, i, m) for i in range(2) for m in range(copies)],
        *[(DOWN, h, m) for h in range(1, halves) for m in range(1, copies)],
    )
    down_parts = {0: jnp.concatenate([v[DOWN_Z, h] for h in range(halves)], axis=0)}
    for m in range(1, copies):
        down_parts[m] = jnp.concatenate([v[DOWN, h, m] for h in range(halves)], axis=0)

    def down_step(i):
        pairs = [(v[VALUE, i, m], down_parts[m]) for m in range(copies)]
        v[PARTIAL, i] = dot("nn", pairs, plain, [F32 if i == 0 else BF])

    def hop_start(i):
        first_hop(v[PARTIAL, i])
        order(KEPT, AWAY)
        v[AWAY] = swap(v[AWAY], 1)

    def hop_end(i, *beside):
        order(KEPT, AWAY, *beside)
        v[SEND, i] = next_hop()
        order((SEND, i), *beside)
        v[BACK, i] = swap(v[SEND, i], 2)

    down_step(2)
    hop_start(2)
    down_step(3)
    hop_end(2, (PARTIAL, 3))
    hop_start(3)
    down_step(1)
    hop_end(3, (PARTIAL, 1))
    order((PARTIAL, 1), (VALUE, 0, 0), (BACK, 2))
    v[THEIRS] = swap(v[PARTIAL, 1], 1)
    down_step(0)
    order((PARTIAL, 0), THEIRS, (BACK, 2), (BACK, 3))
    theirs = v[THEIRS]
    backs = [v[BACK, 2], v[BACK, 3]]
    summed2 = normed1 + chunk_sum((v[PARTIAL, 0], theirs, backs)) + bias_down
    normal2, scale2 = normalise(summed2)
    result = (valid * (normal2 * gain_two + shift_two)).astype(BF)

    v[COTANGENT] = cotangent
    order(COTANGENT, (VALUE, 3, 0))
    v[COT, 0], v[COT, 1] = to_team(v[COTANGENT])
    v[NORMAL2] = normal2
    order(NORMAL2, (COT, 0), (COT, 1))
    normal2 = v[NORMAL2]
    grad_out = jnp.concatenate([v[COT, 0], v[COT, 1]], axis=0).astype(F32) * valid
    dsum2 = norm_backward(grad_out, gain_two, normal2, scale2)
    gain_two_grad = jnp.sum(grad_out * normal2, axis=0)
    shift_two_grad = jnp.sum(grad_out, axis=0)
    v[DDOWN, 0] = dsum2.astype(BF)
    down_bias_grad = jnp.sum(v[DDOWN, 0].astype(F32), axis=0)
    v[RESULT] = result
    order(RESULT, (DDOWN, 0))
    v[LAYER, 0], v[LAYER, 1] = leave_team(v[RESULT][:block], v[RESULT][block:])

    def over_copies(shares):
        total = shares[0].astype(F32)
        for m in range(1, copies):
            total = total + swap(shares[m], TEAM * m).astype(F32)
        return total.astype(BF)

    def to_owner(x):
        return lax.psum_scatter(x, "fsdp", scatter_dimension=0, tiled=True)

    def from_all(x):
        return lax.all_gather(x, "rep", axis=0, tiled=True)

    def in_order(pieces):
        stacked = jnp.stack([pieces[m] for m in range(reps)])
        return jnp.stack([pick(stacked, rep ^ r) for r in range(reps)])

    sub = parts * half_unit

    def backward_step(i):
        for m in range(copies):
            v[DBEFORE, i, m] = dot(
                "nt",
                [(v[DDOWN, i], down_parts[m])],
                lambda t, s: (t * s.astype(F32),),
                [BF],
                tiles=[v[SLOPE, i, m]],
            )
        pairs = [(v[DBEFORE, i, m], up_parts[m]) for m in range(copies)]
        v[PARTIAL, i] = dot("nt", pairs, plain, [F32 if i == 0 else BF])

    def down_grad_step(m, h):
        pairs = [(v[VALUE, i, m], v[DDOWN, i]) for i in range(4)]
        v[DOWN, SHARE, h, m] = dot("tn", pairs, plain, [BF], left=(h, halves))

    def up_grad_step(m, h):
        pairs = [(v[HIDDEN, i], v[DBEFORE, i, m]) for i in range(4)]
        v[UP, SHARE, h, m] = dot("tn", pairs, plain, [BF], right=(h, halves))

    def swap_share(kind, h):
        for m in range(1, copies):
            v[kind, RECEIVED, h, m] = swap(v[kind, SHARE, h, m], TEAM * m)

    def shares(kind, *those):
        return [(kind, SHARE, h, m) for h in those for m in range(1, copies)]

    def received(kind, *those):
        return [(kind, RECEIVED, h, m) for h in those for m in range(1, copies)]

    def reduce_step(kind, h):
        total = add(v[kind, SHARE, h, 0], [v[n] for n in received(kind, h)])
        v[kind, PART, h] = to_owner(total)

    more = range(1, copies)
    late = range(1, halves)
    far, v[DDOWN, 1] = first_swaps(v[DDOWN, 0])
    v[FAR, 0], v[FAR, 1] = far
    backward_step(0)
    order((DDOWN, 1), (PARTIAL, 0))
    backward_step(1)
    order((PARTIAL, 1), (FAR, 0), (FAR, 1))
    v[THEIRS] = swap(v[PARTIAL, 1], 1)
    for i in (2, 3):
        v[DDOWN, i] = chunk_of(v[FAR, i - 2])
    for h in range(halves):
        for m in more:
            down_grad_step(m, h)
    order(*shares(DOWN, *range(halves)), (DDOWN, 2))
    for h in range(halves):
        swap_share(DOWN, h)
    backward_step(2)
    hop_start(2)
    order((PARTIAL, 2), (DDOWN, 3))
    backward_step(3)
    hop_end(2, (PARTIAL, 3), (DDOWN, 0))
    hop_start(3)
    order((PARTIAL, 3), (DDOWN, 0))
    down_grad_step(0, 0)
    hop_end(3, (DOWN, SHARE, 0, 0), (DDOWN, 0), (LAYER, 0), (LAYER, 1))
    for h in late:
        down_grad_step(0, h)
    order(*[(DOWN, SHARE, h, 0) for h in range(halves)], *received(DOWN, 0), (BACK, 2))
    reduce_step(DOWN, 0)
    order(
        (PARTIAL, 0),
        (BACK, 2),
        (BACK, 3),
        THEIRS,
        *[(DOWN, SHARE, h, 0) for h in late],
    )
    backs = [v[BACK, 2], v[BACK, 3]]
    dnormed1 = dsum2 + chunk_sum((v[PARTIAL, 0], v[THEIRS], backs))
    dsum1 = norm_backward(dnormed1, gain_one, normal1, scale1)
    gain_one_grad = jnp.sum(dnormed1 * normal1, axis=0)
    shift_one_grad = jnp.sum(dnormed1, axis=0)
    v[DATTN] = dsum1.astype(BF)
    out_bias_grad = jnp.sum(v[DATTN].astype(F32), axis=0)

    order((HIDDEN, 0), DATTN)
    v[DATTN_NEAR] = swap(v[DATTN], 1)
    v[DATTN_FAR] = swap(v[DATTN], 2)
    for h in range(halves):
        for m in more:
            up_grad_step(m, h)
    order(
        *shares(UP, *range(halves)),
        DATTN_NEAR,
        (HIDDEN, 0),
        *received(DOWN, *late),
        *[(DOWN, SHARE, h, 0) for h in late],
    )
    for h in range(halves):
        swap_share(UP, h)
    for h in late:
        reduce_step(DOWN, h)

    v[DATTN_MINE] = jnp.concatenate([v[DATTN], v[DATTN_NEAR]], axis=0)
    qkv_sums = {}

    def back_step(name, dcontext, m):
        v[DQKV, name, m], qkv_sums[name, m] = attend_backward(
            v[QKV, name, m], dcontext, log_totals[name, m], slot_masks[name][:, None], run, m
        )

    def context_grad(x):
        return dot("nt", [(x, out_full)], plain, [BF])

    def far_rows():
        return jnp.concatenate([v[DATTN_FAR], swap(v[DATTN_FAR], 1)], axis=0)

    def out_grad_step():
        pairs = [(v[CONTEXT, MINE], v[DATTN_MINE]), (v[CONTEXT, OTHER], dattn_other)]
        share = dot("tn", pairs, plain, [BF])
        for m in range(copies):
            rows_of = [
                lax.dynamic_slice(share, ((d ^ e) * span, (d ^ m) * wide), (span, wide))
                for e in range(copies)
            ]
            v[OUT, SHARE, 0, m] = jnp.concatenate(rows_of, axis=0)

    def out_reduce_step():
        total = add(v[OUT, SHARE, 0, 0], [v[n] for n in received(OUT, 0)])
        if per_shard < TEAM:
            fill = TEAM // per_shard
            total = total.reshape(HEADS // TEAM, 1, head_dim, -1)
            chosen = (jnp.arange(fill) == q // per_shard)[None, :, None, None]
            total = jnp.where(chosen, total, jnp.zeros((), BF))
            total = total.reshape(parts * head_dim, -1)
        v[OUT, PART, 0] = to_owner(total)

    def to_more(kind, mask):
        for m in [m for m in range(reps) if (kind, WHOLE, m) in v]:
            v[kind, WHOLE, m ^ mask] = swap(v[kind, WHOLE, m], mask)

    def all_of(kind):
        return [(kind, WHOLE, m) for m in range(reps) if (kind, WHOLE, m) in v]

    near_far = [2] + [TEAM << i for i in range(copies.bit_length() - 1)]

    def vector_table():
        def place_heads(i):
            full = jnp.zeros((copies, run, TEAM, head_dim), F32)
            for m in range(copies):
                share = sum(qkv_sums[name, m] for name in names)
                share = share.reshape(run, 3, head_dim)[:, i].reshape(1, run, 1, head_dim)
                full = lax.dynamic_update_slice(full, share, (d ^ m, 0, q, 0))
            return full.reshape(width)

        up_sums = jnp.zeros((parts, reps, halves, half_unit), F32)
        for m in range(copies):
            share = sum(jnp.sum(v[DBEFORE, i, m].astype(F32), axis=0) for i in range(4))
            share = share.reshape(halves, parts, half_unit).transpose(1, 0, 2)[:, None]
            up_sums = lax.dynamic_update_slice(up_sums, share, (0, rep ^ (TEAM * m), 0, 0))
        vector_sums = [
            place_heads(0),
            place_heads(2),
            out_bias_grad,
            gain_one_grad,
            shift_one_grad,
            down_bias_grad,
            gain_two_grad,
            shift_two_grad,
        ]
        return jnp.concatenate(
            [s.reshape(parts, shard) for s in vector_sums] + [up_sums.reshape(parts, -1)], axis=1
        )

    def vector_start():
        vector_sums = vector_table()
        v[VECTOR, 0] = pick(vector_sums, z)
        for k in range(1, parts):
            v[VECTOR, k] = shift(pick(vector_sums, (z - k) % parts), k)

    def vector_names():
        return [(VECTOR, k) for k in range(parts)]

    def vector_step(mask):
        if mask == 1:
            v[VECTOR, 0] = sum(v[n] for n in vector_names())
        v[VECTOR, 0] = v[VECTOR, 0] + swap(v[VECTOR, 0], mask)

    backwards = list(reversed(range(copies)))
    if held == 2:
        names = (MINE, OTHER)
        dcontext = context_grad(v[DATTN_MINE])
        for m in backwards:
            back_step(MINE, dcontext, m)
        order(
            DATTN_FAR,
            *[(DQKV, MINE, m) for m in range(copies)],
        )
        v[DATTN_OTHER] = far_rows()
        dattn_other = v[DATTN_OTHER]
        out_grad_step()
        order(*[(OUT, SHARE, 0, m) for m in range(copies)], DATTN_OTHER, (HIDDEN, 0))
        swap_share(OUT, 0)
        up_grad_step(0, 0)
        order(DATTN_OTHER, *received(UP, 0), (UP, SHARE, 0, 0))
        reduce_step(UP, 0)
        dattn_other = v[DATTN_OTHER]
        dcontext = context_grad(dattn_other)
        for m in backwards:
            back_step(OTHER, dcontext, m)
    else:
        names = (BOTH,)
        dattn_other = far_rows()
        dattn_both = jnp.concatenate([v[DATTN_MINE], dattn_other], axis=0)
        dcontext = context_grad(dattn_both)
        for m in backwards:
            back_step(BOTH, dcontext, m)
        up_grad_step(0, 0)
        reduce_step(UP, 0)
        v[CONTEXT, MINE] = v[CONTEXT, BOTH][: 2 * rows]
        v[CONTEXT, OTHER] = v[CONTEXT, BOTH][2 * rows :]
        out_grad_step()
        swap_share(OUT, 0)
        for m in range(copies):
            v[DQKV, MINE, m] = v[DQKV, BOTH, m][: 2 * rows]
            v[DQKV, OTHER, m] = v[DQKV, BOTH, m][2 * rows :]
    order(
        *[(DQKV, OTHER, m) for m in range(copies)],
        *[(DOWN, PART, h) for h in range(halves)],
    )
    vector_start()
    v[DOWN, WHOLE, 0] = jnp.concatenate([v[DOWN, PART, h] for h in range(halves)], axis=0)
    to_more(DOWN, near_far[0])

    def qkv_grad_step(m):
        pairs = [(tokens_mine, v[DQKV, MINE, m]), (tokens_other, v[DQKV, OTHER, m])]
        v[QKV, SHARE, 0, m] = dot("tn", pairs, plain, [BF])

    def dtokens_partial(name, kind):
        pairs = [(v[DQKV, name, m], qkv_weight[m]) for m in range(copies)]
        return dot("nt", pairs, plain, [kind])

    for m in more:
        qkv_grad_step(m)
    first_hop(dtokens_partial(OTHER, BF))
    order(
        KEPT,
        AWAY,
        *[(DQKV, MINE, m) for m in range(copies)],
        *vector_names(),
        (HIDDEN, 0),
    )
    v[AWAY] = swap(v[AWAY], 1)
    vector_step(1)
    qkv_grad_step(0)
    for h in late:
        up_grad_step(0, h)
    order(
        *shares(QKV, 0),
        (QKV, SHARE, 0, 0),
        KEPT,
        AWAY,
        *received(OUT, 0),
        (OUT, SHARE, 0, 0),
        *received(UP, *late),
        *[(UP, SHARE, h, 0) for h in late],
        *[(DQKV, MINE, m) for m in range(copies)],
    )
    swap_share(QKV, 0)
    v[SEND] = next_hop()
    v[BACK] = swap(v[SEND], 2)
    out_reduce_step()
    for h in late:
        reduce_step(UP, h)
    partial = dtokens_partial(MINE, F32)
    v[THEIRS] = partial[rows:].astype(BF)
    order(
        THEIRS,
        BACK,
        (QKV, SHARE, 0, 0),
        *received(QKV, 0),
        *all_of(DOWN),
        (OUT, PART, 0),
        *[(UP, PART, h) for h in range(halves)],
        (VECTOR, 0),
    )
    reduce_step(QKV, 0)
    v[THEIRS] = swap(v[THEIRS], 1)
    v[OUT, WHOLE, 0] = v[OUT, PART, 0]
    v[UP, WHOLE, 0] = jnp.concatenate([v[UP, PART, h] for h in range(halves)], axis=1)
    far_near = near_far[1:] + near_far[:1]
    to_more(UP, far_near[0])
    to_more(OUT, far_near[0])
    order(THEIRS, BACK, *all_of(UP), *all_of(OUT), *all_of(DOWN))
    for i, mask in enumerate(far_near[1:]):
        to_more(UP, mask)
        to_more(OUT, mask)
        to_more(DOWN, near_far[1 + i])
    vector_step(2)
    dtokens = dsum1 + partial[:rows] + v[THEIRS].astype(F32) + v[BACK].astype(F32)
    v[OWN] = dtokens.astype(BF)
    order(
        (QKV, PART, 0),
        OWN,
        (VECTOR, 0),
        *all_of(UP),
        *all_of(OUT),
        *all_of(DOWN),
    )
    qkv_part = lax.all_gather(v[QKV, PART, 0], "rep", axis=0, tiled=False)
    v[GRAD, 0], v[GRAD, 1] = leave_team(v[OWN][:block], v[OWN][block:])
    to_more(UP, 1)
    to_more(DOWN, 1)
    to_more(OUT, 1)
    for mask in near_far[1:]:
        vector_step(mask)
    order(*all_of(UP), *all_of(OUT), *all_of(DOWN), (VECTOR, 0))
    layer_out = settle(v[LAYER, 0], v[LAYER, 1])
    tokens_grad = settle(v[GRAD, 0], v[GRAD, 1]).astype(F32)
    out_grad = in_order({m: v[OUT, WHOLE, m] for m in range(reps)})

    if per_shard >= TEAM:
        out_grad = out_grad.reshape(copies, TEAM, per_shard // TEAM, head_dim, wide)
        out_grad = out_grad.transpose(2, 1, 3, 0, 4)
    else:
        fill = TEAM // per_shard
        out_grad = out_grad.reshape(copies, fill, per_shard, head_dim, wide)
        out_grad = pick(out_grad, z % fill, 1).transpose(1, 2, 0, 3)
    out_grad = out_grad.reshape(-1, width).astype(F32)

    aligned = half_unit % LANES == 0 and head_dim % LANES == 0
    if aligned:
        places = [rep ^ m for m in range(reps)]
        down_grad = place_rows(
            [v[DOWN, WHOLE, m] for m in range(reps)], places, (hidden // parts, width)
        )
        up_grad = place_columns(
            [v[UP, WHOLE, m] for m in range(reps)],
            places,
            (shard, hidden),
            half_unit,
            lambda i, r: ((i % parts) * reps + r) * halves + i // parts,
        )
        qkv_grads = place_heads_grad(qkv_part, reps, run, head_dim)
    else:
        def in_order_of(kind):
            return in_order({m: v[kind, WHOLE, m] for m in range(reps)})

        down_grad = in_order_of(DOWN).reshape(-1, width).astype(F32)
        up_grad = in_order_of(UP).reshape(reps, shard, halves, parts, half_unit)
        up_grad = up_grad.transpose(1, 3, 0, 2, 4).reshape(shard, hidden).astype(F32)
        qkv_final = qkv_part.reshape(copies, TEAM, shard, run, 3, head_dim)
        qkv_grads = [
            qkv_final[:, :, :, :, i].transpose(2, 0, 3, 1, 4).reshape(shard, width).astype(F32)
            for i in range(3)
        ]

    total = v[VECTOR, 0]
    small = [total[i * shard : (i + 1) * shard] for i in range(8)]
    up_bias_grad = total[8 * shard :]
    return (
        layer_out,
        tokens_grad,
        qkv_grads[0],
        qkv_grads[1],
        qkv_grads[2],
        out_grad,
        small[0],
        small[1],
        small[2],
        small[3],
        small[4],
        up_grad,
        up_bias_grad,
        down_grad,
        small[5],
        small[6],
        small[7],
    )


def solution(mesh):
    three, two, one = P("rep", "fsdp", None), P("fsdp", None), P("fsdp")
    placed = (three, P("rep"), two, two, two, two, one, one, one, one, one)
    placed += (two, one, two, one, one, one, three)
    given = (three, three, two, two, two, two, one, one, one, one, one)
    given += (two, one, two, one, one, one)
    return jax.shard_map(local, mesh=mesh, in_specs=placed, out_specs=given, check_vma=False)
```

time: 1820 us -> 1190 us (0.65)
  waiting for transfers between devices: 1000 us -> 429 us
  Pallas kernels: 0 us -> 406 us
  matrix products: 349 us -> 0 us
  local copies, waits for them, and re-layouts: 205 us -> 138 us
  other arithmetic: 152 us -> 103 us
  starting transfers between devices: 41.5 us -> 83.8 us
  blocking collectives: 36.2 us -> 0 us
    pallas_call x0 -> x60, Pallas kernels: none -> 406 us  [the longest x45 309 us: dot(): pl.pallas_call(kernel, grid=(size // step,), in_specs=x_specs + w_specs +...]
    dot_general x66 -> x0, matrix products: 349 us -> none  [the longest x14 105 us: mm_t(): lax.dot_general(left, right, (((1,), (1,)), ((), ())), preferred_element_...]
    ppermute x32 -> x75, waiting for transfers between devices: 674 us -> 344 us  [swap(): return lax.ppermute(x, 'rep', [(i, i ^ mask) for i in range(reps)])]
    all_gather x4 -> x1, waiting for transfers between devices: 113 us -> 0.01 us  [local(): qkv_part = lax.all_gather(v[QKV, PART, 0], 'rep', axis=0, tiled=False)]
    convert_element_type x9 -> x0, local copies, waits for them, and re-layouts: 67.1 us -> none  [the longest x6 34.8 us: local(): qkv_final[:, :, :, i].transpose(2, 0, 3, 1, 4).reshape(shard, width)]
    psum x1 -> x0, waiting for transfers between devices: 62.4 us -> none  [local(): sums = pick(lax.psum(sums, ('rep', 'fsdp')), z)]
    reduce_scatter x4 -> x6, waiting for transfers between devices: 55.1 us -> 0.03 us  [to_owner(): return lax.psum_scatter(x, 'fsdp', scatter_dimension=0, tiled=True)]
    ppermute x2, waiting for transfers between devices: 54.5 us -> 0.01 us  [to_team(): first = lax.ppermute(pick(x, parity), axes, even)]
  transfers between devices with their start and end apart: 53 -> 103, of which waited for: 22 -> 37; matrix products, arithmetic and copies ran while one was open for 31% -> 15% of each run, Pallas kernels for 0% -> 30%
where the time goes in v2:
time: 1190 us; the launch traced here: 1180 us
  waiting for transfers between devices  429 us (36%)
  Pallas kernels  406 us (34%)
  local copies, waits for them, and re-layouts  138 us (12%)
  other arithmetic  103 us (9%)
  starting transfers between devices  83.8 us (7%)
  between operations  17.1 us (1%)
    ppermute x75, waiting for transfers between devices, swap(): return lax.ppermute(x, 'rep', [(i, i ^ mask) for i in range(reps)])  344 us
    pallas_call x45, Pallas kernels, dot(): pl.pallas_call(kernel, grid=(size // step,), in_specs=x_specs + w_specs +...  309 us
    unnamed x380, local copies, waits for them, and re-layouts  79.6 us
    ppermute x75, starting transfers between devices, swap(): return lax.ppermute(x, 'rep', [(i, i ^ mask) for i in range(reps)])  53.9 us
    convert_element_type x12, other arithmetic, add(): return total.astype(BF)  37.3 us
    all_gather x7, waiting for transfers between devices, over_z(): return lax.all_gather(x, 'fsdp', axis=0, tiled=True)  36.2 us
    pallas_call x4, Pallas kernels, attend_backward(): pl.pallas_call(kernel, grid=(heads,), in_specs=[pl.BlockSpec((rows, 3 * h...  34.6 us
    ppermute x2, waiting for transfers between devices, leave_team(): second = lax.ppermute(second, axes, [(b, a) for a, b in odd])  26.6 us
  transfers between devices with their start and end apart: 103, of which 37 were waited for; matrix products, arithmetic and copies ran while one was open for 15% of the time, Pallas kernels for 30%

profile of v2, /device:TPU:18, one launch (start us, length us, event | category | flops | bytes accessed | tf_op | source)
XLA Modules:
  0.0 1177.0 jit_solution(1811580149760799069)
XLA Ops:
  66.3 24.1 %collective-permute-done.10 = bf16[256,2048]{1,0:T(8,128)(2,1)S(1)} collective-permute-done((bf16[256,2048]{1,0:T(8,128)(2,1)}, bf16[256,2048]{1,0:T(8,128)(2,1)S(1)}, u32[]{:S(2)}, u32[]{:S(2)}) %collective-permute-start.10) | collective-permute-done | bytes 1048608 | tf_op jit(solution)/shard_map/ppermute | solution.py:419
  90.4 21.8 %collective-permute-done.11 = bf16[256,2048]{1,0:T(8,128)(2,1)S(1)} collective-permute-done((bf16[256,2048]{1,0:T(8,128)(2,1)}, bf16[256,2048]{1,0:T(8,128)(2,1)S(1)}, u32[]{:S(2)}, u32[]{:S(2)}) %collective-permute-start.11) | collective-permute-done | bytes 1048608 | tf_op jit(solution)/shard_map/ppermute | solution.py:419
  126.9 11.2 all-gather.12.cloned.1.call-done
  177.0 11.9 %collective-permute-done.15 = bf16[2048,384]{1,0:T(8,128)(2,1)} collective-permute-done((bf16[2048,384]{1,0:T(8,128)(2,1)}, bf16[2048,384]{1,0:T(8,128)(2,1)}, u32[]{:S(2)}, u32[]{:S(2)}) %collective-permute-start.15) | collective-permute-done | bytes 1572896 | tf_op jit(solution)/shard_map/ppermute | solution.py:419
  256.0 25.0 %all-gather.18.cloned.1.call-done = bf16[2048,512]{1,0:T(8,128)(2,1)} async-done(((bf16[512,512]{1,0:T(8,128)(2,1)}), bf16[2048,512]{1,0:T(8,128)(2,1)}) %all-gather.18.cloned.1.call-update) | async-done | bytes 2097168 | tf_op jit(solution)/shard_map/all_gather | solution.py:513
  313.1 22.1 %collective-permute-done.22 = bf16[2048,512]{1,0:T(8,128)(2,1)} collective-permute-done((bf16[2048,512]{1,0:T(8,128)(2,1)}, bf16[2048,512]{1,0:T(8,128)(2,1)}, u32[]{:S(2)}, u32[]{:S(2)}) %collective-permute-start.22) | collective-permute-done | bytes 2097184 | tf_op jit(solution)/shard_map/ppermute | solution.py:419
  354.0 15.0 %collective-permute-done.23 = bf16[256,2048]{1,0:T(8,128)(2,1)S(1)} collective-permute-done((bf16[256,2048]{1,0:T(8,128)(2,1)}, bf16[256,2048]{1,0:T(8,128)(2,1)S(1)}, u32[]{:S(2)}, u32[]{:S(2)}) %collective-permute-start.23) | collective-permute-done | bytes 1048608 | tf_op jit(solution)/shard_map/ppermute | solution.py:419
  411.7 28.3 %collective-permute-done.28 = bf16[512,2048]{1,0:T(8,128)(2,1)} collective-permute-done((bf16[512,2048]{1,0:T(8,128)(2,1)}, bf16[512,2048]{1,0:T(8,128)(2,1)}, u32[]{:S(2)}, u32[]{:S(2)}) %collective-permute-start.28) | collective-permute-done | bytes 2097184 | tf_op jit(solution)/shard_map/ppermute | solution.py:419
  476.8 15.3 %collective-permute-done.31 = bf16[256,2048]{1,0:T(8,128)(2,1)} collective-permute-done((bf16[256,2048]{1,0:T(8,128)(2,1)S(1)}, bf16[256,2048]{1,0:T(8,128)(2,1)}, u32[]{:S(2)}, u32[]{:S(2)}) %collective-permute-start.31) | collective-permute-done | bytes 1048608 | tf_op jit(solution)/shard_map/ppermute | solution.py:419
  504.5 13.4 %collective-permute-done.33 = bf16[256,2048]{1,0:T(8,128)(2,1)} collective-permute-done((bf16[256,2048]{1,0:T(8,128)(2,1)}, bf16[256,2048]{1,0:T(8,128)(2,1)}, u32[]{:S(2)}, u32[]{:S(2)}) %collective-permute-start.33) | collective-permute-done | bytes 1048608 | tf_op jit(solution)/shard_map/ppermute | solution.py:419
  530.0 12.4 %collective-permute-done.35 = bf16[256,2048]{1,0:T(8,128)(2,1)S(1)} collective-permute-done((bf16[256,2048]{1,0:T(8,128)(2,1)}, bf16[256,2048]{1,0:T(8,128)(2,1)S(1)}, u32[]{:S(2)}, u32[]{:S(2)}) %collective-permute-start.35) | collective-permute-done | bytes 1048608 | tf_op jit(solution)/shard_map/ppermute | solution.py:449
  586.5 10.6 collective-permute-done.38
  680.0 10.7 collective-permute-done.44
  718.0 9.8 multiply_reduce_fusion.1
  816.9 14.4 %collective-permute-done.53 = bf16[2048,512]{1,0:T(8,128)(2,1)} collective-permute-done((bf16[2048,512]{1,0:T(8,128)(2,1)}, bf16[2048,512]{1,0:T(8,128)(2,1)}, u32[]{:S(2)}, u32[]{:S(2)}) %collective-permute-start.53) | collective-permute-done | bytes 2097184 | tf_op jit(solution)/shard_map/ppermute | solution.py:419
  883.3 10.0 shard_map.357
  901.6 9.9 shard_map.359
  926.8 10.4 shard_map.361
  941.1 52.4 %collective-permute-done.62.refs_2_ = bf16[256,2048]{1,0:T(8,128)(2,1)} collective-permute-done((bf16[256,2048]{1,0:T(8,128)(2,1)S(1)}, bf16[256,2048]{1,0:T(8,128)(2,1)}, u32[]{:S(2)}, u32[]{:S(2)}) %collective-permute-start.62) | collective-permute-done | bytes 1048608 | tf_op jit(solution)/shard_map/ppermute | solution.py:419
  1002.1 28.2 %collective-permute-done.66 = bf16[128,1024]{1,0:T(8,128)(2,1)S(1)} collective-permute-done((bf16[128,1024]{1,0:T(8,128)(2,1)S(1)}, bf16[128,1024]{1,0:T(8,128)(2,1)S(1)}, u32[]{:S(2)}, u32[]{:S(2)}) %collective-permute-start.66) | collective-permute-done | bytes 262176 | tf_op jit(solution)/shard_map/ppermute | solution.py:419
  1048.1 40.3 %collective-permute-done.71 = bf16[128,1024]{1,0:T(8,128)(2,1)S(1)} collective-permute-done((bf16[128,1024]{1,0:T(8,128)(2,1)S(1)}, bf16[128,1024]{1,0:T(8,128)(2,1)S(1)}, u32[]{:S(2)}, u32[]{:S(2)}) %collective-permute-start.71) | collective-permute-done | bytes 262176 | tf_op jit(solution)/shard_map/ppermute | solution.py:419
  1122.1 10.3 shard_map.364
  1132.4 10.0 shard_map.363
  1143.0 15.8 %collective-permute-done.75 = bf16[256,2048]{1,0:T(8,128)(2,1)S(1)} collective-permute-done((bf16[256,2048]{1,0:T(8,128)(2,1)S(1)}, bf16[256,2048]{1,0:T(8,128)(2,1)S(1)}, u32[]{:S(2)}, u32[]{:S(2)}) %collective-permute-start.75) | collective-permute-done | bytes 1048608 | tf_op jit(solution)/shard_map/ppermute | solution.py:457
  (799 shorter events, 726.4 us)
Async XLA Ops:
  7.2 105.0 %all-gather.10.cloned.1.call-start = ((), (), s32[]{:S(2)}) async-start(), calls=%async_computation.6 | async-start | bytes 1966080 | tf_op jit(solution)/shard_map/all_gather | solution.py:513
  63.3 74.8 %all-gather.12.cloned.1.call-start = ((), (), s32[]{:S(2)}) async-start(), calls=%async_computation.7 | async-start | bytes 1966080 | tf_op jit(solution)/shard_map/all_gather | solution.py:513
  64.1 112.9 %all-gather.14.cloned.1.call-start = ((), (), s32[]{:S(2)}) async-start(), calls=%async_computation.8 | async-start | bytes 1310720 | tf_op jit(solution)/shard_map/all_gather | solution.py:513
  114.6 123.4 %all-gather.16.cloned.1.call-start = ((), (), s32[]{:S(2)}) async-start(), calls=%async_computation.9 | async-start | bytes 2621440 | tf_op jit(solution)/shard_map/all_gather | solution.py:513
  118.5 58.5 %collective-permute-start.14 = (bf16[2048,384]{1,0:T(8,128)(2,1)}, bf16[2048,384]{1,0:T(8,128)(2,1)}, u32[]{:S(2)}, u32[]{:S(2)}) collective-permute-start(bf16[2048,384]{1,0:T(8,128)(2,1)} %all-gather.10.cloned.1.call-done), channel_id=1, source_target_pairs={{0,16},{4,20},{8,24},{12,28},{16,0},{20,4},{24,8},{28,12},{1,17},{... | collective-permute-start | bytes 4718600 | tf_op jit(solution)/shard_map/ppermute | solution.py:419
  138.1 50.8 %collective-permute-start.15 = (bf16[2048,384]{1,0:T(8,128)(2,1)}, bf16[2048,384]{1,0:T(8,128)(2,1)}, u32[]{:S(2)}, u32[]{:S(2)}) collective-permute-start(bf16[2048,384]{1,0:T(8,128)(2,1)} %all-gather.12.cloned.1.call-done), channel_id=1, source_target_pairs={{0,16},{4,20},{8,24},{12,28},{16,0},{20,4},{24,8},{28,12},{1,17},{... | collective-permute-start | bytes 4718600 | tf_op jit(solution)/shard_map/ppermute | solution.py:419
  190.5 90.5 %all-gather.18.cloned.1.call-start = ((), (), s32[]{:S(2)}) async-start(), calls=%async_computation.10 | async-start | bytes 2621440 | tf_op jit(solution)/shard_map/all_gather | solution.py:513
  225.2 118.0 %all-gather.20.cloned.1.call-start = ((), (), s32[]{:S(2)}) async-start(), calls=%async_computation.11 | async-start | bytes 2621440 | tf_op jit(solution)/shard_map/all_gather | solution.py:513
  286.7 103.8 %all-gather.22.cloned.1.call-start = ((), (), s32[]{:S(2)}) async-start(), calls=%async_computation.12 | async-start | bytes 2621440 | tf_op jit(solution)/shard_map/all_gather | solution.py:513
  301.6 565.4 %reduce-scatter.7.cloned.1.call-start = ((), (), s32[]{:S(2)}) async-start(), calls=%async_computation.13 | async-start | bytes 2621440 | tf_op jit(solution)/shard_map/reduce_scatter | solution.py:805
  693.6 61.1 %collective-permute-start.51 = (bf16[512,2048]{1,0:T(8,128)(2,1)}, bf16[512,2048]{1,0:T(8,128)(2,1)}, u32[]{:S(2)}, u32[]{:S(2)}) collective-permute-start(bf16[512,2048]{1,0:T(8,128)(2,1)} %shard_map.338), channel_id=1, source_target_pairs={{0,16},{4,20},{8,24},{12,28},{16,0},{20,4},{24,8},{28,12},{1,17},{... | collective-permute-start | bytes 6291464 | tf_op jit(solution)/shard_map/ppermute | solution.py:419
  708.6 158.4 %reduce-scatter.9.cloned.1.call-start = ((), (), s32[]{:S(2)}) async-start(), calls=%async_computation.14 | async-start | bytes 2621440 | tf_op jit(solution)/shard_map/reduce_scatter | solution.py:805
  786.9 206.5 %reduce-scatter.13.cloned.1.call-start = ((), (), s32[]{:S(2)}) async-start(), calls=%async_computation.16 | async-start | bytes 2621440 | tf_op jit(solution)/shard_map/reduce_scatter | solution.py:805
  790.2 121.3 %collective-permute-start.59 = (bf16[2048,512]{1,0:T(8,128)(2,1)}, bf16[2048,512]{1,0:T(8,128)(2,1)}, u32[]{:S(2)}, u32[]{:S(2)}) collective-permute-start(bf16[2048,512]{1,0:T(8,128)(2,1)} %shard_map.348), channel_id=1, source_target_pairs={{0,16},{4,20},{8,24},{12,28},{16,0},{20,4},{24,8},{28,12},{1,17},{... | collective-permute-start | bytes 6291464 | tf_op jit(solution)/shard_map/ppermute | solution.py:419
  861.2 132.3 %reduce-scatter.11.cloned.1.call-start = ((), (), s32[]{:S(2)}) async-start(), calls=%async_computation.15 | async-start | bytes 1310720 | tf_op jit(solution)/shard_map/reduce_scatter | solution.py:805
  912.9 80.6 %reduce-scatter.15.cloned.1.call-start = ((), (), s32[]{:S(2)}) async-start(), calls=%async_computation.17 | async-start | bytes 2621440 | tf_op jit(solution)/shard_map/reduce_scatter | solution.py:805
  917.3 173.5 %reduce-scatter.17.cloned.1.call-start = ((), (), s32[]{:S(2)}) async-start(), calls=%async_computation.18 | async-start | bytes 3932160 | tf_op jit(solution)/shard_map/reduce_scatter | solution.py:805
  917.4 76.1 %collective-permute-start.61 = (bf16[2048,768]{1,0:T(8,128)(2,1)}, bf16[2048,768]{1,0:T(8,128)(2,1)}, u32[]{:S(2)}, u32[]{:S(2)}) collective-permute-start(bf16[2048,768]{1,0:T(8,128)(2,1)} %shard_map.357), channel_id=1, source_target_pairs={{0,16},{4,20},{8,24},{12,28},{16,0},{20,4},{24,8},{28,12},{1,17},{... | collective-permute-start | bytes 9437192 | tf_op jit(solution)/shard_map/ppermute | solution.py:419
  923.3 70.1 %collective-permute-start.60 = (bf16[512,2048]{1,0:T(8,128)(2,1)}, bf16[512,2048]{1,0:T(8,128)(2,1)}, u32[]{:S(2)}, u32[]{:S(2)}) collective-permute-start(bf16[512,2048]{1,0:T(8,128)(2,1)} %add_convert_fusion.3), channel_id=1, source_target_pairs={{0,8},{4,12},{8,0},{12,4},{16,24},{20,28},{24,16},{28,20},{1,9},{5... | collective-permute-start | bytes 6291464 | tf_op jit(solution)/shard_map/ppermute | solution.py:419
  924.0 69.4 %collective-permute-start.62 = (bf16[256,2048]{1,0:T(8,128)(2,1)S(1)}, bf16[256,2048]{1,0:T(8,128)(2,1)}, u32[]{:S(2)}, u32[]{:S(2)}) collective-permute-start(bf16[256,2048]{1,0:T(8,128)(2,1)S(1)} %constant_dynamic-update-slice_fusion.41.refs_0_), channel_id=1, source_target_pairs={{0,8},{4,12},{8,0},{12,4},{16,24},{20,28},{24,16},{28,20},{1,9},{5... | collective-permute-start | bytes 3145736 | tf_op jit(solution)/shard_map/ppermute | solution.py:419
  998.8 162.4 %all-gather.24.cloned.1.call-start = ((), (), s32[]{:S(2)}) async-start(), calls=%async_computation.19 | async-start | bytes 7077888 | tf_op jit(solution)/shard_map/all_gather | solution.py:1119
  1032.4 56.0 %collective-permute-start.68 = (bf16[512,1024]{1,0:T(8,128)(2,1)S(1)}, bf16[512,1024]{1,0:T(8,128)(2,1)S(1)}, u32[]{:S(2)}, u32[]{:S(2)}) collective-permute-start(bf16[512,1024]{1,0:T(8,128)(2,1)S(1)} %constant_dynamic-update-slice_fusion.43.refs_0_), channel_id=1, source_target_pairs={{0,8},{4,12},{8,0},{12,4},{16,24},{20,28},{24,16},{28,20},{1,9},{5... | collective-permute-start | bytes 3145736 | tf_op jit(solution)/shard_map/ppermute | solution.py:419
  1033.0 55.4 %collective-permute-start.69 = (bf16[512,1024]{1,0:T(8,128)(2,1)S(1)}, bf16[512,1024]{1,0:T(8,128)(2,1)S(1)}, u32[]{:S(2)}, u32[]{:S(2)}) collective-permute-start(bf16[512,1024]{1,0:T(8,128)(2,1)S(1)} %collective-permute-done.65.refs_4_), channel_id=1, source_target_pairs={{0,8},{4,12},{8,0},{12,4},{16,24},{20,28},{24,16},{28,20},{1,9},{5... | collective-permute-start | bytes 3145736 | tf_op jit(solution)/shard_map/ppermute | solution.py:419
  1034.5 54.0 %collective-permute-start.72 = (bf16[256,2048]{1,0:T(8,128)(2,1)S(1)}, bf16[256,2048]{1,0:T(8,128)(2,1)S(1)}, u32[]{:S(2)}, u32[]{:S(2)}) collective-permute-start(bf16[256,2048]{1,0:T(8,128)(2,1)S(1)} %constant_dynamic-update-slice_fusion.41.refs_0_), channel_id=1, source_target_pairs={{0,16},{4,20},{8,24},{12,28},{16,0},{20,4},{24,8},{28,12},{1,17},{... | collective-permute-start | bytes 3145736 | tf_op jit(solution)/shard_map/ppermute | solution.py:419
  (240 other events, 3468.5 us)
Sparse Core Ops, SparseCore 0:
  63.4 36.5 all-gather.9
  102.1 35.9 all-gather.11
  140.3 27.4 all-gather.13
  190.6 43.6 all-gather.15
  236.3 44.6 all-gather.17
  286.8 44.7 all-gather.19
  333.2 44.6 all-gather.21
  708.7 47.9 reduce-scatter.6
  787.0 44.5 reduce-scatter.8
  861.3 43.8 reduce-scatter.12
  913.0 26.7 reduce-scatter.10
  942.5 43.1 reduce-scatter.14
  998.9 60.6 reduce-scatter.16
  1091.0 45.8 all-gather.23

commit v3 on v2

--- a/solution.py
+++ b/solution.py
@@ -15,6 +15,8 @@
 FREE = pl.CostEstimate(flops=0, bytes_accessed=0, transcendentals=0)
 
 (
+    ROWS,
+    COLUMNS,
     QKV_Z,
     OUT_Z,
     UP_Z,
@@ -30,21 +32,22 @@
     OUT_SWAPPED,
     SEND,
     BACK,
+    OWN,
+    THEIRS,
     UP,
-    THEIRS,
     ATTENDED,
+    NEAR,
     HIDDEN,
     VALUE,
     SLOPE,
     DOWN,
-    PARTIAL,
     COTANGENT,
     COT,
     NORMAL2,
-    DDOWN,
     RESULT,
     LAYER,
     DBEFORE,
+    DDOWN,
     SHARE,
     RECEIVED,
     PART,
@@ -57,9 +60,10 @@
     WHOLE,
     VECTOR,
     DATTN_OTHER,
-    OWN,
     GRAD,
-) = range(44)
+    DOWN_GRAD,
+    UP_GRAD,
+) = range(48)
 
 
 def mm(left, right):
@@ -104,18 +108,20 @@
     return u * half, slope
 
 
-def dot(kind, pairs, finish, outs, columns=(), tiles=(), left=(0, 1), right=(0, 1), strip=256):
+def dot(
+    kind, pairs, finish, outs, columns=(), tiles=(), left=(0, 1), right=(0, 1), rows=(0, 1), split=None
+):
     count = len(pairs)
     xs, ws = [x for x, _ in pairs], [w for _, w in pairs]
     flip = kind == "tn"
-    m = xs[0].shape[1] // left[1] if flip else xs[0].shape[0]
+    m = xs[0].shape[1] // left[1] if flip else xs[0].shape[0] // rows[1]
     n = ws[0].shape[0] if kind == "nt" else ws[0].shape[1] // right[1]
     depths = [x.shape[0] if flip else x.shape[1] for x in xs]
     by_rows = flip and m > n
     size = m if by_rows else n
     step = next((s for s in (512, 384, 256) if size % s == 0), size)
     m_block, n_block = (step, n) if by_rows else (m, step)
-    strip = strip if m_block % strip == 0 else m_block
+    strip = next((s for s in (256, 128, 64) if (m_block // 2) % s == 0), m_block // 2)
     inputs = 2 * count + len(columns) + len(tiles)
 
     def kernel(*refs):
@@ -142,25 +148,34 @@
                 product = mm_t(x[some, :], w[...]) if kind == "nt" else mm(x[some, :], w[...])
                 total = total + product
             extra = [c[...] for c in column_refs] + [t[some, :] for t in tile_refs]
-            for ref, value in zip(out_refs, finish(total, *extra), strict=True):
+            values = finish(total, *extra)
+            if split == ROWS:
+                to = at * 2 // m_block
+                at = at - to * (m_block // 2)
+                out_refs[to][at : at + strip, :] = values[0].astype(out_refs[to].dtype)
+                continue
+            if split == COLUMNS:
+                values = values[0][:, : n_block // 2], values[0][:, n_block // 2 :]
+            for ref, value in zip(out_refs, values, strict=True):
                 ref[some, :] = value.astype(ref.dtype)
 
+    m_out, n_out = m // 2 if split == ROWS else m, n // 2 if split == COLUMNS else n
     if by_rows:
         per = left[0] * (m // step)
         x_specs = [pl.BlockSpec((k, step), lambda j: (0, per + j)) for k in depths]
         w_specs = [pl.BlockSpec((k, n), lambda j: (0, right[0])) for k in depths]
-        out_spec = pl.BlockSpec((step, n), lambda j: (j, 0))
+        out_spec = pl.BlockSpec((step, n_out), lambda j: (j, 0))
     else:
         per = right[0] * (n // step)
         if flip:
             x_specs = [pl.BlockSpec((k, m), lambda j: (0, left[0])) for k in depths]
         else:
-            x_specs = [pl.BlockSpec((m, k), lambda j: (0, 0)) for k in depths]
+            x_specs = [pl.BlockSpec((m, k), lambda j: (rows[0], 0)) for k in depths]
         if kind == "nt":
             w_specs = [pl.BlockSpec((step, k), lambda j: (j, 0)) for k in depths]
         else:
             w_specs = [pl.BlockSpec((k, step), lambda j: (0, per + j)) for k in depths]
-        out_spec = pl.BlockSpec((m, step), lambda j: (0, j))
+        out_spec = pl.BlockSpec((m_out, step), lambda j: (0, j))
     results = pl.pallas_call(
         kernel,
         grid=(size // step,),
@@ -169,7 +184,7 @@
         + [pl.BlockSpec((1, step), lambda j: (0, j))] * len(columns)
         + [out_spec] * len(tiles),
         out_specs=[out_spec] * len(outs),
-        out_shape=[jax.ShapeDtypeStruct((m, n), t) for t in outs],
+        out_shape=[jax.ShapeDtypeStruct((m_out, n_out), t) for t in outs],
         scratch_shapes=[pltpu.VMEM((m_block, k), BF) for k in depths] if flip else [],
         compiler_params=pltpu.CompilerParams(vmem_limit_bytes=VMEM_LIMIT),
         cost_estimate=FREE,
@@ -601,20 +616,19 @@
         project_step(name, m)
         attend_only(name, m)
 
-    def out_step(name, kind):
-        context = jnp.concatenate([v[CONTEXT, name, m] for m in range(copies)], axis=1)
-        v[CONTEXT, name] = context
-        return dot("nn", [(context, out_full)], plain, [kind])
+    def out_step(name, first):
+        at = (0, 1) if held == 2 else (int(name == OTHER), 2)
+        pairs = [
+            (v[CONTEXT, name if held == 2 else BOTH, m], out_full[m * span : (m + 1) * span])
+            for m in range(copies)
+        ]
+        return dot("nn", pairs, plain, [first, BF], rows=at, split=ROWS)
 
     def add(x, received):
         total = x.astype(F32)
         for y in received:
             total = total + y.astype(F32)
         return total.astype(BF)
-
-    def first_hop(partial):
-        n = partial.shape[0] // 2
-        v[KEPT], v[AWAY] = partial[:n], partial[n:]
 
     def next_hop():
         return add(v[KEPT], [v[AWAY]])
@@ -648,7 +662,7 @@
     ]
     out_full = jnp.concatenate(out_rows, axis=0)
     if held == 2:
-        first_hop(out_step(OTHER, BF))
+        v[KEPT], v[AWAY] = out_step(OTHER, BF)
         order(KEPT, AWAY, MINE)
         v[AWAY] = swap(v[AWAY], 1)
         project_step(MINE, 1)
@@ -660,18 +674,17 @@
             if m > 1:
                 project_step(MINE, m)
             attend_only(MINE, m)
-        partial = out_step(MINE, F32)
+        v[OWN], v[THEIRS] = out_step(MINE, F32)
     else:
         order((CONTEXT, BOTH, 0), (UP_Z, 0))
-        partial = out_step(BOTH, F32)
-        first_hop(partial[2 * rows :].astype(BF))
+        v[KEPT], v[AWAY] = out_step(OTHER, BF)
         v[AWAY] = swap(v[AWAY], 1)
         v[BACK] = swap(next_hop(), 2)
-        partial = partial[: 2 * rows]
+        v[OWN], v[THEIRS] = out_step(MINE, F32)
     for m in range(1, copies):
         v[UP, 0, m] = swap(v[UP_Z, 0], TEAM * m)
-    v[THEIRS] = partial[rows:].astype(BF)
     order(
+        OWN,
         THEIRS,
         BACK,
         *[(UP_Z, h) for h in range(1, halves)],
@@ -680,23 +693,17 @@
     for h in range(1, halves):
         for m in range(1, copies):
             v[UP, h, m] = swap(v[UP_Z, h], TEAM * m)
-    v[ATTENDED] = partial[:rows] + swap(v[THEIRS], 1).astype(F32)
+    v[ATTENDED] = v[OWN] + swap(v[THEIRS], 1).astype(F32)
     summed1 = own_tokens.astype(F32) + v[ATTENDED] + v[BACK].astype(F32) + bias_out
     normal1, scale1 = normalise(summed1)
     normed1 = normal1 * gain_one + shift_one
 
-    def first_swaps(own):
-        return [swap(own[:half], 2), swap(own[half:], 2)], swap(own, 1)
-
-    def chunk_of(far_rows):
-        return jnp.concatenate([far_rows, swap(far_rows, 1)], axis=0)
-
-    def chunk_sum(sums):
-        mine, theirs, backs = sums
-        return mine + theirs.astype(F32) + jnp.concatenate(backs, axis=0).astype(F32)
-
-    v[HIDDEN, 0] = normed1.astype(BF)
-    (v[FAR, 0], v[FAR, 1]), v[HIDDEN, 1] = first_swaps(v[HIDDEN, 0])
+    def team_chunk(name):
+        return jnp.concatenate([v[name], swap(v[name], 1)], axis=0)
+
+    v[NEAR] = normed1.astype(BF)
+    v[FAR] = swap(v[NEAR], 2)
+    v[HIDDEN, 0] = team_chunk(NEAR)
     up_parts = {0: jnp.concatenate([v[UP_Z, h] for h in range(halves)], axis=1)}
 
     def up_step(i, m):
@@ -710,77 +717,56 @@
 
     up_step(0, 0)
     order(
-        (HIDDEN, 1),
         (VALUE, 0, 0),
+        FAR,
+        (DOWN_Z, 0),
         *[(UP, h, m) for h in range(1, halves) for m in range(1, copies)],
     )
-    up_step(1, 0)
-    order((FAR, 0), (VALUE, 1, 0), (DOWN_Z, 0))
     for m in range(1, copies):
         v[DOWN, 0, m] = swap(v[DOWN_Z, 0], TEAM * m)
-    v[HIDDEN, 2] = chunk_of(v[FAR, 0])
-    up_step(2, 0)
-    order((FAR, 1), (VALUE, 2, 0))
-    v[HIDDEN, 3] = chunk_of(v[FAR, 1])
-    up_step(3, 0)
+    v[HIDDEN, 1] = team_chunk(FAR)
+    up_step(1, 0)
     for m in range(1, copies):
         up_parts[m] = jnp.concatenate([v[UP, h, m] for h in range(halves)], axis=1)
-        for i in (2, 3, 0, 1):
+        for i in (1, 0):
             up_step(i, m)
-            if m == 1 and i == 3:
-                order(
-                    (VALUE, 3, 1),
-                    (VALUE, 2, 1),
-                    (HIDDEN, 0),
-                    (HIDDEN, 1),
-                    *[(DOWN_Z, h) for h in range(1, halves)],
-                    *[(DOWN, 0, n) for n in range(1, copies)],
-                )
-                for h in range(1, halves):
-                    for n in range(1, copies):
-                        v[DOWN, h, n] = swap(v[DOWN_Z, h], TEAM * n)
     order(
         *[(VALUE, i, m) for i in range(2) for m in range(copies)],
-        *[(DOWN, h, m) for h in range(1, halves) for m in range(1, copies)],
+        *[(DOWN_Z, h) for h in range(1, halves)],
+        *[(DOWN, 0, n) for n in range(1, copies)],
     )
+    for h in range(1, halves):
+        for n in range(1, copies):
+            v[DOWN, h, n] = swap(v[DOWN_Z, h], TEAM * n)
     down_parts = {0: jnp.concatenate([v[DOWN_Z, h] for h in range(halves)], axis=0)}
     for m in range(1, copies):
         down_parts[m] = jnp.concatenate([v[DOWN, h, m] for h in range(halves)], axis=0)
 
-    def down_step(i):
+    def down_step(i, kinds, **which):
         pairs = [(v[VALUE, i, m], down_parts[m]) for m in range(copies)]
-        v[PARTIAL, i] = dot("nn", pairs, plain, [F32 if i == 0 else BF])
-
-    def hop_start(i):
-        first_hop(v[PARTIAL, i])
-        order(KEPT, AWAY)
-        v[AWAY] = swap(v[AWAY], 1)
-
-    def hop_end(i, *beside):
-        order(KEPT, AWAY, *beside)
-        v[SEND, i] = next_hop()
-        order((SEND, i), *beside)
-        v[BACK, i] = swap(v[SEND, i], 2)
-
-    down_step(2)
-    hop_start(2)
-    down_step(3)
-    hop_end(2, (PARTIAL, 3))
-    hop_start(3)
-    down_step(1)
-    hop_end(3, (PARTIAL, 1))
-    order((PARTIAL, 1), (VALUE, 0, 0), (BACK, 2))
-    v[THEIRS] = swap(v[PARTIAL, 1], 1)
-    down_step(0)
-    order((PARTIAL, 0), THEIRS, (BACK, 2), (BACK, 3))
-    theirs = v[THEIRS]
-    backs = [v[BACK, 2], v[BACK, 3]]
-    summed2 = normed1 + chunk_sum((v[PARTIAL, 0], theirs, backs)) + bias_down
+        return dot("nn", pairs, plain, kinds, **which)
+
+    v[KEPT], v[AWAY] = down_step(1, [BF, BF], split=ROWS)
+    order(KEPT, AWAY, (VALUE, 0, 0))
+    v[AWAY] = swap(v[AWAY], 1)
+    v[THEIRS] = down_step(0, [BF], rows=(1, 2))
+    order(KEPT, AWAY, THEIRS, (VALUE, 0, 0))
+    v[SEND] = next_hop()
+    order(SEND, THEIRS, (VALUE, 0, 0))
+    v[BACK] = swap(v[SEND], 2)
+    v[THEIRS] = swap(v[THEIRS], 1)
+    v[OWN] = down_step(0, [F32], rows=(0, 2))
+    order(OWN, THEIRS, BACK)
+
+    def team_sum():
+        return v[OWN] + v[THEIRS].astype(F32) + v[BACK].astype(F32)
+
+    summed2 = normed1 + team_sum() + bias_down
     normal2, scale2 = normalise(summed2)
     result = (valid * (normal2 * gain_two + shift_two)).astype(BF)
 
     v[COTANGENT] = cotangent
-    order(COTANGENT, (VALUE, 3, 0))
+    order(COTANGENT, (VALUE, 0, 0))
     v[COT, 0], v[COT, 1] = to_team(v[COTANGENT])
     v[NORMAL2] = normal2
     order(NORMAL2, (COT, 0), (COT, 1))
@@ -789,10 +775,10 @@
     dsum2 = norm_backward(grad_out, gain_two, normal2, scale2)
     gain_two_grad = jnp.sum(grad_out * normal2, axis=0)
     shift_two_grad = jnp.sum(grad_out, axis=0)
-    v[DDOWN, 0] = dsum2.astype(BF)
-    down_bias_grad = jnp.sum(v[DDOWN, 0].astype(F32), axis=0)
+    v[NEAR] = dsum2.astype(BF)
+    down_bias_grad = jnp.sum(v[NEAR].astype(F32), axis=0)
     v[RESULT] = result
-    order(RESULT, (DDOWN, 0))
+    order(RESULT, NEAR)
     v[LAYER, 0], v[LAYER, 1] = leave_team(v[RESULT][:block], v[RESULT][block:])
 
     def over_copies(shares):
@@ -813,7 +799,7 @@
 
     sub = parts * half_unit
 
-    def backward_step(i):
+    def backward_step(i, first):
         for m in range(copies):
             v[DBEFORE, i, m] = dot(
                 "nt",
@@ -823,15 +809,25 @@
                 tiles=[v[SLOPE, i, m]],
             )
         pairs = [(v[DBEFORE, i, m], up_parts[m]) for m in range(copies)]
-        v[PARTIAL, i] = dot("nt", pairs, plain, [F32 if i == 0 else BF])
-
-    def down_grad_step(m, h):
-        pairs = [(v[VALUE, i, m], v[DDOWN, i]) for i in range(4)]
-        v[DOWN, SHARE, h, m] = dot("tn", pairs, plain, [BF], left=(h, halves))
-
-    def up_grad_step(m, h):
-        pairs = [(v[HIDDEN, i], v[DBEFORE, i, m]) for i in range(4)]
-        v[UP, SHARE, h, m] = dot("tn", pairs, plain, [BF], right=(h, halves))
+        return dot("nt", pairs, plain, [first, BF], split=ROWS)
+
+    def down_grad_step(m, *those):
+        pairs = [(v[VALUE, i, m], v[DDOWN, i]) for i in range(2)]
+        if len(those) == 2:
+            both = dot("tn", pairs, plain, [BF, BF], split=ROWS)
+        else:
+            both = [dot("tn", pairs, plain, [BF], left=(h, halves)) for h in those]
+        for h, share in zip(those, both, strict=True):
+            v[DOWN, SHARE, h, m] = share
+
+    def up_grad_step(m, *those):
+        pairs = [(v[HIDDEN, i], v[DBEFORE, i, m]) for i in range(2)]
+        if len(those) == 2:
+            both = dot("tn", pairs, plain, [BF, BF], split=COLUMNS)
+        else:
+            both = [dot("tn", pairs, plain, [BF], right=(h, halves)) for h in those]
+        for h, share in zip(those, both, strict=True):
+            v[UP, SHARE, h, m] = share
 
     def swap_share(kind, h):
         for m in range(1, copies):
@@ -849,43 +845,31 @@
 
     more = range(1, copies)
     late = range(1, halves)
-    far, v[DDOWN, 1] = first_swaps(v[DDOWN, 0])
-    v[FAR, 0], v[FAR, 1] = far
-    backward_step(0)
-    order((DDOWN, 1), (PARTIAL, 0))
-    backward_step(1)
-    order((PARTIAL, 1), (FAR, 0), (FAR, 1))
-    v[THEIRS] = swap(v[PARTIAL, 1], 1)
-    for i in (2, 3):
-        v[DDOWN, i] = chunk_of(v[FAR, i - 2])
-    for h in range(halves):
-        for m in more:
-            down_grad_step(m, h)
-    order(*shares(DOWN, *range(halves)), (DDOWN, 2))
+    v[FAR] = swap(v[NEAR], 2)
+    v[DDOWN, 0] = team_chunk(NEAR)
+    v[OWN], v[THEIRS] = backward_step(0, F32)
+    order(THEIRS, FAR, (VALUE, 0, 0))
+    v[THEIRS] = swap(v[THEIRS], 1)
+    v[DDOWN, 1] = team_chunk(FAR)
+    for m in more:
+        down_grad_step(m, *range(halves))
+    order(*shares(DOWN, *range(halves)), (DDOWN, 1))
     for h in range(halves):
         swap_share(DOWN, h)
-    backward_step(2)
-    hop_start(2)
-    order((PARTIAL, 2), (DDOWN, 3))
-    backward_step(3)
-    hop_end(2, (PARTIAL, 3), (DDOWN, 0))
-    hop_start(3)
-    order((PARTIAL, 3), (DDOWN, 0))
+    v[KEPT], v[AWAY] = backward_step(1, BF)
+    order(KEPT, AWAY, (DDOWN, 0))
+    v[AWAY] = swap(v[AWAY], 1)
     down_grad_step(0, 0)
-    hop_end(3, (DOWN, SHARE, 0, 0), (DDOWN, 0), (LAYER, 0), (LAYER, 1))
+    order(KEPT, AWAY, (DOWN, SHARE, 0, 0), (DDOWN, 0))
+    v[SEND] = next_hop()
+    order(SEND, (DOWN, SHARE, 0, 0), (DDOWN, 0))
+    v[BACK] = swap(v[SEND], 2)
     for h in late:
         down_grad_step(0, h)
-    order(*[(DOWN, SHARE, h, 0) for h in range(halves)], *received(DOWN, 0), (BACK, 2))
+    order(*[(DOWN, SHARE, h, 0) for h in range(halves)], *received(DOWN, 0))
     reduce_step(DOWN, 0)
-    order(
-        (PARTIAL, 0),
-        (BACK, 2),
-        (BACK, 3),
-        THEIRS,
-        *[(DOWN, SHARE, h, 0) for h in late],
-    )
-    backs = [v[BACK, 2], v[BACK, 3]]
-    dnormed1 = dsum2 + chunk_sum((v[PARTIAL, 0], v[THEIRS], backs))
+    order(OWN, BACK, THEIRS, *[(DOWN, SHARE, h, 0) for h in late])
+    dnormed1 = dsum2 + team_sum()
     dsum1 = norm_backward(dnormed1, gain_one, normal1, scale1)
     gain_one_grad = jnp.sum(dnormed1 * normal1, axis=0)
     shift_one_grad = jnp.sum(dnormed1, axis=0)
@@ -895,9 +879,8 @@
     order((HIDDEN, 0), DATTN)
     v[DATTN_NEAR] = swap(v[DATTN], 1)
     v[DATTN_FAR] = swap(v[DATTN], 2)
-    for h in range(halves):
-        for m in more:
-            up_grad_step(m, h)
+    for m in more:
+        up_grad_step(m, *range(halves))
     order(
         *shares(UP, *range(halves)),
         DATTN_NEAR,
@@ -925,8 +908,25 @@
         return jnp.concatenate([v[DATTN_FAR], swap(v[DATTN_FAR], 1)], axis=0)
 
     def out_grad_step():
-        pairs = [(v[CONTEXT, MINE], v[DATTN_MINE]), (v[CONTEXT, OTHER], dattn_other)]
-        share = dot("tn", pairs, plain, [BF])
+        if held == 2:
+            share = jnp.concatenate(
+                [
+                    dot(
+                        "tn",
+                        [
+                            (v[CONTEXT, MINE, m], v[DATTN_MINE]),
+                            (v[CONTEXT, OTHER, m], dattn_other),
+                        ],
+                        plain,
+                        [BF],
+                    )
+                    for m in range(copies)
+                ],
+                axis=0,
+            )
+        else:
+            pairs = [[(v[CONTEXT, BOTH, m], dattn_both)] for m in range(copies)]
+            share = jnp.concatenate([dot("tn", p, plain, [BF]) for p in pairs], axis=0)
         for m in range(copies):
             rows_of = [
                 lax.dynamic_slice(share, ((d ^ e) * span, (d ^ m) * wide), (span, wide))
@@ -964,7 +964,7 @@
 
         up_sums = jnp.zeros((parts, reps, halves, half_unit), F32)
         for m in range(copies):
-            share = sum(jnp.sum(v[DBEFORE, i, m].astype(F32), axis=0) for i in range(4))
+            share = sum(jnp.sum(v[DBEFORE, i, m].astype(F32), axis=0) for i in range(2))
             share = share.reshape(halves, parts, half_unit).transpose(1, 0, 2)[:, None]
             up_sums = lax.dynamic_update_slice(up_sums, share, (0, rep ^ (TEAM * m), 0, 0))
         vector_sums = [
@@ -1004,6 +1004,7 @@
         order(
             DATTN_FAR,
             *[(DQKV, MINE, m) for m in range(copies)],
+            *received(UP, 0),
         )
         v[DATTN_OTHER] = far_rows()
         dattn_other = v[DATTN_OTHER]
@@ -1011,7 +1012,7 @@
         order(*[(OUT, SHARE, 0, m) for m in range(copies)], DATTN_OTHER, (HIDDEN, 0))
         swap_share(OUT, 0)
         up_grad_step(0, 0)
-        order(DATTN_OTHER, *received(UP, 0), (UP, SHARE, 0, 0))
+        order(DATTN_OTHER, (UP, SHARE, 0, 0))
         reduce_step(UP, 0)
         dattn_other = v[DATTN_OTHER]
         dcontext = context_grad(dattn_other)
@@ -1026,8 +1027,6 @@
             back_step(BOTH, dcontext, m)
         up_grad_step(0, 0)
         reduce_step(UP, 0)
-        v[CONTEXT, MINE] = v[CONTEXT, BOTH][: 2 * rows]
-        v[CONTEXT, OTHER] = v[CONTEXT, BOTH][2 * rows :]
         out_grad_step()
         swap_share(OUT, 0)
         for m in range(copies):
@@ -1036,7 +1035,13 @@
     order(
         *[(DQKV, OTHER, m) for m in range(copies)],
         *[(DOWN, PART, h) for h in range(halves)],
+        *received(OUT, 0),
+        (OUT, SHARE, 0, 0),
+        *received(UP, *late),
+        (LAYER, 0),
+        (LAYER, 1),
     )
+    out_reduce_step()
     vector_start()
     v[DOWN, WHOLE, 0] = jnp.concatenate([v[DOWN, PART, h] for h in range(halves)], axis=0)
     to_more(DOWN, near_far[0])
@@ -1045,13 +1050,20 @@
         pairs = [(tokens_mine, v[DQKV, MINE, m]), (tokens_other, v[DQKV, OTHER, m])]
         v[QKV, SHARE, 0, m] = dot("tn", pairs, plain, [BF])
 
-    def dtokens_partial(name, kind):
+    def dtokens_partial(name, first):
         pairs = [(v[DQKV, name, m], qkv_weight[m]) for m in range(copies)]
-        return dot("nt", pairs, plain, [kind])
+        return dot("nt", pairs, plain, [first, BF], split=ROWS)
 
     for m in more:
         qkv_grad_step(m)
-    first_hop(dtokens_partial(OTHER, BF))
+    order(
+        *shares(QKV, 0),
+        *[(DQKV, name, m) for name in (MINE, OTHER) for m in range(copies)],
+        (HIDDEN, 0),
+        *all_of(DOWN),
+    )
+    swap_share(QKV, 0)
+    v[KEPT], v[AWAY] = dtokens_partial(OTHER, BF)
     order(
         KEPT,
         AWAY,
@@ -1061,70 +1073,63 @@
     )
     v[AWAY] = swap(v[AWAY], 1)
     vector_step(1)
-    qkv_grad_step(0)
+    order(KEPT, AWAY, *[(DQKV, MINE, m) for m in range(copies)], (HIDDEN, 0))
+    v[SEND] = next_hop()
+    v[BACK] = swap(v[SEND], 2)
     for h in late:
         up_grad_step(0, h)
-    order(
-        *shares(QKV, 0),
-        (QKV, SHARE, 0, 0),
-        KEPT,
-        AWAY,
-        *received(OUT, 0),
-        (OUT, SHARE, 0, 0),
-        *received(UP, *late),
-        *[(UP, SHARE, h, 0) for h in late],
-        *[(DQKV, MINE, m) for m in range(copies)],
-    )
-    swap_share(QKV, 0)
-    v[SEND] = next_hop()
-    v[BACK] = swap(v[SEND], 2)
-    out_reduce_step()
-    for h in late:
         reduce_step(UP, h)
-    partial = dtokens_partial(MINE, F32)
-    v[THEIRS] = partial[rows:].astype(BF)
+    qkv_grad_step(0)
+    v[OWN], v[THEIRS] = dtokens_partial(MINE, F32)
     order(
         THEIRS,
         BACK,
         (QKV, SHARE, 0, 0),
         *received(QKV, 0),
         *all_of(DOWN),
-        (OUT, PART, 0),
         *[(UP, PART, h) for h in range(halves)],
         (VECTOR, 0),
+        (OUT, PART, 0),
     )
     reduce_step(QKV, 0)
     v[THEIRS] = swap(v[THEIRS], 1)
-    v[OUT, WHOLE, 0] = v[OUT, PART, 0]
     v[UP, WHOLE, 0] = jnp.concatenate([v[UP, PART, h] for h in range(halves)], axis=1)
     far_near = near_far[1:] + near_far[:1]
     to_more(UP, far_near[0])
+    v[OUT, WHOLE, 0] = v[OUT, PART, 0]
     to_more(OUT, far_near[0])
-    order(THEIRS, BACK, *all_of(UP), *all_of(OUT), *all_of(DOWN))
+    order(OWN, THEIRS, BACK, *all_of(UP), *all_of(DOWN), *all_of(OUT))
     for i, mask in enumerate(far_near[1:]):
         to_more(UP, mask)
-        to_more(OUT, mask)
         to_more(DOWN, near_far[1 + i])
-    vector_step(2)
-    dtokens = dsum1 + partial[:rows] + v[THEIRS].astype(F32) + v[BACK].astype(F32)
-    v[OWN] = dtokens.astype(BF)
-    order(
-        (QKV, PART, 0),
-        OWN,
-        (VECTOR, 0),
-        *all_of(UP),
-        *all_of(OUT),
-        *all_of(DOWN),
-    )
+    v[OWN] = (dsum1 + team_sum()).astype(BF)
+    order((QKV, PART, 0), OWN, (VECTOR, 0), *all_of(UP), *all_of(DOWN))
     qkv_part = lax.all_gather(v[QKV, PART, 0], "rep", axis=0, tiled=False)
     v[GRAD, 0], v[GRAD, 1] = leave_team(v[OWN][:block], v[OWN][block:])
     to_more(UP, 1)
     to_more(DOWN, 1)
+    for mask in far_near[1:]:
+        to_more(OUT, mask)
+    vector_step(2)
+    layer_out = settle(v[LAYER, 0], v[LAYER, 1])
+    order(*all_of(UP), *all_of(DOWN))
+    places = [rep ^ m for m in range(reps)]
+    aligned = half_unit % LANES == 0 and head_dim % LANES == 0
+    if aligned:
+        v[DOWN_GRAD] = place_rows(
+            [v[DOWN, WHOLE, m] for m in range(reps)], places, (hidden // parts, width)
+        )
+        v[UP_GRAD] = place_columns(
+            [v[UP, WHOLE, m] for m in range(reps)],
+            places,
+            (shard, hidden),
+            half_unit,
+            lambda i, r: ((i % parts) * reps + r) * halves + i // parts,
+        )
+        order(DOWN_GRAD, UP_GRAD, *all_of(OUT), (VECTOR, 0))
     to_more(OUT, 1)
     for mask in near_far[1:]:
         vector_step(mask)
-    order(*all_of(UP), *all_of(OUT), *all_of(DOWN), (VECTOR, 0))
-    layer_out = settle(v[LAYER, 0], v[LAYER, 1])
     tokens_grad = settle(v[GRAD, 0], v[GRAD, 1]).astype(F32)
     out_grad = in_order({m: v[OUT, WHOLE, m] for m in range(reps)})
 
@@ -1137,19 +1142,8 @@
         out_grad = pick(out_grad, z % fill, 1).transpose(1, 2, 0, 3)
     out_grad = out_grad.reshape(-1, width).astype(F32)
 
-    aligned = half_unit % LANES == 0 and head_dim % LANES == 0
     if aligned:
-        places = [rep ^ m for m in range(reps)]
-        down_grad = place_rows(
-            [v[DOWN, WHOLE, m] for m in range(reps)], places, (hidden // parts, width)
-        )
-        up_grad = place_columns(
-            [v[UP, WHOLE, m] for m in range(reps)],
-            places,
-            (shard, hidden),
-            half_unit,
-            lambda i, r: ((i % parts) * reps + r) * halves + i // parts,
-        )
+        down_grad, up_grad = v[DOWN_GRAD], v[UP_GRAD]
         qkv_grads = place_heads_grad(qkv_part, reps, run, head_dim)
     else:
         def in_order_of(kind):

time: 1190 us -> 1160 us (0.975)
  Pallas kernels: 406 us -> 381 us
    ppermute x2, waiting for transfers between devices: 26.6 us -> 0.01 us  [leave_team(): second = lax.ppermute(second, axes, [(b, a) for a, b in odd])]
    pallas_call x45 -> x33, Pallas kernels: 309 us -> 285 us  [dot(): pl.pallas_call(kernel, grid=(size // step,), in_specs=x_specs + w_specs +...]
    slice x10 -> x0, local copies, waits for them, and re-layouts: 23.3 us -> none  [the longest x6 12.1 us: first_hop(): v[KEPT], v[AWAY] = (partial[:n], partial[n:])]
    all_gather x7, waiting for transfers between devices: 36.2 us -> 53.3 us  [over_z(): return lax.all_gather(x, 'fsdp', axis=0, tiled=True)]
    unnamed x380 -> x309, local copies, waits for them, and re-layouts: 79.6 us -> 95.7 us
    ppermute x75 -> x67, waiting for transfers between devices: 344 us -> 360 us  [swap(): return lax.ppermute(x, 'rep', [(i, i ^ mask) for i in range(reps)])]
    ppermute x75 -> x67, starting transfers between devices: 53.9 us -> 51.5 us  [swap(): return lax.ppermute(x, 'rep', [(i, i ^ mask) for i in range(reps)])]
    convert_element_type x12 -> x10, other arithmetic: 37.3 us -> 35.2 us  [add(): return total.astype(BF)]
  transfers between devices with their start and end apart: 103 -> 95, of which waited for: 37 -> 38; matrix products, arithmetic and copies ran while one was open for 15% -> 14% of each run, Pallas kernels for 30% -> 28%
where the time goes in v3:
time: 1160 us; the launch traced here: 1150 us
  waiting for transfers between devices  428 us (37%)
  Pallas kernels  381 us (33%)
  local copies, waits for them, and re-layouts  136 us (12%)
  other arithmetic  109 us (9%)
  starting transfers between devices  79.4 us (7%)
  between operations  16.4 us (1%)
    ppermute x67, waiting for transfers between devices, swap(): return lax.ppermute(x, 'rep', [(i, i ^ mask) for i in range(reps)])  360 us
    pallas_call x33, Pallas kernels, dot(): pl.pallas_call(kernel, grid=(size // step,), in_specs=x_specs + w_specs +...  285 us
    unnamed x309, local copies, waits for them, and re-layouts  95.7 us
    all_gather x7, waiting for transfers between devices, over_z(): return lax.all_gather(x, 'fsdp', axis=0, tiled=True)  53.3 us
    ppermute x67, starting transfers between devices, swap(): return lax.ppermute(x, 'rep', [(i, i ^ mask) for i in range(reps)])  51.5 us
    convert_element_type x10, other arithmetic, add(): return total.astype(BF)  35.2 us
    pallas_call x4, Pallas kernels, attend_backward(): pl.pallas_call(kernel, grid=(heads,), in_specs=[pl.BlockSpec((rows, 3 * h...  34.4 us
  transfers between devices with their start and end apart: 95, of which 38 were waited for; matrix products, arithmetic and copies ran while one was open for 14% of the time, Pallas kernels for 28%

profile of v3, /device:TPU:18, one launch (start us, length us, event | category | flops | bytes accessed | tf_op | source)
XLA Modules:
  0.0 1150.3 jit_solution(15939546114361653347)
XLA Ops:
  66.1 24.1 %collective-permute-done.8 = bf16[256,2048]{1,0:T(8,128)(2,1)S(1)} collective-permute-done((bf16[256,2048]{1,0:T(8,128)(2,1)}, bf16[256,2048]{1,0:T(8,128)(2,1)S(1)}, u32[]{:S(2)}, u32[]{:S(2)}) %collective-permute-start.8) | collective-permute-done | bytes 1048608 | tf_op jit(solution)/shard_map/ppermute | solution.py:434
  90.2 21.9 %collective-permute-done.9 = bf16[256,2048]{1,0:T(8,128)(2,1)} collective-permute-done((bf16[256,2048]{1,0:T(8,128)(2,1)}, bf16[256,2048]{1,0:T(8,128)(2,1)}, u32[]{:S(2)}, u32[]{:S(2)}) %collective-permute-start.9) | collective-permute-done | bytes 1048608 | tf_op jit(solution)/shard_map/ppermute | solution.py:434
  123.3 14.6 %all-gather.12.cloned.1.call-done = bf16[2048,384]{1,0:T(8,128)(2,1)} async-done(((bf16[512,384]{1,0:T(8,128)(2,1)}), bf16[2048,384]{1,0:T(8,128)(2,1)}) %all-gather.12.cloned.1.call-update) | async-done | bytes 1572880 | tf_op jit(solution)/shard_map/all_gather | solution.py:528
  177.0 11.6 %collective-permute-done.15 = bf16[2048,384]{1,0:T(8,128)(2,1)} collective-permute-done((bf16[2048,384]{1,0:T(8,128)(2,1)}, bf16[2048,384]{1,0:T(8,128)(2,1)}, u32[]{:S(2)}, u32[]{:S(2)}) %collective-permute-start.15) | collective-permute-done | bytes 1572896 | tf_op jit(solution)/shard_map/ppermute | solution.py:434
  251.4 29.3 %all-gather.18.cloned.1.call-done = bf16[2048,512]{1,0:T(8,128)(2,1)} async-done(((bf16[512,512]{1,0:T(8,128)(2,1)}), bf16[2048,512]{1,0:T(8,128)(2,1)}) %all-gather.18.cloned.1.call-update) | async-done | bytes 2097168 | tf_op jit(solution)/shard_map/all_gather | solution.py:528
  307.8 10.3 shard_map.319
  328.9 15.2 %collective-permute-done.23 = bf16[2048,512]{1,0:T(8,128)(2,1)} collective-permute-done((bf16[2048,512]{1,0:T(8,128)(2,1)}, bf16[2048,512]{1,0:T(8,128)(2,1)}, u32[]{:S(2)}, u32[]{:S(2)}) %collective-permute-start.23) | collective-permute-done | bytes 2097184 | tf_op jit(solution)/shard_map/ppermute | solution.py:434
  351.8 10.2 shard_map.320
  381.8 10.6 shard_map.322
  402.0 41.0 %collective-permute-done.26 = bf16[512,2048]{1,0:T(8,128)(2,1)S(1)} collective-permute-done((bf16[512,2048]{1,0:T(8,128)(2,1)}, bf16[512,2048]{1,0:T(8,128)(2,1)S(1)}, u32[]{:S(2)}, u32[]{:S(2)}) %collective-permute-start.26) | collective-permute-done | bytes 2097184 | tf_op jit(solution)/shard_map/ppermute | solution.py:434
  445.3 12.6 %shard_map.323 = (bf16[512,2048]{1,0:T(8,128)(2,1)S(1)}, bf16[512,2048]{1,0:T(8,128)(2,1)S(1)}) custom-call(bf16[1024,1024]{1,0:T(8,128)(2,1)} %copy-done.12, bf16[1024,1024]{1,0:T(8,128)(2,1)} %copy-done.34, bf16[1024,2048]{1,0:T(8,128)(2,1)} %copy-done.94, bf16[1024,2048]{1,0:T(8,128)(2,1)} %copy-done.93), custom_call_target="tpu_custom_call" | custom-call | tf_op jit(solution)/shard_map/pallas_call | solution.py:179
  479.4 35.0 %collective-permute-done.29 = bf16[512,2048]{1,0:T(8,128)(2,1)} collective-permute-done((bf16[512,2048]{1,0:T(8,128)(2,1)S(1)}, bf16[512,2048]{1,0:T(8,128)(2,1)}, u32[]{:S(2)}, u32[]{:S(2)}) %collective-permute-start.29) | collective-permute-done | bytes 2097184 | tf_op jit(solution)/shard_map/ppermute | solution.py:434
  554.7 12.8 %shard_map.328 = (f32[512,2048]{1,0:T(8,128)}, bf16[512,2048]{1,0:T(8,128)(2,1)}) custom-call(bf16[1024,1024]{1,0:T(8,128)(2,1)S(1)} %shard_map.326.refs_0_.refs_2_, bf16[1024,1024]{1,0:T(8,128)(2,1)} %copy-done.6, bf16[2048,1024]{1,0:T(8,128)(2,1)} %copy-done.97, bf16[2048,1024]{1,0:T(8,128)(2,1)} %copy-done.96), custom_call_target="tpu_custom_call" | custom-call | tf_op jit(solution)/shard_map/pallas_call | solution.py:179
  567.5 12.0 %collective-permute-done.33 = bf16[512,2048]{1,0:T(8,128)(2,1)} collective-permute-done((bf16[512,2048]{1,0:T(8,128)(2,1)}, bf16[512,2048]{1,0:T(8,128)(2,1)}, u32[]{:S(2)}, u32[]{:S(2)}) %collective-permute-start.33) | collective-permute-done | bytes 2097184 | tf_op jit(solution)/shard_map/ppermute | solution.py:434
  586.0 14.6 %shard_map.329 = (bf16[512,2048]{1,0:T(8,128)(2,1)S(1)}, bf16[512,2048]{1,0:T(8,128)(2,1)}) custom-call(bf16[1024,1024]{1,0:T(8,128)(2,1)} %copy-done.13, bf16[1024,1024]{1,0:T(8,128)(2,1)} %copy-done.34, bf16[1024,2048]{1,0:T(8,128)(2,1)} %copy-done.92, bf16[1024,2048]{1,0:T(8,128)(2,1)} %copy-done.91), custom_call_target="tpu_custom_call" | custom-call | tf_op jit(solution)/shard_map/pallas_call | solution.py:179
  618.9 12.8 %shard_map.332 = (bf16[512,2048]{1,0:T(8,128)(2,1)S(1)}, bf16[512,2048]{1,0:T(8,128)(2,1)S(1)}) custom-call(bf16[1024,1024]{1,0:T(8,128)(2,1)} %copy-done.2, bf16[1024,1024]{1,0:T(8,128)(2,1)} %copy-done.8, bf16[2048,1024]{1,0:T(8,128)(2,1)} %copy-done.97, bf16[2048,1024]{1,0:T(8,128)(2,1)} %copy-done.96), custom_call_target="tpu_custom_call" | custom-call | tf_op jit(solution)/shard_map/pallas_call | solution.py:179
  656.5 24.3 %collective-permute-done.38 = bf16[512,2048]{1,0:T(8,128)(2,1)S(1)} collective-permute-done((bf16[512,2048]{1,0:T(8,128)(2,1)S(1)}, bf16[512,2048]{1,0:T(8,128)(2,1)S(1)}, u32[]{:S(2)}, u32[]{:S(2)}) %collective-permute-start.38) | collective-permute-done | bytes 2097184 | tf_op jit(solution)/shard_map/ppermute | solution.py:434
  683.1 10.6 collective-permute-done.36
  707.1 13.0 %shard_map.335 = (bf16[2048,512]{1,0:T(8,128)(2,1)}, bf16[2048,512]{1,0:T(8,128)(2,1)S(1)}) custom-call(bf16[1024,2048]{1,0:T(8,128)(2,1)} %pad_maximum_fusion.1.refs_0_, bf16[1024,2048]{1,0:T(8,128)(2,1)} %copy-done.95, bf16[1024,1024]{1,0:T(8,128)(2,1)} %copy-done.6, bf16[1024,1024]{1,0:T(8,128)(2,1)} %copy-done.8), custom_call_target="tpu_custom_call" | custom-call | tf_op jit(solution)/shard_map/pallas_call | solution.py:179
  860.0 10.3 shard_map.345
  933.3 42.1 %collective-permute-done.54 = bf16[2048,768]{1,0:T(8,128)(2,1)} collective-permute-done((bf16[2048,768]{1,0:T(8,128)(2,1)}, bf16[2048,768]{1,0:T(8,128)(2,1)}, u32[]{:S(2)}, u32[]{:S(2)}) %collective-permute-start.54) | collective-permute-done | bytes 3145760 | tf_op jit(solution)/shard_map/ppermute | solution.py:434
  985.3 29.0 %collective-permute-done.58 = bf16[128,1024]{1,0:T(8,128)(2,1)S(1)} collective-permute-done((bf16[128,1024]{1,0:T(8,128)(2,1)S(1)}, bf16[128,1024]{1,0:T(8,128)(2,1)S(1)}, u32[]{:S(2)}, u32[]{:S(2)}) %collective-permute-start.58) | collective-permute-done | bytes 262176 | tf_op jit(solution)/shard_map/ppermute | solution.py:434
  1026.0 15.1 %collective-permute-done.59.refs_2_ = bf16[512,1024]{1,0:T(8,128)(2,1)S(1)} collective-permute-done((bf16[512,1024]{1,0:T(8,128)(2,1)S(1)}, bf16[512,1024]{1,0:T(8,128)(2,1)S(1)}, u32[]{:S(2)}, u32[]{:S(2)}) %collective-permute-start.59) | collective-permute-done | bytes 1048608 | tf_op jit(solution)/shard_map/ppermute | solution.py:434
  1041.1 21.1 %collective-permute-done.60.refs_6_ = bf16[512,1024]{1,0:T(8,128)(2,1)S(1)} collective-permute-done((bf16[512,1024]{1,0:T(8,128)(2,1)S(1)}, bf16[512,1024]{1,0:T(8,128)(2,1)S(1)}, u32[]{:S(2)}, u32[]{:S(2)}) %collective-permute-start.60) | collective-permute-done | bytes 1048608 | tf_op jit(solution)/shard_map/ppermute | solution.py:434
  (682 shorter events, 679.9 us)
Async XLA Ops:
  7.3 104.8 %all-gather.10.cloned.1.call-start = ((), (), s32[]{:S(2)}) async-start(), calls=%async_computation.6 | async-start | bytes 1966080 | tf_op jit(solution)/shard_map/all_gather | solution.py:528
  12.4 50.7 %collective-permute-start.1 = (bf16[256,2048]{1,0:T(8,128)(2,1)}, bf16[256,2048]{1,0:T(8,128)(2,1)}, u32[]{:S(2)}, u32[]{:S(2)}) collective-permute-start(bf16[256,2048]{1,0:T(8,128)(2,1)} %get-tuple-element.545), channel_id=1, source_target_pairs={{0,1},{1,0},{2,5},{3,4},{4,3},{5,2},{6,7},{7,6},{8,9},{9,8},{10,13... | collective-permute-start | bytes 3145736 | tf_op jit(solution)/shard_map/ppermute | solution.py:464
  63.2 74.8 %all-gather.12.cloned.1.call-start = ((), (), s32[]{:S(2)}) async-start(), calls=%async_computation.7 | async-start | bytes 1966080 | tf_op jit(solution)/shard_map/all_gather | solution.py:528
  63.9 113.1 %all-gather.14.cloned.1.call-start = ((), (), s32[]{:S(2)}) async-start(), calls=%async_computation.8 | async-start | bytes 1310720 | tf_op jit(solution)/shard_map/all_gather | solution.py:528
  114.6 120.7 %all-gather.16.cloned.1.call-start = ((), (), s32[]{:S(2)}) async-start(), calls=%async_computation.9 | async-start | bytes 2621440 | tf_op jit(solution)/shard_map/all_gather | solution.py:528
  118.2 58.9 %collective-permute-start.14 = (bf16[2048,384]{1,0:T(8,128)(2,1)}, bf16[2048,384]{1,0:T(8,128)(2,1)}, u32[]{:S(2)}, u32[]{:S(2)}) collective-permute-start(bf16[2048,384]{1,0:T(8,128)(2,1)} %all-gather.10.cloned.1.call-done), channel_id=1, source_target_pairs={{0,16},{4,20},{8,24},{12,28},{16,0},{20,4},{24,8},{28,12},{1,17},{... | collective-permute-start | bytes 4718600 | tf_op jit(solution)/shard_map/ppermute | solution.py:434
  190.2 90.5 %all-gather.18.cloned.1.call-start = ((), (), s32[]{:S(2)}) async-start(), calls=%async_computation.10 | async-start | bytes 2621440 | tf_op jit(solution)/shard_map/all_gather | solution.py:528
  222.2 106.7 %all-gather.20.cloned.1.call-start = ((), (), s32[]{:S(2)}) async-start(), calls=%async_computation.11 | async-start | bytes 2621440 | tf_op jit(solution)/shard_map/all_gather | solution.py:528
  283.9 111.0 %all-gather.22.cloned.1.call-start = ((), (), s32[]{:S(2)}) async-start(), calls=%async_computation.12 | async-start | bytes 2621440 | tf_op jit(solution)/shard_map/all_gather | solution.py:528
  299.2 538.8 %reduce-scatter.7.cloned.1.call-start = ((), (), s32[]{:S(2)}) async-start(), calls=%async_computation.13 | async-start | bytes 2621440 | tf_op jit(solution)/shard_map/reduce_scatter | solution.py:791
  631.9 51.2 %collective-permute-start.37 = (bf16[512,2048]{1,0:T(8,128)(2,1)}, bf16[512,2048]{1,0:T(8,128)(2,1)}, u32[]{:S(2)}, u32[]{:S(2)}) collective-permute-start(bf16[512,2048]{1,0:T(8,128)(2,1)} %get-tuple-element.373), channel_id=1, source_target_pairs={{0,4},{4,0},{8,12},{12,8},{16,20},{20,16},{24,28},{28,24},{1,5},{5... | collective-permute-start | bytes 6291464 | tf_op jit(solution)/shard_map/ppermute | solution.py:434
  646.6 78.4 %collective-permute-start.40 = (bf16[512,2048]{1,0:T(8,128)(2,1)}, bf16[512,2048]{1,0:T(8,128)(2,1)}, u32[]{:S(2)}, u32[]{:S(2)}) collective-permute-start(bf16[512,2048]{1,0:T(8,128)(2,1)} %get-tuple-element.385), channel_id=1, source_target_pairs={{0,16},{4,20},{8,24},{12,28},{16,0},{20,4},{24,8},{28,12},{1,17},{... | collective-permute-start | bytes 6291464 | tf_op jit(solution)/shard_map/ppermute | solution.py:434
  683.1 155.0 %reduce-scatter.9.cloned.1.call-start = ((), (), s32[]{:S(2)}) async-start(), calls=%async_computation.14 | async-start | bytes 2621440 | tf_op jit(solution)/shard_map/reduce_scatter | solution.py:791
  706.6 58.2 %collective-permute-start.41 = (bf16[512,2048]{1,0:T(8,128)(2,1)}, bf16[512,2048]{1,0:T(8,128)(2,1)}, u32[]{:S(2)}, u32[]{:S(2)}) collective-permute-start(bf16[512,2048]{1,0:T(8,128)(2,1)} %get-tuple-element.381), channel_id=1, source_target_pairs={{0,8},{4,12},{8,0},{12,4},{16,24},{20,28},{24,16},{28,20},{1,9},{5... | collective-permute-start | bytes 6291464 | tf_op jit(solution)/shard_map/ppermute | solution.py:434
  734.3 198.9 %reduce-scatter.15.cloned.1.call-start = ((), (), s32[]{:S(2)}) async-start(), calls=%async_computation.17 | async-start | bytes 1310720 | tf_op jit(solution)/shard_map/reduce_scatter | solution.py:791
  772.4 65.7 %collective-permute-start.45 = (bf16[2048,512]{1,0:T(8,128)(2,1)}, bf16[2048,512]{1,0:T(8,128)(2,1)}, u32[]{:S(2)}, u32[]{:S(2)}) collective-permute-start(bf16[2048,512]{1,0:T(8,128)(2,1)} %copy-done.85), channel_id=1, source_target_pairs={{0,16},{4,20},{8,24},{12,28},{16,0},{20,4},{24,8},{28,12},{1,17},{... | collective-permute-start | bytes 6291464 | tf_op jit(solution)/shard_map/ppermute | solution.py:434
  777.2 60.8 %collective-permute-start.46 = (bf16[256,2048]{1,0:T(8,128)(2,1)}, bf16[256,2048]{1,0:T(8,128)(2,1)}, u32[]{:S(2)}, u32[]{:S(2)}) collective-permute-start(bf16[256,2048]{1,0:T(8,128)(2,1)} %get-tuple-element.534), channel_id=1, source_target_pairs={{0,0},{1,1},{4,2},{5,3},{2,4},{3,5},{6,6},{7,7},{8,8},{9,9},{12,10... | collective-permute-start | bytes 3145736 | tf_op jit(solution)/shard_map/ppermute | solution.py:471
  779.3 58.7 %collective-permute-start.47 = (bf16[256,2048]{1,0:T(8,128)(2,1)}, bf16[256,2048]{1,0:T(8,128)(2,1)}, u32[]{:S(2)}, u32[]{:S(2)}) collective-permute-start(bf16[256,2048]{1,0:T(8,128)(2,1)} %get-tuple-element.533), channel_id=1, source_target_pairs={{1,0},{0,1},{5,2},{4,3},{3,4},{2,5},{7,6},{6,7},{9,8},{8,9},{13,10... | collective-permute-start | bytes 3145736 | tf_op jit(solution)/shard_map/ppermute | solution.py:472
  846.3 87.0 %reduce-scatter.11.cloned.1.call-start = ((), (), s32[]{:S(2)}) async-start(), calls=%async_computation.15 | async-start | bytes 2621440 | tf_op jit(solution)/shard_map/reduce_scatter | solution.py:791
  850.8 124.5 %reduce-scatter.13.cloned.1.call-start = ((), (), s32[]{:S(2)}) async-start(), calls=%async_computation.16 | async-start | bytes 2621440 | tf_op jit(solution)/shard_map/reduce_scatter | solution.py:791
  904.8 159.4 %reduce-scatter.17.cloned.1.call-start = ((), (), s32[]{:S(2)}) async-start(), calls=%async_computation.18 | async-start | bytes 3932160 | tf_op jit(solution)/shard_map/reduce_scatter | solution.py:791
  904.8 70.5 %collective-permute-start.54 = (bf16[2048,768]{1,0:T(8,128)(2,1)}, bf16[2048,768]{1,0:T(8,128)(2,1)}, u32[]{:S(2)}, u32[]{:S(2)}) collective-permute-start(bf16[2048,768]{1,0:T(8,128)(2,1)} %shard_map.345), channel_id=1, source_target_pairs={{0,16},{4,20},{8,24},{12,28},{16,0},{20,4},{24,8},{28,12},{1,17},{... | collective-permute-start | bytes 9437192 | tf_op jit(solution)/shard_map/ppermute | solution.py:434
  910.8 64.6 %collective-permute-start.53 = (bf16[512,2048]{1,0:T(8,128)(2,1)}, bf16[512,2048]{1,0:T(8,128)(2,1)}, u32[]{:S(2)}, u32[]{:S(2)}) collective-permute-start(bf16[512,2048]{1,0:T(8,128)(2,1)} %add_convert_fusion.4), channel_id=1, source_target_pairs={{0,8},{4,12},{8,0},{12,4},{16,24},{20,28},{24,16},{28,20},{1,9},{5... | collective-permute-start | bytes 6291464 | tf_op jit(solution)/shard_map/ppermute | solution.py:434
  980.7 153.9 %all-gather.24.cloned.1.call-start = ((), (), s32[]{:S(2)}) async-start(), calls=%async_computation.19 | async-start | bytes 7077888 | tf_op jit(solution)/shard_map/all_gather | solution.py:1107
  (198 other events, 2792.1 us)
Sparse Core Ops, SparseCore 0:
  63.3 36.5 all-gather.9
  102.0 35.9 all-gather.11
  140.1 27.4 all-gather.13
  190.3 43.6 all-gather.15
  236.0 44.6 all-gather.17
  284.1 44.7 all-gather.19
  331.0 44.6 all-gather.21
  683.2 43.5 reduce-scatter.6
  734.5 42.4 reduce-scatter.8
  846.4 28.8 reduce-scatter.14
  878.3 43.2 reduce-scatter.10
  923.7 43.1 reduce-scatter.12
  980.8 60.1 reduce-scatter.16
  1064.3 49.1 all-gather.23

commit v4 on v3

--- a/solution.py
+++ b/solution.py
@@ -121,7 +121,7 @@
     size = m if by_rows else n
     step = next((s for s in (512, 384, 256) if size % s == 0), size)
     m_block, n_block = (step, n) if by_rows else (m, step)
-    strip = next((s for s in (256, 128, 64) if (m_block // 2) % s == 0), m_block // 2)
+    strip = next((s for s in (512, 256, 128, 64) if (m_block // 2) % s == 0), m_block // 2)
     inputs = 2 * count + len(columns) + len(tiles)
 
     def kernel(*refs):
@@ -718,26 +718,31 @@
     up_step(0, 0)
     order(
         (VALUE, 0, 0),
-        FAR,
         (DOWN_Z, 0),
         *[(UP, h, m) for h in range(1, halves) for m in range(1, copies)],
     )
     for m in range(1, copies):
         v[DOWN, 0, m] = swap(v[DOWN_Z, 0], TEAM * m)
+    order((VALUE, 0, 0), FAR)
     v[HIDDEN, 1] = team_chunk(FAR)
     up_step(1, 0)
     for m in range(1, copies):
         up_parts[m] = jnp.concatenate([v[UP, h, m] for h in range(halves)], axis=1)
-        for i in (1, 0):
-            up_step(i, m)
+        up_step(1, m)
     order(
-        *[(VALUE, i, m) for i in range(2) for m in range(copies)],
+        *[(VALUE, 1, m) for m in range(copies)],
+        (HIDDEN, 0),
         *[(DOWN_Z, h) for h in range(1, halves)],
-        *[(DOWN, 0, n) for n in range(1, copies)],
     )
     for h in range(1, halves):
         for n in range(1, copies):
             v[DOWN, h, n] = swap(v[DOWN_Z, h], TEAM * n)
+    for m in range(1, copies):
+        up_step(0, m)
+    order(
+        *[(VALUE, i, m) for i in range(2) for m in range(copies)],
+        *[(DOWN, 0, n) for n in range(1, copies)],
+    )
     down_parts = {0: jnp.concatenate([v[DOWN_Z, h] for h in range(halves)], axis=0)}
     for m in range(1, copies):
         down_parts[m] = jnp.concatenate([v[DOWN, h, m] for h in range(halves)], axis=0)
@@ -749,12 +754,15 @@
     v[KEPT], v[AWAY] = down_step(1, [BF, BF], split=ROWS)
     order(KEPT, AWAY, (VALUE, 0, 0))
     v[AWAY] = swap(v[AWAY], 1)
+    order(KEPT, AWAY, (VALUE, 0, 0))
+    v[SEND] = next_hop()
+    order(SEND, (VALUE, 0, 0))
+    v[BACK] = swap(v[SEND], 2)
     v[THEIRS] = down_step(0, [BF], rows=(1, 2))
-    order(KEPT, AWAY, THEIRS, (VALUE, 0, 0))
-    v[SEND] = next_hop()
-    order(SEND, THEIRS, (VALUE, 0, 0))
-    v[BACK] = swap(v[SEND], 2)
-    v[THEIRS] = swap(v[THEIRS], 1)
+    order(THEIRS, (VALUE, 0, 0))
+    v[THEIRS] = jnp.concatenate(
+        [swap(v[THEIRS][:half], 1), swap(v[THEIRS][half:], 1)], axis=0
+    )
     v[OWN] = down_step(0, [F32], rows=(0, 2))
     order(OWN, THEIRS, BACK)
 
@@ -859,16 +867,22 @@
     v[KEPT], v[AWAY] = backward_step(1, BF)
     order(KEPT, AWAY, (DDOWN, 0))
     v[AWAY] = swap(v[AWAY], 1)
-    down_grad_step(0, 0)
-    order(KEPT, AWAY, (DOWN, SHARE, 0, 0), (DDOWN, 0))
+    order(KEPT, AWAY, (DDOWN, 0))
     v[SEND] = next_hop()
-    order(SEND, (DOWN, SHARE, 0, 0), (DDOWN, 0))
+    order(SEND, (DDOWN, 0))
     v[BACK] = swap(v[SEND], 2)
-    for h in late:
+    for h in range(halves):
         down_grad_step(0, h)
     order(*[(DOWN, SHARE, h, 0) for h in range(halves)], *received(DOWN, 0))
     reduce_step(DOWN, 0)
-    order(OWN, BACK, THEIRS, *[(DOWN, SHARE, h, 0) for h in late])
+    order(
+        OWN,
+        BACK,
+        THEIRS,
+        (LAYER, 0),
+        (LAYER, 1),
+        *[(DOWN, SHARE, h, 0) for h in late],
+    )
     dnormed1 = dsum2 + team_sum()
     dsum1 = norm_backward(dnormed1, gain_one, normal1, scale1)
     gain_one_grad = jnp.sum(dnormed1 * normal1, axis=0)
@@ -1035,16 +1049,8 @@
     order(
         *[(DQKV, OTHER, m) for m in range(copies)],
         *[(DOWN, PART, h) for h in range(halves)],
-        *received(OUT, 0),
-        (OUT, SHARE, 0, 0),
         *received(UP, *late),
-        (LAYER, 0),
-        (LAYER, 1),
     )
-    out_reduce_step()
-    vector_start()
-    v[DOWN, WHOLE, 0] = jnp.concatenate([v[DOWN, PART, h] for h in range(halves)], axis=0)
-    to_more(DOWN, near_far[0])
 
     def qkv_grad_step(m):
         pairs = [(tokens_mine, v[DQKV, MINE, m]), (tokens_other, v[DQKV, OTHER, m])]
@@ -1060,7 +1066,8 @@
         *shares(QKV, 0),
         *[(DQKV, name, m) for name in (MINE, OTHER) for m in range(copies)],
         (HIDDEN, 0),
-        *all_of(DOWN),
+        *received(OUT, 0),
+        (OUT, SHARE, 0, 0),
     )
     swap_share(QKV, 0)
     v[KEPT], v[AWAY] = dtokens_partial(OTHER, BF)
@@ -1068,17 +1075,17 @@
         KEPT,
         AWAY,
         *[(DQKV, MINE, m) for m in range(copies)],
-        *vector_names(),
         (HIDDEN, 0),
     )
     v[AWAY] = swap(v[AWAY], 1)
-    vector_step(1)
     order(KEPT, AWAY, *[(DQKV, MINE, m) for m in range(copies)], (HIDDEN, 0))
     v[SEND] = next_hop()
     v[BACK] = swap(v[SEND], 2)
+    vector_start()
     for h in late:
         up_grad_step(0, h)
         reduce_step(UP, h)
+    out_reduce_step()
     qkv_grad_step(0)
     v[OWN], v[THEIRS] = dtokens_partial(MINE, F32)
     order(
@@ -1088,22 +1095,24 @@
         *received(QKV, 0),
         *all_of(DOWN),
         *[(UP, PART, h) for h in range(halves)],
-        (VECTOR, 0),
-        (OUT, PART, 0),
+        *vector_names(),
     )
     reduce_step(QKV, 0)
+    vector_step(1)
+    v[DOWN, WHOLE, 0] = jnp.concatenate([v[DOWN, PART, h] for h in range(halves)], axis=0)
+    to_more(DOWN, near_far[0])
     v[THEIRS] = swap(v[THEIRS], 1)
     v[UP, WHOLE, 0] = jnp.concatenate([v[UP, PART, h] for h in range(halves)], axis=1)
     far_near = near_far[1:] + near_far[:1]
     to_more(UP, far_near[0])
+    order(OWN, THEIRS, BACK, *all_of(UP), *all_of(DOWN), (OUT, PART, 0))
     v[OUT, WHOLE, 0] = v[OUT, PART, 0]
     to_more(OUT, far_near[0])
-    order(OWN, THEIRS, BACK, *all_of(UP), *all_of(DOWN), *all_of(OUT))
     for i, mask in enumerate(far_near[1:]):
         to_more(UP, mask)
         to_more(DOWN, near_far[1 + i])
     v[OWN] = (dsum1 + team_sum()).astype(BF)
-    order((QKV, PART, 0), OWN, (VECTOR, 0), *all_of(UP), *all_of(DOWN))
+    order((QKV, PART, 0), OWN, (VECTOR, 0), *all_of(UP), *all_of(DOWN), *all_of(OUT))
     qkv_part = lax.all_gather(v[QKV, PART, 0], "rep", axis=0, tiled=False)
     v[GRAD, 0], v[GRAD, 1] = leave_team(v[OWN][:block], v[OWN][block:])
     to_more(UP, 1)

time: 1160 us -> 1140 us (0.983)
  waiting for transfers between devices: 428 us -> 409 us
    ppermute x67 -> x68, waiting for transfers between devices: 360 us -> 322 us  [swap(): return lax.ppermute(x, 'rep', [(i, i ^ mask) for i in range(reps)])]
    ppermute x2, waiting for transfers between devices: 0.01 us -> 12.2 us  [leave_team(): second = lax.ppermute(second, axes, [(b, a) for a, b in odd])]
    unnamed x309 -> x295, local copies, waits for them, and re-layouts: 95.7 us -> 91.9 us
    ppermute x67 -> x68, starting transfers between devices: 51.5 us -> 53.4 us  [swap(): return lax.ppermute(x, 'rep', [(i, i ^ mask) for i in range(reps)])]
  transfers between devices with their start and end apart: 95 -> 96, of which waited for: 38 -> 38; matrix products, arithmetic and copies ran while one was open for 14% -> 15% of each run, Pallas kernels for 28% -> 28%
where the time goes in v4:
time: 1140 us; the launch traced here: 1120 us
  waiting for transfers between devices  409 us (36%)
  Pallas kernels  380 us (33%)
  local copies, waits for them, and re-layouts  131 us (11%)
  other arithmetic  108 us (9%)
  starting transfers between devices  77.1 us (7%)
  between operations  16.5 us (1%)
    ppermute x68, waiting for transfers between devices, swap(): return lax.ppermute(x, 'rep', [(i, i ^ mask) for i in range(reps)])  322 us
    pallas_call x33, Pallas kernels, dot(): pl.pallas_call(kernel, grid=(size // step,), in_specs=x_specs + w_specs +...  284 us
    unnamed x295, local copies, waits for them, and re-layouts  91.9 us
    all_gather x7, waiting for transfers between devices, over_z(): return lax.all_gather(x, 'fsdp', axis=0, tiled=True)  55.2 us
    ppermute x68, starting transfers between devices, swap(): return lax.ppermute(x, 'rep', [(i, i ^ mask) for i in range(reps)])  53.4 us
    pallas_call x4, Pallas kernels, attend_backward(): pl.pallas_call(kernel, grid=(heads,), in_specs=[pl.BlockSpec((rows, 3 * h...  34.8 us
    convert_element_type x10, other arithmetic, add(): return total.astype(BF)  33.2 us
  transfers between devices with their start and end apart: 96, of which 38 were waited for; matrix products, arithmetic and copies ran while one was open for 15% of the time, Pallas kernels for 28%

profile of v4, /device:TPU:18, one launch (start us, length us, event | category | flops | bytes accessed | tf_op | source)
XLA Modules:
  0.0 1122.0 jit_solution(180058386519448037)
XLA Ops:
  66.1 24.1 %collective-permute-done.10 = bf16[256,2048]{1,0:T(8,128)(2,1)S(1)} collective-permute-done((bf16[256,2048]{1,0:T(8,128)(2,1)}, bf16[256,2048]{1,0:T(8,128)(2,1)S(1)}, u32[]{:S(2)}, u32[]{:S(2)}) %collective-permute-start.10) | collective-permute-done | bytes 1048608 | tf_op jit(solution)/shard_map/ppermute | solution.py:434
  90.2 21.9 %collective-permute-done.11 = bf16[256,2048]{1,0:T(8,128)(2,1)} collective-permute-done((bf16[256,2048]{1,0:T(8,128)(2,1)}, bf16[256,2048]{1,0:T(8,128)(2,1)}, u32[]{:S(2)}, u32[]{:S(2)}) %collective-permute-start.11) | collective-permute-done | bytes 1048608 | tf_op jit(solution)/shard_map/ppermute | solution.py:434
  123.3 14.7 %all-gather.12.cloned.1.call-done = bf16[2048,384]{1,0:T(8,128)(2,1)} async-done(((bf16[512,384]{1,0:T(8,128)(2,1)}), bf16[2048,384]{1,0:T(8,128)(2,1)}) %all-gather.12.cloned.1.call-update) | async-done | bytes 1572880 | tf_op jit(solution)/shard_map/all_gather | solution.py:528
  176.9 11.6 %collective-permute-done.15 = bf16[2048,384]{1,0:T(8,128)(2,1)} collective-permute-done((bf16[2048,384]{1,0:T(8,128)(2,1)}, bf16[2048,384]{1,0:T(8,128)(2,1)}, u32[]{:S(2)}, u32[]{:S(2)}) %collective-permute-start.15) | collective-permute-done | bytes 1572896 | tf_op jit(solution)/shard_map/ppermute | solution.py:434
  249.8 30.8 %all-gather.18.cloned.1.call-done = bf16[2048,512]{1,0:T(8,128)(2,1)} async-done(((bf16[512,512]{1,0:T(8,128)(2,1)}), bf16[2048,512]{1,0:T(8,128)(2,1)}) %all-gather.18.cloned.1.call-update) | async-done | bytes 2097168 | tf_op jit(solution)/shard_map/all_gather | solution.py:528
  307.3 10.1 shard_map.319
  328.3 15.3 %collective-permute-done.22 = bf16[2048,512]{1,0:T(8,128)(2,1)} collective-permute-done((bf16[2048,512]{1,0:T(8,128)(2,1)}, bf16[2048,512]{1,0:T(8,128)(2,1)}, u32[]{:S(2)}, u32[]{:S(2)}) %collective-permute-start.22) | collective-permute-done | bytes 2097184 | tf_op jit(solution)/shard_map/ppermute | solution.py:434
  353.4 10.5 shard_map.320
  382.7 10.2 shard_map.322
  400.5 39.5 %collective-permute-done.26 = bf16[512,2048]{1,0:T(8,128)(2,1)S(1)} collective-permute-done((bf16[512,2048]{1,0:T(8,128)(2,1)}, bf16[512,2048]{1,0:T(8,128)(2,1)S(1)}, u32[]{:S(2)}, u32[]{:S(2)}) %collective-permute-start.26) | collective-permute-done | bytes 2097184 | tf_op jit(solution)/shard_map/ppermute | solution.py:434
  441.6 13.0 %shard_map.323 = (bf16[512,2048]{1,0:T(8,128)(2,1)S(1)}, bf16[512,2048]{1,0:T(8,128)(2,1)S(1)}) custom-call(bf16[1024,1024]{1,0:T(8,128)(2,1)} %copy-done.11, bf16[1024,1024]{1,0:T(8,128)(2,1)} %copy-done.31, bf16[1024,2048]{1,0:T(8,128)(2,1)} %copy-done.82, bf16[1024,2048]{1,0:T(8,128)(2,1)} %constant_dynamic-update-slice_fusion.16.refs_3_.refs_1_), custom_call_target="tpu_custom_call" | custom-call | tf_op jit(solution)/shard_map/pallas_call | solution.py:179
  484.9 22.5 %collective-permute-done.30 = bf16[512,2048]{1,0:T(8,128)(2,1)S(1)} collective-permute-done((bf16[512,2048]{1,0:T(8,128)(2,1)S(1)}, bf16[512,2048]{1,0:T(8,128)(2,1)S(1)}, u32[]{:S(2)}, u32[]{:S(2)}) %collective-permute-start.30) | collective-permute-done | bytes 2097184 | tf_op jit(solution)/shard_map/ppermute | solution.py:434
  516.9 11.4 %collective-permute-done.32 = bf16[256,2048]{1,0:T(8,128)(2,1)S(1)} collective-permute-done((bf16[256,2048]{1,0:T(8,128)(2,1)S(1)}, bf16[256,2048]{1,0:T(8,128)(2,1)S(1)}, u32[]{:S(2)}, u32[]{:S(2)}) %collective-permute-start.32) | collective-permute-done | bytes 1048608 | tf_op jit(solution)/shard_map/ppermute | solution.py:464
  556.2 12.8 %shard_map.328 = (f32[512,2048]{1,0:T(8,128)}, bf16[512,2048]{1,0:T(8,128)(2,1)}) custom-call(bf16[1024,1024]{1,0:T(8,128)(2,1)S(1)} %shard_map.326.refs_0_.refs_2_, bf16[1024,1024]{1,0:T(8,128)(2,1)} %copy-done.6, bf16[2048,1024]{1,0:T(8,128)(2,1)} %copy-done.85, bf16[2048,1024]{1,0:T(8,128)(2,1)} %copy-done.84), custom_call_target="tpu_custom_call" | custom-call | tf_op jit(solution)/shard_map/pallas_call | solution.py:179
  569.0 12.3 %collective-permute-done.34 = bf16[512,2048]{1,0:T(8,128)(2,1)} collective-permute-done((bf16[512,2048]{1,0:T(8,128)(2,1)S(1)}, bf16[512,2048]{1,0:T(8,128)(2,1)}, u32[]{:S(2)}, u32[]{:S(2)}) %collective-permute-start.34) | collective-permute-done | bytes 2097184 | tf_op jit(solution)/shard_map/ppermute | solution.py:434
  587.8 14.6 %shard_map.329 = (bf16[512,2048]{1,0:T(8,128)(2,1)S(1)}, bf16[512,2048]{1,0:T(8,128)(2,1)}) custom-call(bf16[1024,1024]{1,0:T(8,128)(2,1)} %copy-done.12, bf16[1024,1024]{1,0:T(8,128)(2,1)} %copy-done.31, bf16[1024,2048]{1,0:T(8,128)(2,1)} %copy-done.81, bf16[1024,2048]{1,0:T(8,128)(2,1)} %copy-done.80), custom_call_target="tpu_custom_call" | custom-call | tf_op jit(solution)/shard_map/pallas_call | solution.py:179
  620.7 12.6 %shard_map.332 = (bf16[512,2048]{1,0:T(8,128)(2,1)S(1)}, bf16[512,2048]{1,0:T(8,128)(2,1)S(1)}) custom-call(bf16[1024,1024]{1,0:T(8,128)(2,1)} %copy-done.2, bf16[1024,1024]{1,0:T(8,128)(2,1)} %copy-done.7, bf16[2048,1024]{1,0:T(8,128)(2,1)} %copy-done.85, bf16[2048,1024]{1,0:T(8,128)(2,1)} %copy-done.84), custom_call_target="tpu_custom_call" | custom-call | tf_op jit(solution)/shard_map/pallas_call | solution.py:179
  664.1 17.6 %collective-permute-done.41 = bf16[512,2048]{1,0:T(8,128)(2,1)S(1)} collective-permute-done((bf16[512,2048]{1,0:T(8,128)(2,1)S(1)}, bf16[512,2048]{1,0:T(8,128)(2,1)S(1)}, u32[]{:S(2)}, u32[]{:S(2)}) %collective-permute-start.41) | collective-permute-done | bytes 2097184 | tf_op jit(solution)/shard_map/ppermute | solution.py:434
  684.4 12.2 %collective-permute-done.40 = bf16[256,2048]{1,0:T(8,128)(2,1)} collective-permute-done((bf16[256,2048]{1,0:T(8,128)(2,1)}, bf16[256,2048]{1,0:T(8,128)(2,1)}, u32[]{:S(2)}, u32[]{:S(2)}) %collective-permute-start.40) | collective-permute-done | bytes 1048608 | tf_op jit(solution)/shard_map/ppermute | solution.py:472
  715.0 13.0 %shard_map.335 = (bf16[2048,512]{1,0:T(8,128)(2,1)}, bf16[2048,512]{1,0:T(8,128)(2,1)S(1)}) custom-call(bf16[1024,2048]{1,0:T(8,128)(2,1)} %pad_maximum_fusion.1.refs_0_, bf16[1024,2048]{1,0:T(8,128)(2,1)} %copy-done.83, bf16[1024,1024]{1,0:T(8,128)(2,1)} %copy-done.6, bf16[1024,1024]{1,0:T(8,128)(2,1)} %copy-done.7), custom_call_target="tpu_custom_call" | custom-call | tf_op jit(solution)/shard_map/pallas_call | solution.py:179
  767.2 10.2 collective-permute-done.45
  913.7 39.2 %collective-permute-done.51 = bf16[2048,768]{1,0:T(8,128)(2,1)} collective-permute-done((bf16[2048,768]{1,0:T(8,128)(2,1)}, bf16[2048,768]{1,0:T(8,128)(2,1)}, u32[]{:S(2)}, u32[]{:S(2)}) %collective-permute-start.51) | collective-permute-done | bytes 3145760 | tf_op jit(solution)/shard_map/ppermute | solution.py:434
  963.8 20.3 %collective-permute-done.57.refs_2_ = bf16[256,2048]{1,0:T(8,128)(2,1)S(1)} collective-permute-done((bf16[256,2048]{1,0:T(8,128)(2,1)S(1)}, bf16[256,2048]{1,0:T(8,128)(2,1)S(1)}, u32[]{:S(2)}, u32[]{:S(2)}) %collective-permute-start.57) | collective-permute-done | bytes 1048608 | tf_op jit(solution)/shard_map/ppermute | solution.py:434
  1001.0 38.4 %collective-permute-done.63 = bf16[128,1024]{1,0:T(8,128)(2,1)S(1)} collective-permute-done((bf16[128,1024]{1,0:T(8,128)(2,1)}, bf16[128,1024]{1,0:T(8,128)(2,1)S(1)}, u32[]{:S(2)}, u32[]{:S(2)}) %collective-permute-start.63) | collective-permute-done | bytes 262176 | tf_op jit(solution)/shard_map/ppermute | solution.py:434
  (672 shorter events, 667.0 us)
Async XLA Ops:
  7.3 104.8 %all-gather.10.cloned.1.call-start = ((), (), s32[]{:S(2)}) async-start(), calls=%async_computation.6 | async-start | bytes 1966080 | tf_op jit(solution)/shard_map/all_gather | solution.py:528
  63.2 74.8 %all-gather.12.cloned.1.call-start = ((), (), s32[]{:S(2)}) async-start(), calls=%async_computation.7 | async-start | bytes 1966080 | tf_op jit(solution)/shard_map/all_gather | solution.py:528
  63.9 113.0 %all-gather.14.cloned.1.call-start = ((), (), s32[]{:S(2)}) async-start(), calls=%async_computation.8 | async-start | bytes 1310720 | tf_op jit(solution)/shard_map/all_gather | solution.py:528
  114.5 120.2 %all-gather.16.cloned.1.call-start = ((), (), s32[]{:S(2)}) async-start(), calls=%async_computation.9 | async-start | bytes 2621440 | tf_op jit(solution)/shard_map/all_gather | solution.py:528
  118.1 58.8 %collective-permute-start.14 = (bf16[2048,384]{1,0:T(8,128)(2,1)}, bf16[2048,384]{1,0:T(8,128)(2,1)}, u32[]{:S(2)}, u32[]{:S(2)}) collective-permute-start(bf16[2048,384]{1,0:T(8,128)(2,1)} %all-gather.10.cloned.1.call-done), channel_id=1, source_target_pairs={{0,16},{4,20},{8,24},{12,28},{16,0},{20,4},{24,8},{28,12},{1,17},{... | collective-permute-start | bytes 4718600 | tf_op jit(solution)/shard_map/ppermute | solution.py:434
  190.1 90.5 %all-gather.18.cloned.1.call-start = ((), (), s32[]{:S(2)}) async-start(), calls=%async_computation.10 | async-start | bytes 2621440 | tf_op jit(solution)/shard_map/all_gather | solution.py:528
  222.1 106.2 %all-gather.20.cloned.1.call-start = ((), (), s32[]{:S(2)}) async-start(), calls=%async_computation.11 | async-start | bytes 2621440 | tf_op jit(solution)/shard_map/all_gather | solution.py:528
  283.4 95.9 %all-gather.22.cloned.1.call-start = ((), (), s32[]{:S(2)}) async-start(), calls=%async_computation.12 | async-start | bytes 2621440 | tf_op jit(solution)/shard_map/all_gather | solution.py:528
  298.6 540.6 %reduce-scatter.7.cloned.1.call-start = ((), (), s32[]{:S(2)}) async-start(), calls=%async_computation.13 | async-start | bytes 2621440 | tf_op jit(solution)/shard_map/reduce_scatter | solution.py:799
  379.3 60.7 %collective-permute-start.26 = (bf16[512,2048]{1,0:T(8,128)(2,1)}, bf16[512,2048]{1,0:T(8,128)(2,1)S(1)}, u32[]{:S(2)}, u32[]{:S(2)}) collective-permute-start(bf16[512,2048]{1,0:T(8,128)(2,1)} %all-gather.22.cloned.1.call-done), channel_id=1, source_target_pairs={{0,16},{4,20},{8,24},{12,28},{16,0},{20,4},{24,8},{28,12},{1,17},{... | collective-permute-start | bytes 6291464 | tf_op jit(solution)/shard_map/ppermute | solution.py:434
  633.6 63.0 %collective-permute-start.38 = (bf16[512,2048]{1,0:T(8,128)(2,1)}, bf16[512,2048]{1,0:T(8,128)(2,1)}, u32[]{:S(2)}, u32[]{:S(2)}) collective-permute-start(bf16[512,2048]{1,0:T(8,128)(2,1)} %get-tuple-element.372), channel_id=1, source_target_pairs={{0,4},{4,0},{8,12},{12,8},{16,20},{20,16},{24,28},{28,24},{1,5},{5... | collective-permute-start | bytes 6291464 | tf_op jit(solution)/shard_map/ppermute | solution.py:434
  641.3 55.3 %collective-permute-start.37 = (bf16[512,2048]{1,0:T(8,128)(2,1)}, bf16[512,2048]{1,0:T(8,128)(2,1)}, u32[]{:S(2)}, u32[]{:S(2)}) collective-permute-start(bf16[512,2048]{1,0:T(8,128)(2,1)} %add_convert_fusion.7), channel_id=1, source_target_pairs={{0,8},{4,12},{8,0},{12,4},{16,24},{20,28},{24,16},{28,20},{1,9},{5... | collective-permute-start | bytes 6291464 | tf_op jit(solution)/shard_map/ppermute | solution.py:434
  684.3 154.9 %reduce-scatter.9.cloned.1.call-start = ((), (), s32[]{:S(2)}) async-start(), calls=%async_computation.14 | async-start | bytes 2621440 | tf_op jit(solution)/shard_map/reduce_scatter | solution.py:799
  709.4 57.7 %collective-permute-start.42 = (bf16[512,2048]{1,0:T(8,128)(2,1)}, bf16[512,2048]{1,0:T(8,128)(2,1)}, u32[]{:S(2)}, u32[]{:S(2)}) collective-permute-start(bf16[512,2048]{1,0:T(8,128)(2,1)} %get-tuple-element.383), channel_id=1, source_target_pairs={{0,8},{4,12},{8,0},{12,4},{16,24},{20,28},{24,16},{28,20},{1,9},{5... | collective-permute-start | bytes 6291464 | tf_op jit(solution)/shard_map/ppermute | solution.py:434
  734.9 178.8 %reduce-scatter.11.cloned.1.call-start = ((), (), s32[]{:S(2)}) async-start(), calls=%async_computation.15 | async-start | bytes 2621440 | tf_op jit(solution)/shard_map/reduce_scatter | solution.py:799
  777.4 61.8 %collective-permute-start.47 = (bf16[2048,512]{1,0:T(8,128)(2,1)}, bf16[2048,512]{1,0:T(8,128)(2,1)}, u32[]{:S(2)}, u32[]{:S(2)}) collective-permute-start(bf16[2048,512]{1,0:T(8,128)(2,1)} %copy-done.75), channel_id=1, source_target_pairs={{0,16},{4,20},{8,24},{12,28},{16,0},{20,4},{24,8},{28,12},{1,17},{... | collective-permute-start | bytes 6291464 | tf_op jit(solution)/shard_map/ppermute | solution.py:434
  812.5 140.4 %reduce-scatter.13.cloned.1.call-start = ((), (), s32[]{:S(2)}) async-start(), calls=%async_computation.16 | async-start | bytes 2621440 | tf_op jit(solution)/shard_map/reduce_scatter | solution.py:799
  878.6 105.4 %reduce-scatter.17.cloned.1.call-start = ((), (), s32[]{:S(2)}) async-start(), calls=%async_computation.18 | async-start | bytes 1310720 | tf_op jit(solution)/shard_map/reduce_scatter | solution.py:799
  882.3 70.5 %collective-permute-start.51 = (bf16[2048,768]{1,0:T(8,128)(2,1)}, bf16[2048,768]{1,0:T(8,128)(2,1)}, u32[]{:S(2)}, u32[]{:S(2)}) collective-permute-start(bf16[2048,768]{1,0:T(8,128)(2,1)} %shard_map.345), channel_id=1, source_target_pairs={{0,16},{4,20},{8,24},{12,28},{16,0},{20,4},{24,8},{28,12},{1,17},{... | collective-permute-start | bytes 9437192 | tf_op jit(solution)/shard_map/ppermute | solution.py:434
  888.3 64.5 %collective-permute-start.50 = (bf16[512,2048]{1,0:T(8,128)(2,1)}, bf16[512,2048]{1,0:T(8,128)(2,1)}, u32[]{:S(2)}, u32[]{:S(2)}) collective-permute-start(bf16[512,2048]{1,0:T(8,128)(2,1)} %add_convert_fusion.4), channel_id=1, source_target_pairs={{0,8},{4,12},{8,0},{12,4},{16,24},{20,28},{24,16},{28,20},{1,9},{5... | collective-permute-start | bytes 6291464 | tf_op jit(solution)/shard_map/ppermute | solution.py:434
  891.4 150.5 %reduce-scatter.15.cloned.1.call-start = ((), (), s32[]{:S(2)}) async-start(), calls=%async_computation.17 | async-start | bytes 3932160 | tf_op jit(solution)/shard_map/reduce_scatter | solution.py:799
  958.2 148.1 %all-gather.24.cloned.1.call-start = ((), (), s32[]{:S(2)}) async-start(), calls=%async_computation.19 | async-start | bytes 7077888 | tf_op jit(solution)/shard_map/all_gather | solution.py:1116
  986.5 53.0 %collective-permute-start.59 = (bf16[512,1024]{1,0:T(8,128)(2,1)S(1)}, bf16[512,1024]{1,0:T(8,128)(2,1)S(1)}, u32[]{:S(2)}, u32[]{:S(2)}) collective-permute-start(bf16[512,1024]{1,0:T(8,128)(2,1)S(1)} %constant_dynamic-update-slice_fusion.35.refs_0_), channel_id=1, source_target_pairs={{0,8},{4,12},{8,0},{12,4},{16,24},{20,28},{24,16},{28,20},{1,9},{5... | collective-permute-start | bytes 3145736 | tf_op jit(solution)/shard_map/ppermute | solution.py:434
  990.2 51.6 %collective-permute-start.62 = (bf16[256,2048]{1,0:T(8,128)(2,1)S(1)}, bf16[256,2048]{1,0:T(8,128)(2,1)}, u32[]{:S(2)}, u32[]{:S(2)}) collective-permute-start(bf16[256,2048]{1,0:T(8,128)(2,1)S(1)} %collective-permute-done.57.refs_2_), channel_id=1, source_target_pairs={{0,16},{4,20},{8,24},{12,28},{16,0},{20,4},{24,8},{28,12},{1,17},{... | collective-permute-start | bytes 3145736 | tf_op jit(solution)/shard_map/ppermute | solution.py:434
  (192 other events, 2691.0 us)
Sparse Core Ops, SparseCore 0:
  63.3 36.5 all-gather.9
  102.0 35.9 all-gather.11
  140.1 27.4 all-gather.13
  190.2 43.6 all-gather.15
  235.9 44.6 all-gather.17
  283.5 44.7 all-gather.19
  330.5 44.6 all-gather.21
  684.4 43.4 reduce-scatter.6
  735.0 43.7 reduce-scatter.8
  812.6 42.2 reduce-scatter.10
  878.8 44.8 reduce-scatter.12
  926.4 25.8 reduce-scatter.16
  958.3 60.4 reduce-scatter.14
  1042.0 49.0 all-gather.23

commit v5 on v4

--- a/solution.py
+++ b/solution.py
@@ -290,7 +290,7 @@
     )(qkv, dcontext, log_total, mask)
 
 
-def place_rows(pieces, places, shape):
+def place_rows(pieces, places, shape, spot=lambda place: (place, 0)):
     count, (rows, width) = len(pieces), pieces[0].shape
 
     def kernel(places_ref, *refs):
@@ -306,7 +306,7 @@
             num_scalar_prefetch=1,
             grid=(count,),
             in_specs=[pl.BlockSpec((rows, width), lambda i, s: (0, 0))] * count,
-            out_specs=pl.BlockSpec((rows, width), lambda i, s: (s[i], 0)),
+            out_specs=pl.BlockSpec((rows, width), lambda i, s: spot(s[i])),
         ),
         out_shape=jax.ShapeDtypeStruct(shape, F32),
         compiler_params=pltpu.CompilerParams(vmem_limit_bytes=VMEM_LIMIT),
@@ -1140,16 +1140,24 @@
     for mask in near_far[1:]:
         vector_step(mask)
     tokens_grad = settle(v[GRAD, 0], v[GRAD, 1]).astype(F32)
-    out_grad = in_order({m: v[OUT, WHOLE, m] for m in range(reps)})
-
-    if per_shard >= TEAM:
-        out_grad = out_grad.reshape(copies, TEAM, per_shard // TEAM, head_dim, wide)
-        out_grad = out_grad.transpose(2, 1, 3, 0, 4)
+
+    if aligned and per_shard == TEAM:
+        out_grad = place_rows(
+            [v[OUT, WHOLE, m].reshape(head_dim, wide) for m in range(reps)],
+            places,
+            (shard, width),
+            lambda place: (lax.rem(place, TEAM), lax.div(place, TEAM)),
+        )
     else:
-        fill = TEAM // per_shard
-        out_grad = out_grad.reshape(copies, fill, per_shard, head_dim, wide)
-        out_grad = pick(out_grad, z % fill, 1).transpose(1, 2, 0, 3)
-    out_grad = out_grad.reshape(-1, width).astype(F32)
+        out_grad = in_order({m: v[OUT, WHOLE, m] for m in range(reps)})
+        if per_shard >= TEAM:
+            out_grad = out_grad.reshape(copies, TEAM, per_shard // TEAM, head_dim, wide)
+            out_grad = out_grad.transpose(2, 1, 3, 0, 4)
+        else:
+            fill = TEAM // per_shard
+            out_grad = out_grad.reshape(copies, fill, per_shard, head_dim, wide)
+            out_grad = pick(out_grad, z % fill, 1).transpose(1, 2, 0, 3)
+        out_grad = out_grad.reshape(-1, width).astype(F32)
 
     if aligned:
         down_grad, up_grad = v[DOWN_GRAD], v[UP_GRAD]

time: 1140 us -> 1130 us (level)
  local copies, waits for them, and re-layouts: 131 us -> 118 us
    unnamed x295 -> x276, local copies, waits for them, and re-layouts: 91.9 us -> 82.3 us
  transfers between devices with their start and end apart: 96 -> 96, of which waited for: 38 -> 39; matrix products, arithmetic and copies ran while one was open for 15% -> 14% of each run, Pallas kernels for 28% -> 29%
where the time goes in v5:
time: 1130 us; the launch traced here: 1120 us
  waiting for transfers between devices  408 us (36%)
  Pallas kernels  386 us (34%)
  local copies, waits for them, and re-layouts  118 us (10%)
  other arithmetic  109 us (10%)
  starting transfers between devices  81.8 us (7%)
  between operations  16.3 us (1%)
    ppermute x68, waiting for transfers between devices, swap(): return lax.ppermute(x, 'rep', [(i, i ^ mask) for i in range(reps)])  319 us
    pallas_call x33, Pallas kernels, dot(): pl.pallas_call(kernel, grid=(size // step,), in_specs=x_specs + w_specs +...  286 us
    unnamed x276, local copies, waits for them, and re-layouts  82.3 us
    all_gather x7, waiting for transfers between devices, over_z(): return lax.all_gather(x, 'fsdp', axis=0, tiled=True)  55.5 us
    ppermute x68, starting transfers between devices, swap(): return lax.ppermute(x, 'rep', [(i, i ^ mask) for i in range(reps)])  53.3 us
    convert_element_type x10, other arithmetic, add(): return total.astype(BF)  34.8 us
    pallas_call x4, Pallas kernels, attend_backward(): pl.pallas_call(kernel, grid=(heads,), in_specs=[pl.BlockSpec((rows, 3 * h...  34.8 us
    pallas_call x4, Pallas kernels, attend(): pl.pallas_call(kernel, grid=(heads,), in_specs=[pl.BlockSpec((rows, 3 * h...  22.6 us
  transfers between devices with their start and end apart: 96, of which 39 were waited for; matrix products, arithmetic and copies ran while one was open for 14% of the time, Pallas kernels for 29%

profile of v5, /device:TPU:18, one launch (start us, length us, event | category | flops | bytes accessed | tf_op | source)
XLA Modules:
  0.0 1119.3 jit_solution(13139347462704070478)
XLA Ops:
  66.2 24.1 %collective-permute-done.10 = bf16[256,2048]{1,0:T(8,128)(2,1)S(1)} collective-permute-done((bf16[256,2048]{1,0:T(8,128)(2,1)}, bf16[256,2048]{1,0:T(8,128)(2,1)S(1)}, u32[]{:S(2)}, u32[]{:S(2)}) %collective-permute-start.10) | collective-permute-done | bytes 1048608 | tf_op jit(solution)/shard_map/ppermute | solution.py:434
  90.4 21.9 %collective-permute-done.11 = bf16[256,2048]{1,0:T(8,128)(2,1)} collective-permute-done((bf16[256,2048]{1,0:T(8,128)(2,1)}, bf16[256,2048]{1,0:T(8,128)(2,1)}, u32[]{:S(2)}, u32[]{:S(2)}) %collective-permute-start.11) | collective-permute-done | bytes 1048608 | tf_op jit(solution)/shard_map/ppermute | solution.py:434
  123.4 14.7 %all-gather.12.cloned.1.call-done = bf16[2048,384]{1,0:T(8,128)(2,1)} async-done(((bf16[512,384]{1,0:T(8,128)(2,1)}), bf16[2048,384]{1,0:T(8,128)(2,1)}) %all-gather.12.cloned.1.call-update) | async-done | bytes 1572880 | tf_op jit(solution)/shard_map/all_gather | solution.py:528
  176.1 12.6 %collective-permute-done.15 = bf16[2048,384]{1,0:T(8,128)(2,1)} collective-permute-done((bf16[2048,384]{1,0:T(8,128)(2,1)}, bf16[2048,384]{1,0:T(8,128)(2,1)}, u32[]{:S(2)}, u32[]{:S(2)}) %collective-permute-start.15) | collective-permute-done | bytes 1572896 | tf_op jit(solution)/shard_map/ppermute | solution.py:434
  249.6 31.1 %all-gather.18.cloned.1.call-done = bf16[2048,512]{1,0:T(8,128)(2,1)} async-done(((bf16[512,512]{1,0:T(8,128)(2,1)}), bf16[2048,512]{1,0:T(8,128)(2,1)}) %all-gather.18.cloned.1.call-update) | async-done | bytes 2097168 | tf_op jit(solution)/shard_map/all_gather | solution.py:528
  307.1 10.1 shard_map.319
  328.1 15.2 %collective-permute-done.22 = bf16[2048,512]{1,0:T(8,128)(2,1)} collective-permute-done((bf16[2048,512]{1,0:T(8,128)(2,1)}, bf16[2048,512]{1,0:T(8,128)(2,1)}, u32[]{:S(2)}, u32[]{:S(2)}) %collective-permute-start.22) | collective-permute-done | bytes 2097184 | tf_op jit(solution)/shard_map/ppermute | solution.py:434
  353.2 10.5 shard_map.320
  366.4 10.1 shard_map.321
  382.5 10.2 shard_map.322
  400.3 39.5 %collective-permute-done.26 = bf16[512,2048]{1,0:T(8,128)(2,1)S(1)} collective-permute-done((bf16[512,2048]{1,0:T(8,128)(2,1)}, bf16[512,2048]{1,0:T(8,128)(2,1)S(1)}, u32[]{:S(2)}, u32[]{:S(2)}) %collective-permute-start.26) | collective-permute-done | bytes 2097184 | tf_op jit(solution)/shard_map/ppermute | solution.py:434
  441.4 13.0 %shard_map.323 = (bf16[512,2048]{1,0:T(8,128)(2,1)S(1)}, bf16[512,2048]{1,0:T(8,128)(2,1)S(1)}) custom-call(bf16[1024,1024]{1,0:T(8,128)(2,1)} %copy-done.11, bf16[1024,1024]{1,0:T(8,128)(2,1)} %copy-done.31, bf16[1024,2048]{1,0:T(8,128)(2,1)} %copy-done.84, bf16[1024,2048]{1,0:T(8,128)(2,1)} %constant_dynamic-update-slice_fusion.16.refs_3_.refs_1_), custom_call_target="tpu_custom_call" | custom-call | tf_op jit(solution)/shard_map/pallas_call | solution.py:179
  486.1 22.6 %collective-permute-done.30 = bf16[512,2048]{1,0:T(8,128)(2,1)} collective-permute-done((bf16[512,2048]{1,0:T(8,128)(2,1)}, bf16[512,2048]{1,0:T(8,128)(2,1)}, u32[]{:S(2)}, u32[]{:S(2)}) %collective-permute-start.30) | collective-permute-done | bytes 2097184 | tf_op jit(solution)/shard_map/ppermute | solution.py:434
  517.6 11.9 %collective-permute-done.32 = bf16[256,2048]{1,0:T(8,128)(2,1)S(1)} collective-permute-done((bf16[256,2048]{1,0:T(8,128)(2,1)S(1)}, bf16[256,2048]{1,0:T(8,128)(2,1)S(1)}, u32[]{:S(2)}, u32[]{:S(2)}) %collective-permute-start.32) | collective-permute-done | bytes 1048608 | tf_op jit(solution)/shard_map/ppermute | solution.py:464
  557.6 12.8 %shard_map.328 = (f32[512,2048]{1,0:T(8,128)}, bf16[512,2048]{1,0:T(8,128)(2,1)}) custom-call(bf16[1024,1024]{1,0:T(8,128)(2,1)S(1)} %shard_map.326.refs_0_.refs_2_, bf16[1024,1024]{1,0:T(8,128)(2,1)} %copy-done.6, bf16[2048,1024]{1,0:T(8,128)(2,1)} %copy-done.87, bf16[2048,1024]{1,0:T(8,128)(2,1)} %copy-done.86), custom_call_target="tpu_custom_call" | custom-call | tf_op jit(solution)/shard_map/pallas_call | solution.py:179
  570.4 12.2 %collective-permute-done.34 = bf16[512,2048]{1,0:T(8,128)(2,1)} collective-permute-done((bf16[512,2048]{1,0:T(8,128)(2,1)S(1)}, bf16[512,2048]{1,0:T(8,128)(2,1)}, u32[]{:S(2)}, u32[]{:S(2)}) %collective-permute-start.34) | collective-permute-done | bytes 2097184 | tf_op jit(solution)/shard_map/ppermute | solution.py:434
  589.2 14.6 %shard_map.329 = (bf16[512,2048]{1,0:T(8,128)(2,1)S(1)}, bf16[512,2048]{1,0:T(8,128)(2,1)}) custom-call(bf16[1024,1024]{1,0:T(8,128)(2,1)} %copy-done.12, bf16[1024,1024]{1,0:T(8,128)(2,1)} %copy-done.31, bf16[1024,2048]{1,0:T(8,128)(2,1)} %copy-done.83, bf16[1024,2048]{1,0:T(8,128)(2,1)} %copy-done.82), custom_call_target="tpu_custom_call" | custom-call | tf_op jit(solution)/shard_map/pallas_call | solution.py:179
  622.1 12.7 %shard_map.332 = (bf16[512,2048]{1,0:T(8,128)(2,1)S(1)}, bf16[512,2048]{1,0:T(8,128)(2,1)S(1)}) custom-call(bf16[1024,1024]{1,0:T(8,128)(2,1)} %copy-done.2, bf16[1024,1024]{1,0:T(8,128)(2,1)} %copy-done.7, bf16[2048,1024]{1,0:T(8,128)(2,1)} %copy-done.87, bf16[2048,1024]{1,0:T(8,128)(2,1)} %copy-done.86), custom_call_target="tpu_custom_call" | custom-call | tf_op jit(solution)/shard_map/pallas_call | solution.py:179
  665.2 17.8 %collective-permute-done.41 = bf16[512,2048]{1,0:T(8,128)(2,1)S(1)} collective-permute-done((bf16[512,2048]{1,0:T(8,128)(2,1)S(1)}, bf16[512,2048]{1,0:T(8,128)(2,1)S(1)}, u32[]{:S(2)}, u32[]{:S(2)}) %collective-permute-start.41) | collective-permute-done | bytes 2097184 | tf_op jit(solution)/shard_map/ppermute | solution.py:434
  685.9 10.7 collective-permute-done.40
  716.0 13.0 %shard_map.335 = (bf16[2048,512]{1,0:T(8,128)(2,1)}, bf16[2048,512]{1,0:T(8,128)(2,1)S(1)}) custom-call(bf16[1024,2048]{1,0:T(8,128)(2,1)} %pad_maximum_fusion.1.refs_0_, bf16[1024,2048]{1,0:T(8,128)(2,1)} %copy-done.85, bf16[1024,1024]{1,0:T(8,128)(2,1)} %copy-done.6, bf16[1024,1024]{1,0:T(8,128)(2,1)} %copy-done.7), custom_call_target="tpu_custom_call" | custom-call | tf_op jit(solution)/shard_map/pallas_call | solution.py:179
  916.7 36.4 %collective-permute-done.51 = bf16[2048,768]{1,0:T(8,128)(2,1)} collective-permute-done((bf16[2048,768]{1,0:T(8,128)(2,1)}, bf16[2048,768]{1,0:T(8,128)(2,1)}, u32[]{:S(2)}, u32[]{:S(2)}) %collective-permute-start.51) | collective-permute-done | bytes 3145760 | tf_op jit(solution)/shard_map/ppermute | solution.py:434
  964.0 20.4 %collective-permute-done.57.refs_2_ = bf16[256,2048]{1,0:T(8,128)(2,1)S(1)} collective-permute-done((bf16[256,2048]{1,0:T(8,128)(2,1)S(1)}, bf16[256,2048]{1,0:T(8,128)(2,1)S(1)}, u32[]{:S(2)}, u32[]{:S(2)}) %collective-permute-start.57) | collective-permute-done | bytes 1048608 | tf_op jit(solution)/shard_map/ppermute | solution.py:434
  1001.3 38.6 %collective-permute-done.63.refs_4_ = bf16[128,1024]{1,0:T(8,128)(2,1)S(1)} collective-permute-done((bf16[128,1024]{1,0:T(8,128)(2,1)}, bf16[128,1024]{1,0:T(8,128)(2,1)S(1)}, u32[]{:S(2)}, u32[]{:S(2)}) %collective-permute-start.63) | collective-permute-done | bytes 262176 | tf_op jit(solution)/shard_map/ppermute | solution.py:434
  (650 shorter events, 666.4 us)
Async XLA Ops:
  7.3 105.0 %all-gather.10.cloned.1.call-start = ((), (), s32[]{:S(2)}) async-start(), calls=%async_computation.6 | async-start | bytes 1966080 | tf_op jit(solution)/shard_map/all_gather | solution.py:528
  63.3 74.8 %all-gather.12.cloned.1.call-start = ((), (), s32[]{:S(2)}) async-start(), calls=%async_computation.7 | async-start | bytes 1966080 | tf_op jit(solution)/shard_map/all_gather | solution.py:528
  64.0 112.0 %all-gather.14.cloned.1.call-start = ((), (), s32[]{:S(2)}) async-start(), calls=%async_computation.8 | async-start | bytes 1310720 | tf_op jit(solution)/shard_map/all_gather | solution.py:528
  114.7 119.8 %all-gather.16.cloned.1.call-start = ((), (), s32[]{:S(2)}) async-start(), calls=%async_computation.9 | async-start | bytes 2621440 | tf_op jit(solution)/shard_map/all_gather | solution.py:528
  118.2 57.8 %collective-permute-start.14 = (bf16[2048,384]{1,0:T(8,128)(2,1)}, bf16[2048,384]{1,0:T(8,128)(2,1)}, u32[]{:S(2)}, u32[]{:S(2)}) collective-permute-start(bf16[2048,384]{1,0:T(8,128)(2,1)} %all-gather.10.cloned.1.call-done), channel_id=1, source_target_pairs={{0,16},{4,20},{8,24},{12,28},{16,0},{20,4},{24,8},{28,12},{1,17},{... | collective-permute-start | bytes 4718600 | tf_op jit(solution)/shard_map/ppermute | solution.py:434
  190.2 90.5 %all-gather.18.cloned.1.call-start = ((), (), s32[]{:S(2)}) async-start(), calls=%async_computation.10 | async-start | bytes 2621440 | tf_op jit(solution)/shard_map/all_gather | solution.py:528
  222.0 106.1 %all-gather.20.cloned.1.call-start = ((), (), s32[]{:S(2)}) async-start(), calls=%async_computation.11 | async-start | bytes 2621440 | tf_op jit(solution)/shard_map/all_gather | solution.py:528
  283.2 95.9 %all-gather.22.cloned.1.call-start = ((), (), s32[]{:S(2)}) async-start(), calls=%async_computation.12 | async-start | bytes 2621440 | tf_op jit(solution)/shard_map/all_gather | solution.py:528
  298.5 541.7 %reduce-scatter.7.cloned.1.call-start = ((), (), s32[]{:S(2)}) async-start(), calls=%async_computation.13 | async-start | bytes 2621440 | tf_op jit(solution)/shard_map/reduce_scatter | solution.py:799
  379.1 60.7 %collective-permute-start.26 = (bf16[512,2048]{1,0:T(8,128)(2,1)}, bf16[512,2048]{1,0:T(8,128)(2,1)S(1)}, u32[]{:S(2)}, u32[]{:S(2)}) collective-permute-start(bf16[512,2048]{1,0:T(8,128)(2,1)} %all-gather.22.cloned.1.call-done), channel_id=1, source_target_pairs={{0,16},{4,20},{8,24},{12,28},{16,0},{20,4},{24,8},{28,12},{1,17},{... | collective-permute-start | bytes 6291464 | tf_op jit(solution)/shard_map/ppermute | solution.py:434
  635.0 61.7 %collective-permute-start.38 = (bf16[512,2048]{1,0:T(8,128)(2,1)}, bf16[512,2048]{1,0:T(8,128)(2,1)}, u32[]{:S(2)}, u32[]{:S(2)}) collective-permute-start(bf16[512,2048]{1,0:T(8,128)(2,1)} %get-tuple-element.372), channel_id=1, source_target_pairs={{0,4},{4,0},{8,12},{12,8},{16,20},{20,16},{24,28},{28,24},{1,5},{5... | collective-permute-start | bytes 6291464 | tf_op jit(solution)/shard_map/ppermute | solution.py:434
  642.8 53.8 %collective-permute-start.37 = (bf16[512,2048]{1,0:T(8,128)(2,1)}, bf16[512,2048]{1,0:T(8,128)(2,1)}, u32[]{:S(2)}, u32[]{:S(2)}) collective-permute-start(bf16[512,2048]{1,0:T(8,128)(2,1)} %add_convert_fusion.7), channel_id=1, source_target_pairs={{0,8},{4,12},{8,0},{12,4},{16,24},{20,28},{24,16},{28,20},{1,9},{5... | collective-permute-start | bytes 6291464 | tf_op jit(solution)/shard_map/ppermute | solution.py:434
  685.9 154.3 %reduce-scatter.9.cloned.1.call-start = ((), (), s32[]{:S(2)}) async-start(), calls=%async_computation.14 | async-start | bytes 2621440 | tf_op jit(solution)/shard_map/reduce_scatter | solution.py:799
  709.5 59.3 %collective-permute-start.42 = (bf16[512,2048]{1,0:T(8,128)(2,1)}, bf16[512,2048]{1,0:T(8,128)(2,1)}, u32[]{:S(2)}, u32[]{:S(2)}) collective-permute-start(bf16[512,2048]{1,0:T(8,128)(2,1)} %get-tuple-element.383), channel_id=1, source_target_pairs={{0,8},{4,12},{8,0},{12,4},{16,24},{20,28},{24,16},{28,20},{1,9},{5... | collective-permute-start | bytes 6291464 | tf_op jit(solution)/shard_map/ppermute | solution.py:434
  736.4 180.4 %reduce-scatter.11.cloned.1.call-start = ((), (), s32[]{:S(2)}) async-start(), calls=%async_computation.15 | async-start | bytes 2621440 | tf_op jit(solution)/shard_map/reduce_scatter | solution.py:799
  778.4 61.8 %collective-permute-start.47 = (bf16[2048,512]{1,0:T(8,128)(2,1)}, bf16[2048,512]{1,0:T(8,128)(2,1)}, u32[]{:S(2)}, u32[]{:S(2)}) collective-permute-start(bf16[2048,512]{1,0:T(8,128)(2,1)} %copy-done.77), channel_id=1, source_target_pairs={{0,16},{4,20},{8,24},{12,28},{16,0},{20,4},{24,8},{28,12},{1,17},{... | collective-permute-start | bytes 6291464 | tf_op jit(solution)/shard_map/ppermute | solution.py:434
  813.5 139.7 %reduce-scatter.13.cloned.1.call-start = ((), (), s32[]{:S(2)}) async-start(), calls=%async_computation.16 | async-start | bytes 2621440 | tf_op jit(solution)/shard_map/reduce_scatter | solution.py:799
  878.9 105.5 %reduce-scatter.17.cloned.1.call-start = ((), (), s32[]{:S(2)}) async-start(), calls=%async_computation.18 | async-start | bytes 1310720 | tf_op jit(solution)/shard_map/reduce_scatter | solution.py:799
  882.6 70.5 %collective-permute-start.51 = (bf16[2048,768]{1,0:T(8,128)(2,1)}, bf16[2048,768]{1,0:T(8,128)(2,1)}, u32[]{:S(2)}, u32[]{:S(2)}) collective-permute-start(bf16[2048,768]{1,0:T(8,128)(2,1)} %shard_map.345), channel_id=1, source_target_pairs={{0,16},{4,20},{8,24},{12,28},{16,0},{20,4},{24,8},{28,12},{1,17},{... | collective-permute-start | bytes 9437192 | tf_op jit(solution)/shard_map/ppermute | solution.py:434
  889.1 64.0 %collective-permute-start.50 = (bf16[512,2048]{1,0:T(8,128)(2,1)}, bf16[512,2048]{1,0:T(8,128)(2,1)}, u32[]{:S(2)}, u32[]{:S(2)}) collective-permute-start(bf16[512,2048]{1,0:T(8,128)(2,1)} %add_convert_fusion.4), channel_id=1, source_target_pairs={{0,8},{4,12},{8,0},{12,4},{16,24},{20,28},{24,16},{28,20},{1,9},{5... | collective-permute-start | bytes 6291464 | tf_op jit(solution)/shard_map/ppermute | solution.py:434
  892.4 150.0 %reduce-scatter.15.cloned.1.call-start = ((), (), s32[]{:S(2)}) async-start(), calls=%async_computation.17 | async-start | bytes 3932160 | tf_op jit(solution)/shard_map/reduce_scatter | solution.py:799
  958.5 145.1 %all-gather.24.cloned.1.call-start = ((), (), s32[]{:S(2)}) async-start(), calls=%async_computation.19 | async-start | bytes 7077888 | tf_op jit(solution)/shard_map/all_gather | solution.py:1116
  986.8 53.1 %collective-permute-start.59 = (bf16[512,1024]{1,0:T(8,128)(2,1)S(1)}, bf16[512,1024]{1,0:T(8,128)(2,1)S(1)}, u32[]{:S(2)}, u32[]{:S(2)}) collective-permute-start(bf16[512,1024]{1,0:T(8,128)(2,1)S(1)} %constant_dynamic-update-slice_fusion.35.refs_0_), channel_id=1, source_target_pairs={{0,8},{4,12},{8,0},{12,4},{16,24},{20,28},{24,16},{28,20},{1,9},{5... | collective-permute-start | bytes 3145736 | tf_op jit(solution)/shard_map/ppermute | solution.py:434
  990.6 51.8 %collective-permute-start.62 = (bf16[256,2048]{1,0:T(8,128)(2,1)S(1)}, bf16[256,2048]{1,0:T(8,128)(2,1)}, u32[]{:S(2)}, u32[]{:S(2)}) collective-permute-start(bf16[256,2048]{1,0:T(8,128)(2,1)S(1)} %collective-permute-done.57.refs_2_), channel_id=1, source_target_pairs={{0,16},{4,20},{8,24},{12,28},{16,0},{20,4},{24,8},{28,12},{1,17},{... | collective-permute-start | bytes 3145736 | tf_op jit(solution)/shard_map/ppermute | solution.py:434
  (190 other events, 2814.9 us)
Sparse Core Ops, SparseCore 0:
  63.4 36.5 all-gather.9
  102.1 35.9 all-gather.11
  140.3 27.4 all-gather.13
  190.4 43.6 all-gather.15
  236.0 44.6 all-gather.17
  283.3 44.7 all-gather.19
  330.3 44.6 all-gather.21
  686.0 43.2 reduce-scatter.6
  736.5 45.2 reduce-scatter.8
  813.6 43.7 reduce-scatter.10
  879.0 46.6 reduce-scatter.12
  928.4 25.7 reduce-scatter.16
  958.7 62.1 reduce-scatter.14
  1042.5 50.0 all-gather.23
